TPU v7x, 512 devices: a whole 4x8x8 slice. The times are simulated.
512 devices in a mesh: sub: 32 (over y, x), clu: 16 (over z, core).
Axes of the slice: x: 4, y: 8, z: 8, core: 2. Of those that a mesh axis runs over, the one named last changes fastest.
Arguments:
- dual_ops: bfloat16 [16, 32, 1536, 1536], P('clu', 'sub'), may hold values from -60 to 60, as said below
- neighbors: int32 [16, 32, 4], P('clu', 'sub'), may hold values from 0 to 31, as said below
- face_counts: int32 [16, 32, 6], P('clu', 'sub'), may hold values from 0 to 256, as said below
- load_terms: float32 [16, 32, 6, 256], P('clu', 'sub'), may hold values from -10 to 10
- precond_terms: float32 [16, 32, 6, 256], P('clu', 'sub'), may hold values from 0.25 to 2
- rigid_terms: float32 [16, 32, 6, 6, 256], P('clu', 'sub'), may hold values from -6 to 6
- recycled_terms: bfloat16 [16, 32, 64, 6, 256], P('clu', 'sub'), may hold values from -6 to 6
Outputs:
- dual_solution: float32 [16, 32, 6, 256], P('clu', 'sub')
- residual: float32 [16, 32, 6, 256], P('clu', 'sub')
Inputs may be any that keep to these rules, and one draw needn't show every extreme that they name: `neighbors`: faces 0 to 3 of subdomain i name four different other subdomains of its cluster, and each such subdomain names i on one of its faces 0 to 3. `face_counts`: both copies of an interface have the same count; faces 4 of the first cluster and faces 5 of the last have none; some face has 256. Each dual_ops[c, i] is positive definite.
All inputs are finite; a program needn't handle non-finite values.
Results may differ from a plain program's by a relative error of at most 0.014.
Values sent between devices are 32-bit elements; how exact they have to be, the bound alone decides.
No kernel may reach another device: no remote copies, remote signals or barrier semaphores. Data moves between devices by JAX's collectives and lax.ppermute only.
A program may use at most 64 MiB of HBM per device.

v0:
```python
import jax
import jax.numpy as jnp
from jax import lax
from jax.sharding import PartitionSpec as P

ITERS = 3


precise = lax.Precision.HIGHEST


def padded_2(block, sides, width):
    for axis, dim in sides:
        count = lax.axis_size(axis)
        forward = [(i, i + 1) for i in range(count - 1)]
        backward = [(target, source) for source, target in forward]
        low = lax.ppermute(
            lax.slice_in_dim(block, block.shape[dim] - width, None, axis=dim), axis, forward
        )
        high = lax.ppermute(lax.slice_in_dim(block, 0, width, axis=dim), axis, backward)
        block = jnp.concatenate([low, block, high], axis=dim)
    return block


def partner_copy(values, onehot, blocks):
    outgoing = jnp.einsum("kq,lkf->qlf", onehot, values[:, :4, :], precision=precise)
    rim_faces = jnp.stack([values[:, 4, :], values[:, 5, :]], axis=0)

    def select_faces(received):
        return jnp.einsum("kq,qlf->lkf", onehot, received, precision=precise)

    if blocks:
        inner_part = select_faces(
            lax.all_to_all(outgoing, "sub", split_axis=0, concat_axis=0, tiled=True)
        )
        rimmed = padded_2(rim_faces, (("clu", 0),), 1)
    else:
        inner_part = select_faces(
            lax.all_to_all(outgoing, "sub", split_axis=0, concat_axis=0, tiled=True)
        )
        rimmed = padded_2(rim_faces, (("clu", 0),), 1)
    return jnp.concatenate([inner_part, rimmed[0][:, None, :], rimmed[3][:, None, :]], axis=1)


def coarse_terms(rigid_cols, values, clu_index, clusters):
    partial_value = jnp.einsum("jrfs,lfs->jrl", rigid_cols, values, precision=precise)
    padded = jnp.zeros((clusters + 2, 6, values.shape[0]), jnp.float32)
    return lax.dynamic_update_slice(padded, partial_value, (clu_index, 0, 0))


def coarse_total(summed, factor, clusters):
    return factor * summed[1 : clusters + 1].reshape(clusters * 6, summed.shape[2])


def coarse_apply(rigid_cols, amounts, clu_index):
    columns = amounts.shape[1]
    blank_rows = jnp.zeros((6, columns), jnp.float32)
    padded = jnp.concatenate([blank_rows, amounts, blank_rows], axis=0)
    nearby = lax.dynamic_slice_in_dim(padded, 6 * clu_index, 18, 0).reshape(3, 6, columns)
    return jnp.einsum("jrfs,jrl->lfs", rigid_cols, nearby, precision=precise)


def spd_solve(matrix, right_side):
    factor_low = jnp.linalg.cholesky(matrix)
    halfway = lax.linalg.triangular_solve(factor_low, right_side, left_side=True, lower=True)
    return lax.linalg.triangular_solve(
        factor_low, halfway, left_side=True, lower=True, transpose_a=True
    )


def local_dot(first, second):
    return jnp.einsum("afs,bfs->ab", first, second, precision=precise)


def local(dual_ops, neighbors, face_counts, load_terms, precond_terms, rigid_terms, recycled_terms):
    local_op = dual_ops[0, 0]
    neighbor_ids = neighbors[0, 0]
    slot_counts = face_counts[0, 0]
    load_vec = load_terms[0, 0]
    precond = precond_terms[0, 0]
    rigid_vec = rigid_terms[0, 0]
    recycled = recycled_terms[0, 0]
    clusters = lax.axis_size("clu")
    members = lax.axis_size("sub")
    clu_index = lax.axis_index("clu")
    slot_total = load_vec.shape[-1]
    basis_count = recycled.shape[0]
    onehot = (neighbor_ids[:, None] == jnp.arange(members, dtype=jnp.int32)[None, :]).astype(
        jnp.float32
    )
    live_slots = (jnp.arange(slot_total, dtype=jnp.int32)[None, :] < slot_counts[:, None]).astype(
        jnp.float32
    )
    face_index = jnp.arange(6, dtype=jnp.int32)
    inner_face = (face_index < 4).astype(jnp.float32)[:, None]
    below_face = (face_index == 4).astype(jnp.float32)[:, None]
    above_face = (face_index == 5).astype(jnp.float32)[:, None]
    stacked = jnp.concatenate(
        [load_vec[None], precond[None], rigid_vec, recycled.astype(jnp.float32)], axis=0
    )
    copies = partner_copy(stacked, onehot, True)
    demand = live_slots * (load_vec[None] + copies[0:1])
    weights = 0.5 * live_slots * (precond[None] + copies[1:2])
    rigid_copy = copies[2:8]
    rigid_cols = jnp.stack(
        [
            live_slots * rigid_copy * below_face,
            live_slots * (rigid_vec + rigid_copy * inner_face),
            live_slots * rigid_copy * above_face,
        ],
        axis=0,
    )
    basis_raw = live_slots * (recycled.astype(jnp.float32) + copies[8:])
    gram_local = jnp.einsum("jrfs,kqfs->jrkq", rigid_cols, rigid_cols, precision=precise).reshape(
        18, 18
    )
    gram_pad = lax.dynamic_update_slice(
        jnp.zeros((6 * clusters + 12, 6 * clusters + 12), jnp.float32),
        gram_local,
        (6 * clu_index, 6 * clu_index),
    )
    combined = jnp.concatenate([demand, basis_raw], axis=0)
    gram_sum, setup_sum = lax.psum(
        (gram_pad, coarse_terms(rigid_cols, combined, clu_index, clusters)), ("sub", "clu")
    )
    coarse_matrix = 0.5 * gram_sum[6 : 6 + 6 * clusters, 6 : 6 + 6 * clusters]

    def project_from(values, summed):
        amounts = spd_solve(coarse_matrix, coarse_total(summed, 0.5, clusters))
        return (values - coarse_apply(rigid_cols, amounts, clu_index), amounts)

    projected = project_from(combined, setup_sum)[0]
    start_res = projected[0:1]
    basis_vec = projected[1:]
    local_images = live_slots * jnp.dot(
        basis_vec.astype(jnp.bfloat16).reshape(basis_count, -1),
        local_op,
        preferred_element_type=jnp.float32,
    ).reshape(basis_count, 6, slot_total)
    images = live_slots * (local_images + partner_copy(local_images, onehot, True))
    image_coarse, energy_sum, start_sum = lax.psum(
        (
            coarse_terms(rigid_cols, images, clu_index, clusters),
            local_dot(basis_vec, images),
            local_dot(basis_vec, start_res),
        ),
        ("sub", "clu"),
    )
    deflated = project_from(images, image_coarse)[0]
    energy = 0.5 * energy_sum
    energy = 0.5 * (energy + energy.T)
    amount = spd_solve(energy, 0.5 * start_sum)
    correction = jnp.einsum("lfs,lk->kfs", deflated, amount, precision=precise)
    against_factor = 0.5
    solution = jnp.einsum("lfs,lk->kfs", basis_vec, amount, precision=precise)
    residual = start_res - correction

    def precondition(current):
        scaled = weights * current
        coarse_sums = lax.psum(
            coarse_terms(rigid_cols, scaled, clu_index, clusters), ("sub", "clu")
        )
        search = project_from(scaled, coarse_sums)[0]
        rho_sum, rhs_sum = lax.psum(
            (local_dot(current, search), local_dot(deflated, search)), ("sub", "clu")
        )
        right_side = against_factor * rhs_sum
        rho_value = 0.5 * rho_sum[0, 0]
        return (search, rho_value, spd_solve(energy, right_side))

    search, rho_now, deflate_coeff = precondition(residual)
    direction = search - jnp.einsum("lfs,lk->kfs", basis_vec, deflate_coeff, precision=precise)
    for iteration in range(ITERS):
        flat_dir = direction.astype(jnp.bfloat16).reshape(1, -1)
        local_image = live_slots * jnp.dot(
            flat_dir, local_op, preferred_element_type=jnp.float32
        ).reshape(1, 6, slot_total)
        assembled = live_slots * (local_image + partner_copy(local_image, onehot, False))
        image_sums = lax.psum(
            coarse_terms(rigid_cols, assembled, clu_index, clusters), ("sub", "clu")
        )
        image_vec = project_from(assembled, image_sums)[0]
        curvature = 0.5 * lax.psum(local_dot(direction, image_vec), ("sub", "clu"))[0, 0]
        step_size = rho_now / curvature
        solution = solution + step_size * direction
        residual = residual - step_size * image_vec
        if iteration + 1 < ITERS:
            search, rho_next, deflate_coeff = precondition(residual)
            direction = (
                search
                - jnp.einsum("lfs,lk->kfs", basis_vec, deflate_coeff, precision=precise)
                + rho_next / rho_now * direction
            )
            rho_now = rho_next
    return (solution[None], residual[None])


def solution(mesh):
    return jax.shard_map(
        local,
        mesh=mesh,
        in_specs=(
            P("clu", "sub", None, None),
            P("clu", "sub", None),
            P("clu", "sub", None),
            P("clu", "sub", None, None),
            P("clu", "sub", None, None),
            P("clu", "sub", None, None, None),
            P("clu", "sub", None, None, None),
        ),
        out_specs=(P("clu", "sub", None, None), P("clu", "sub", None, None)),
        check_vma=False,
    )
```

profile of v0, /device:TPU:1, one launch (start us, length us, event | category | flops | bytes accessed | tf_op | source)
XLA Modules:
  0.0 1794.0 jit_solution(1879936950929192035)
XLA Ops:
  10.4 1.9 fusion.19
  12.3 2.8 copy.62
  15.1 10.6 all-to-all-start
  26.6 2.8 collective-permute-start.1
  29.4 3.9 collective-permute-start
  33.5 46.2 %all-to-all-done = f32[32,72,256]{2,1,0:T(8,128)S(1)} async-done(((f32[32,72,256]{2,1,0:T(8,128)}), f32[32,72,256]{2,1,0:T(8,128)S(1)}, u32[]{:S(2)}, u32[]{:S(2)}) %all-to-all-start) | async-done | bytes 2359328 | tf_op jit(solution)/shard_map/all_to_all | solution.py:34
  86.6 6.6 copy.74
  93.2 259.0 %all-reduce.7.cloned.1.call-done = (f32[18,6,65]{2,1,0:T(8,128)}, f32[108,108]{0,1:T(8,128)}) async-done(((f32[18,6,65]{2,1,0:T(8,128)}, f32[108,108]{0,1:T(8,128)}), (f32[18,6,65]{2,1,0:T(8,128)}, f32[108,108]{0,1:T(8,128)})) %all-reduce.7.cloned.1.call-update) | async-done | bytes 74752 | tf_op jit(solution)/shard_map/psum | solution.py:123
  354.9 8.8 cholesky.45
  365.1 7.4 custom-call.25
  375.0 3.9 fusion.187
  381.0 2.6 copy.76
  383.6 6.1 all-to-all-start.1
  390.8 2.1 slice_bitcast_fusion.1
  392.8 2.2 collective-permute-start.3
  395.0 3.6 collective-permute-start.2
  399.8 38.5 %all-to-all-done.1 = f32[32,64,256]{2,1,0:T(8,128)S(1)} async-done(((f32[32,64,256]{2,1,0:T(8,128)}), f32[32,64,256]{2,1,0:T(8,128)S(1)}, u32[]{:S(2)}, u32[]{:S(2)}) %all-to-all-start.1) | async-done | bytes 2097184 | tf_op jit(solution)/shard_map/all_to_all | solution.py:34
  438.3 2.0 fusion.7
  442.9 97.6 %all-reduce.3 = (f32[64,64]{0,1:T(8,128)S(1)}, f32[64,1]{0,1:T(1,128)S(1)}, f32[18,6,64]{2,1,0:T(8,128)S(1)}) all-reduce(f32[64,64]{0,1:T(8,128)S(1)} %convolution_bitcast_fusion.6, f32[64,1]{0,1:T(1,128)S(1)} %convolution_bitcast_fusion.15, f32[18,6,64]{2,1,0:T(8,128)S(1)} %fusion.10), channel_id=1, replica_groups=mesh['sub'=32,'clu'=16] {'sub','clu'}, use_global_device_ids=true, to_apply=%region_4.0 | all-reduce | flops 11072 | bytes 88576 | tf_op jit(solution)/shard_map/psum | solution.py:141
  540.7 5.8 cholesky.67
  547.9 4.9 custom-call.43
  557.3 93.4 %psum.145 = f32[18,6,1]{1,0,2:T(8,128)S(1)} all-reduce(f32[18,6,1]{1,0,2:T(8,128)S(1)} %dynamic_update_slice.30), channel_id=1, replica_groups=mesh['sub'=32,'clu'=16] {'sub','clu'}, use_global_device_ids=true, to_apply=%region_9.14 | all-reduce | flops 108 | bytes 864 | tf_op jit(solution)/shard_map/psum | solution.py:160
  652.2 95.5 %psum.147 = f32[64,1]{0,1:T(1,128)S(1)} all-reduce(f32[64,1]{0,1:T(1,128)S(1)} %convolution_bitcast_fusion.14), channel_id=1, replica_groups=mesh['sub'=32,'clu'=16] {'sub','clu'}, use_global_device_ids=true, to_apply=%region_11.18 | all-reduce | flops 64 | bytes 512 | tf_op jit(solution)/shard_map/psum | solution.py:164
  748.5 3.6 fusion.188
  752.5 2.6 collective-permute-start.5
  755.1 3.0 collective-permute-start.4
  758.7 5.1 all-to-all-start.2
  765.1 7.7 all-to-all-done.2
  774.1 94.7 %psum.148 = f32[18,6,1]{1,0,2:T(8,128)S(1)} all-reduce(f32[18,6,1]{1,0,2:T(8,128)S(1)} %dynamic_update_slice.31), channel_id=1, replica_groups=mesh['sub'=32,'clu'=16] {'sub','clu'}, use_global_device_ids=true, to_apply=%region_12.19 | all-reduce | flops 108 | bytes 864 | tf_op jit(solution)/shard_map/psum | solution.py:179
  870.5 94.1 %all-reduce.2 = (f32[1,1]{1,0:T(1,128)}, f32[1,1]{1,0:T(1,128)}) all-reduce(f32[1,1]{1,0:T(1,128)} %bitcast.81, f32[1,1]{1,0:T(1,128)} %bitcast.125), channel_id=1, replica_groups=mesh['sub'=32,'clu'=16] {'sub','clu'}, use_global_device_ids=true, to_apply=%region_10.17 | all-reduce | flops 2 | bytes 16 | tf_op jit(solution)/shard_map/psum | solution.py:164
  967.8 94.4 %psum.150 = f32[18,6,1]{1,0,2:T(8,128)S(1)} all-reduce(f32[18,6,1]{1,0,2:T(8,128)S(1)} %dynamic_update_slice.32), channel_id=1, replica_groups=mesh['sub'=32,'clu'=16] {'sub','clu'}, use_global_device_ids=true, to_apply=%region_14.21 | all-reduce | flops 108 | bytes 864 | tf_op jit(solution)/shard_map/psum | solution.py:160
  1064.3 95.1 %all-reduce.1 = (f32[64,1]{0,1:T(1,128)S(1)}, f32[1,1]{1,0:T(1,128)}) all-reduce(f32[64,1]{0,1:T(1,128)S(1)} %convolution_bitcast_fusion.13, f32[1,1]{1,0:T(1,128)} %bitcast.146), channel_id=1, replica_groups=mesh['sub'=32,'clu'=16] {'sub','clu'}, use_global_device_ids=true, to_apply=%region_16.23 | all-reduce | flops 65 | bytes 520 | tf_op jit(solution)/shard_map/psum | solution.py:164
  1160.9 3.6 fusion.189
  1165.5 6.3 all-to-all-start.3
  1171.8 2.9 collective-permute-start.7
  1174.7 2.7 collective-permute-start.6
  1177.4 3.0 all-to-all-done.3
  1181.8 96.2 %psum.153 = f32[18,6,1]{1,0,2:T(8,128)S(1)} all-reduce(f32[18,6,1]{1,0,2:T(8,128)S(1)} %dynamic_update_slice.33), channel_id=1, replica_groups=mesh['sub'=32,'clu'=16] {'sub','clu'}, use_global_device_ids=true, to_apply=%region_17.24 | all-reduce | flops 108 | bytes 864 | tf_op jit(solution)/shard_map/psum | solution.py:179
  1279.6 94.5 %psum.154 = f32[1,1]{1,0:T(1,128)} all-reduce(f32[1,1]{1,0:T(1,128)} %bitcast.189), channel_id=1, replica_groups=mesh['sub'=32,'clu'=16] {'sub','clu'}, use_global_device_ids=true, to_apply=%region_18.25 | all-reduce | flops 1 | bytes 8 | tf_op jit(solution)/shard_map/psum | solution.py:183
  1375.9 95.1 %psum.155 = f32[18,6,1]{1,0,2:T(8,128)S(1)} all-reduce(f32[18,6,1]{1,0,2:T(8,128)S(1)} %dynamic_update_slice.34), channel_id=1, replica_groups=mesh['sub'=32,'clu'=16] {'sub','clu'}, use_global_device_ids=true, to_apply=%region_19.26 | all-reduce | flops 108 | bytes 864 | tf_op jit(solution)/shard_map/psum | solution.py:160
  1473.1 94.4 %all-reduce = (f32[64,1]{0,1:T(1,128)S(1)}, f32[1,1]{1,0:T(1,128)}) all-reduce(f32[64,1]{0,1:T(1,128)S(1)} %convolution_bitcast_fusion.12, f32[1,1]{1,0:T(1,128)} %bitcast.210), channel_id=1, replica_groups=mesh['sub'=32,'clu'=16] {'sub','clu'}, use_global_device_ids=true, to_apply=%region_21.28 | all-reduce | flops 65 | bytes 520 | tf_op jit(solution)/shard_map/psum | solution.py:164
  1569.0 3.6 fusion.190
  1573.6 8.0 all-to-all-start.4
  1581.7 2.9 collective-permute-start.9
  1584.6 4.0 collective-permute-start.8
  1588.6 1.8 all-to-all-done.4
  1591.7 97.2 %psum.158 = f32[18,6,1]{1,0,2:T(8,128)S(1)} all-reduce(f32[18,6,1]{1,0,2:T(8,128)S(1)} %dynamic_update_slice.35), channel_id=1, replica_groups=mesh['sub'=32,'clu'=16] {'sub','clu'}, use_global_device_ids=true, to_apply=%region_22.29 | all-reduce | flops 108 | bytes 864 | tf_op jit(solution)/shard_map/psum | solution.py:179
  1690.7 94.4 %psum.159 = f32[1,1]{1,0:T(1,128)} all-reduce(f32[1,1]{1,0:T(1,128)} %bitcast.253), channel_id=1, replica_groups=mesh['sub'=32,'clu'=16] {'sub','clu'}, use_global_device_ids=true, to_apply=%region_23.30 | all-reduce | flops 1 | bytes 8 | tf_op jit(solution)/shard_map/psum | solution.py:183
  (232 shorter events, 55.6 us)
Async XLA Ops:
  15.1 18.3 %copy-start.7 = (s32[1,1,6]{2,1,0:T(1,128)S(1)}, s32[1,1,6]{2,1,0:T(1,128)}, u32[]{:S(2)}) copy-start(s32[1,1,6]{2,1,0:T(1,128)} %param.19) | copy-start | bytes 76
  15.1 64.5 %copy-start.10 = (s32[1,1,4]{2,1,0:T(1,128)S(1)}, s32[1,1,4]{2,1,0:T(1,128)}, u32[]{:S(2)}) copy-start(s32[1,1,4]{2,1,0:T(1,128)} %param.18) | copy-start | bytes 52
  15.1 64.5 %all-to-all-start = ((f32[32,72,256]{2,1,0:T(8,128)}), f32[32,72,256]{2,1,0:T(8,128)S(1)}, u32[]{:S(2)}, u32[]{:S(2)}) async-start(f32[32,72,256]{2,1,0:T(8,128)} %copy.62), calls=%async_computation | async-start | bytes 4718592 | tf_op jit(solution)/shard_map/all_to_all | solution.py:34
  25.8 55.6 %copy-start.8 = (f32[1,1,6,256]{3,1,2,0:T(1,128)S(1)}, f32[1,1,6,256]{3,1,2,0:T(1,128)}, u32[]{:S(2)}) copy-start(f32[1,1,6,256]{3,1,2,0:T(1,128)} %param.20) | copy-start | bytes 18436
  25.8 326.4 %all-reduce.7.cloned.1.call-start = ((), (), s32[]{:S(2)}) async-start(), calls=%async_computation.5 | async-start | bytes 262144 | tf_op jit(solution)/shard_map/psum | solution.py:123
  26.6 54.5 %collective-permute-start.1 = (f32[1,72,256]{2,0,1:T(1,128)}, f32[1,72,256]{2,0,1:T(1,128)S(1)}, u32[]{:S(2)}, u32[]{:S(2)}) collective-permute-start(f32[1,72,256]{2,0,1:T(1,128)} %get-tuple-element.40), channel_id=1, source_target_pairs={{1,0},{2,1},{3,2},{4,3},{5,4},{6,5},{7,6},{8,7},{9,8},{10,9},{11,1... | collective-permute-start | bytes 221192 | tf_op jit(solution)/shard_map/ppermute | solution.py:20
  29.4 51.7 %collective-permute-start = (f32[1,72,256]{2,0,1:T(1,128)S(1)}, f32[1,72,256]{2,0,1:T(1,128)S(1)}, u32[]{:S(2)}, u32[]{:S(2)}) collective-permute-start(f32[1,72,256]{2,0,1:T(1,128)S(1)} %get-tuple-element.39), channel_id=1, source_target_pairs={{0,1},{1,2},{2,3},{3,4},{4,5},{5,6},{6,7},{7,8},{8,9},{9,10},{10,1... | collective-permute-start | bytes 221192 | tf_op jit(solution)/shard_map/ppermute | solution.py:17
  33.5 49.1 %copy-start.6 = (f32[1,1,6,6,256]{4,1,3,2,0:T(1,128)S(1)}, f32[1,1,6,6,256]{4,1,3,2,0:T(1,128)}, u32[]{:S(2)}) copy-start(f32[1,1,6,6,256]{4,1,3,2,0:T(1,128)} %param.22) | copy-start | bytes 110596
  84.8 1.2 copy-start.4
  85.9 0.6 copy-start.5
  373.9 0.8 copy-start.2
  378.9 4.8 copy-start
  379.1 0.8 copy-start.3
  383.6 54.7 %all-to-all-start.1 = ((f32[32,64,256]{2,1,0:T(8,128)}), f32[32,64,256]{2,1,0:T(8,128)S(1)}, u32[]{:S(2)}, u32[]{:S(2)}) async-start(f32[32,64,256]{2,1,0:T(8,128)} %copy.76), calls=%async_computation.1 | async-start | bytes 4194304 | tf_op jit(solution)/shard_map/all_to_all | solution.py:34
  392.8 47.5 %collective-permute-start.3 = (f32[1,64,256]{2,0,1:T(1,128)}, f32[1,64,256]{2,0,1:T(1,128)}, u32[]{:S(2)}, u32[]{:S(2)}) collective-permute-start(f32[1,64,256]{2,0,1:T(1,128)} %get-tuple-element.42), channel_id=1, source_target_pairs={{1,0},{2,1},{3,2},{4,3},{5,4},{6,5},{7,6},{8,7},{9,8},{10,9},{11,1... | collective-permute-start | bytes 196616 | tf_op jit(solution)/shard_map/ppermute | solution.py:20
  395.0 45.3 %collective-permute-start.2 = (f32[1,64,256]{2,0,1:T(1,128)}, f32[1,64,256]{2,0,1:T(1,128)}, u32[]{:S(2)}, u32[]{:S(2)}) collective-permute-start(f32[1,64,256]{2,0,1:T(1,128)} %get-tuple-element.41), channel_id=1, source_target_pairs={{0,1},{1,2},{2,3},{3,4},{4,5},{5,6},{6,7},{7,8},{8,9},{9,10},{10,1... | collective-permute-start | bytes 196616 | tf_op jit(solution)/shard_map/ppermute | solution.py:17
  438.3 2.0 copy-start.1
  442.3 113.3 %copy-start.9 = (f32[1,1,6,256]{3,1,2,0:T(1,128)S(1)}, f32[1,1,6,256]{3,1,2,0:T(1,128)}, u32[]{:S(2)}) copy-start(f32[1,1,6,256]{3,1,2,0:T(1,128)} %param.21) | copy-start | bytes 18436
  752.5 20.5 %collective-permute-start.5 = (f32[1,1,256]{2,1,0:T(1,128)S(1)}, f32[1,1,256]{2,1,0:T(1,128)S(1)}, u32[]{:S(2)}, u32[]{:S(2)}) collective-permute-start(f32[1,1,256]{2,1,0:T(1,128)S(1)} %get-tuple-element.52), channel_id=1, source_target_pairs={{1,0},{2,1},{3,2},{4,3},{5,4},{6,5},{7,6},{8,7},{9,8},{10,9},{11,1... | collective-permute-start | bytes 3080 | tf_op jit(solution)/shard_map/ppermute | solution.py:20
  755.1 17.9 collective-permute-start.4
  758.7 14.1 all-to-all-start.2
  1165.5 15.0 all-to-all-start.3
  1171.8 8.8 collective-permute-start.7
  1174.7 6.0 collective-permute-start.6
  1573.6 16.8 all-to-all-start.4
  1581.7 8.9 collective-permute-start.9
  1584.6 6.0 collective-permute-start.8
Sparse Core Ops, SparseCore 0:
  86.7 265.4 all-reduce.6
where the time goes:
time: 1800 us; the launch traced here: 1790 us
  blocking collectives  1240 us (69%)
  waiting for transfers between devices  356 us (20%)
  starting transfers between devices  66.7 us (4%)
  other arithmetic  45.4 us (3%)
  matrix products  42 us (2%)
  local copies, waits for them, and re-layouts  27.8 us (2%)
  between operations  19.1 us (1%)
    psum x4, blocking collectives, precondition(): lax.psum((local_dot(current, search), local_dot(deflated, search)), ('sub...  379 us
    psum x3, blocking collectives, local(): lax.psum(coarse_terms(rigid_cols, assembled, clu_index, clusters), ('sub'...  288 us
    psum x3, blocking collectives, precondition(): lax.psum(coarse_terms(rigid_cols, scaled, clu_index, clusters), ('sub', '...  283 us
    psum x1, waiting for transfers between devices, local(): lax.psum((gram_pad, coarse_terms(rigid_cols, combined, clu_index, cluster...  259 us
    psum x2, blocking collectives, local(): lax.psum(local_dot(direction, image_vec), ('sub', 'clu'))[0, 0]  189 us
    psum x1, blocking collectives, local(): lax.psum((coarse_terms(rigid_cols, images, clu_index, clusters), local_do...  97.6 us
    all_to_all x5, waiting for transfers between devices, partner_copy(): lax.all_to_all(outgoing, 'sub', split_axis=0, concat_axis=0, tiled=True)  97.3 us
    all_to_all x5, starting transfers between devices, partner_copy(): lax.all_to_all(outgoing, 'sub', split_axis=0, concat_axis=0, tiled=True)  36.1 us
  transfers between devices with their start and end apart: 16, of which 6 were waited for; matrix products, arithmetic and copies ran while one was open for 1% of the time, Pallas kernels for 0%

commit v1 on v0

v1 whole, which is shorter than its diff:
```python
import jax
import jax.numpy as jnp
from jax import lax
from jax.experimental import pallas as pl
from jax.experimental.pallas import tpu as pltpu
from jax.sharding import PartitionSpec as P

ITERS = 3
LANES = 128


precise = lax.Precision.HIGHEST


def dot(first, second):
    return jnp.dot(first, second, precision=precise, preferred_element_type=jnp.float32)


def dot_t(first, second):
    return lax.dot_general(
        first, second, (((1,), (1,)), ((), ())), precision=precise, preferred_element_type=jnp.float32
    )


def padded_row(values, multiple=LANES):
    flat = values.reshape(-1)
    return jnp.pad(flat, (0, -flat.shape[0] % multiple))


def everyone(row, axis):
    count = lax.axis_size(axis)
    sent = jnp.broadcast_to(row[None, None, :], (count, 1, row.shape[0]))
    return lax.all_to_all(sent, axis, split_axis=0, concat_axis=0, tiled=True)[:, 0, :]


def trade(rows, axis):
    return lax.all_to_all(rows[:, None, :], axis, split_axis=0, concat_axis=0, tiled=True)[:, 0, :]


def rims(values):
    count = lax.axis_size("clu")
    forward = [(i, i + 1) for i in range(count - 1)]
    backward = [(i + 1, i) for i in range(count - 1)]
    low = lax.ppermute(values[:, 5, :], "clu", forward)
    high = lax.ppermute(values[:, 4, :], "clu", backward)
    return low, high


def six_faces(inner, low, high):
    return jnp.concatenate([inner, low[:, None, :], high[:, None, :]], axis=1)


def invert(matrix_ref, inverse_ref):
    size = matrix_ref.shape[0]
    rows = lax.broadcasted_iota(jnp.int32, (size, size), 0)
    lanes = lax.broadcasted_iota(jnp.int32, (size, size), 1)
    row_lanes = lax.broadcasted_iota(jnp.int32, (1, size), 1)
    column_rows = lax.broadcasted_iota(jnp.int32, (size, 1), 0)
    values = matrix_ref[...]
    for k in range(size):
        pivot_row = values[k : k + 1, :]
        reciprocal = 1.0 / pivot_row[:, k : k + 1]
        scaled_row = jnp.where(row_lanes == k, 1.0, pivot_row) * reciprocal
        column = jnp.where(column_rows == k, -1.0, values[:, k : k + 1])
        kept = jnp.where((rows == k) | (lanes == k), 0.0, values)
        values = kept - column * scaled_row
    inverse_ref[...] = values


def spd_inverse(matrix):
    size = matrix.shape[0]
    return pl.pallas_call(
        invert,
        out_shape=jax.ShapeDtypeStruct((size, size), jnp.float32),
        in_specs=[pl.BlockSpec(memory_space=pltpu.VMEM)],
        out_specs=pl.BlockSpec(memory_space=pltpu.VMEM),
        cost_estimate=pl.CostEstimate(flops=2 * size**3, bytes_accessed=8 * size**2, transcendentals=size),
    )(matrix)


def local(dual_ops, neighbors, face_counts, load_terms, precond_terms, rigid_terms, recycled_terms):
    local_op = dual_ops[0, 0]
    neighbor_ids = neighbors[0, 0]
    load = load_terms[0, 0]
    rigid = rigid_terms[0, 0]
    recycled = recycled_terms[0, 0].astype(jnp.float32)
    clusters = lax.axis_size("clu")
    members = lax.axis_size("sub")
    clu_index = lax.axis_index("clu")
    sub_index = lax.axis_index("sub")
    slots = load.shape[-1]
    width = 6 * slots
    count = recycled.shape[0]
    per = count // members
    piece = 4 * per * slots
    coarse = 6 * clusters
    onehot = (neighbor_ids[:, None] == jnp.arange(members, dtype=jnp.int32)[None, :]).astype(
        jnp.float32
    )
    live = (
        jnp.arange(slots, dtype=jnp.int32)[None, :] < face_counts[0, 0][:, None]
    ).astype(jnp.float32)
    flat_live = live.reshape(1, width)

    targets = jnp.arange(coarse, dtype=jnp.int32)[:, None]
    sources = jnp.arange(18 * clusters, dtype=jnp.int32)[None, :]
    spread = (
        targets == 6 * (sources // 18) + (sources % 18) - 6
    ).astype(jnp.float32)
    spread_back = spread.T.reshape(clusters, 18, coarse)

    def nearby(values):
        padded = jnp.pad(values, ((6, 6), (0, 0)))
        return lax.dynamic_slice_in_dim(padded, 6 * clu_index, 18, 0)

    def to_carriers(values):
        faces = values.reshape(members, per, 6, slots)[:, :, :4]
        return faces.transpose(0, 2, 1, 3).reshape(members, piece)

    def from_carriers(received):
        faces = received.reshape(members, 4, per, slots).transpose(0, 2, 1, 3)
        return faces.reshape(count, 4, slots)

    few = jnp.concatenate([load[None], precond_terms[0, 0][None], rigid], axis=0)
    few_count = few.shape[0]
    low, high = rims(jnp.concatenate([few, recycled], axis=0))
    direct = dot(onehot.T, few[:, :4].transpose(1, 0, 2).reshape(4, few_count * slots))
    ids = jnp.broadcast_to(padded_row(neighbor_ids.astype(jnp.float32))[None], (members, LANES))
    received = trade(jnp.concatenate([to_carriers(recycled), direct, ids], axis=1), "sub")
    table = received[:, piece + few_count * slots :][:, :4]
    slots_of = 4 * members
    row_member = (lax.broadcasted_iota(jnp.int32, (slots_of, slots_of), 0) // 4).astype(jnp.float32)
    lane_member = (lax.broadcasted_iota(jnp.int32, (slots_of, slots_of), 1) // 4).astype(jnp.float32)
    route = jnp.where(
        (table.reshape(slots_of, 1) == lane_member) & (table.reshape(1, slots_of) == row_member), 1.0, 0.0
    )

    def carry(arrived):
        return dot(route, arrived.reshape(4 * members, per * slots)).reshape(members, piece)

    few_inner = dot(onehot, received[:, piece : piece + few_count * slots])
    few_inner = few_inner.reshape(4, few_count, slots).transpose(1, 0, 2)
    few_copy = six_faces(few_inner, low[:few_count], high[:few_count])
    demand = (live * (load + few_copy[0])).reshape(1, width)
    weights = (0.5 * live * (few[1] + few_copy[1])).reshape(1, width)
    face_index = jnp.arange(6, dtype=jnp.int32)
    inner_face = (face_index < 4).astype(jnp.float32)[:, None]
    below_face = (face_index == 4).astype(jnp.float32)[:, None]
    above_face = (face_index == 5).astype(jnp.float32)[:, None]
    rigid_copy = few_copy[2:]
    cols = jnp.concatenate(
        [
            live * rigid_copy * below_face,
            live * (rigid + rigid_copy * inner_face),
            live * rigid_copy * above_face,
        ],
        axis=0,
    ).reshape(18, width)
    weighted_cols = weights * cols
    flat_recycled = recycled.reshape(count, width)
    sums = dot_t(
        cols,
        jnp.concatenate(
            [0.5 * cols, 0.5 * weighted_cols, flat_recycled, load.reshape(1, width)], axis=0
        ),
    )
    sums_size = sums.size
    sums_row = padded_row(sums)
    received = trade(
        jnp.concatenate(
            [carry(received[:, :piece]), jnp.broadcast_to(sums_row[None], (members, sums_row.shape[0]))],
            axis=1,
        ),
        "sub",
    )
    basis_raw = (
        live * (recycled + six_faces(from_carriers(received[:, :piece]), low[few_count:], high[few_count:]))
    ).reshape(count, width)
    gathered = everyone(jnp.sum(received[:, piece:], axis=0), "clu")
    gathered = gathered[:, :sums_size].reshape(clusters, 18, 37 + count)
    pairs = jnp.einsum(
        "cgab,cbx->cagx",
        jnp.stack([gathered[:, :, :18], gathered[:, :, 18:36]], axis=1),
        spread_back,
        precision=precise,
    ).reshape(18 * clusters, 2 * coarse)
    assembled = dot(
        spread,
        jnp.concatenate([pairs, gathered[:, :, 36:].reshape(18 * clusters, count + 1)], axis=1),
    )
    coarse_inverse = spd_inverse(assembled[:, :coarse])
    weighted_matrix = assembled[:, coarse : 2 * coarse]
    amounts = nearby(dot(coarse_inverse, assembled[:, 2 * coarse :]))
    projected = jnp.concatenate([basis_raw, demand], axis=0) - dot(amounts.T, cols)
    basis = projected[:count]
    start = projected[count:]

    products = flat_live * jnp.dot(
        basis.astype(jnp.bfloat16), local_op, preferred_element_type=jnp.float32
    )
    low, high = rims(products.reshape(count, 6, slots))
    both_cols = jnp.concatenate([cols, weighted_cols], axis=0)
    grouped = both_cols.reshape(2, 3, 6, width).transpose(0, 2, 1, 3).reshape(12, 3, width)
    grouped = jnp.pad(grouped, ((0, 0), (0, 1), (0, 0))).reshape(48, width)
    tests = jnp.concatenate([basis, grouped], axis=0)
    sums = dot_t(tests, products)
    start_row = dot_t(0.5 * start, tests)
    basis_parts = count // 4
    shares = jnp.concatenate(
        [
            sums.reshape(basis_parts + 12, 4 * count),
            jnp.pad(start_row[:, :count], ((0, 0), (0, 3 * count))),
            jnp.pad(start_row[:, count:], ((0, 0), (0, 4 * count - 48))),
            jnp.zeros((members - basis_parts - 14, 4 * count), jnp.float32),
        ],
        axis=0,
    )
    received = trade(
        jnp.concatenate([to_carriers(products), shares], axis=1), "sub"
    )
    share = everyone(jnp.sum(received[:, piece:], axis=0), "clu").reshape(clusters, 4, count)
    whole = jnp.pad(jnp.sum(share, axis=0), ((0, clusters - 4), (0, 0)))
    beside = jnp.pad(share[:, :3], ((1, 1), (0, 0), (0, 0)))
    shifted = beside[2:, 0] + beside[1:-1, 1] + beside[:-2, 2]
    is_coarse = (sub_index >= basis_parts) & (sub_index < basis_parts + 12)
    is_listed = sub_index == basis_parts + 13
    share = jnp.where(is_coarse, shifted, jnp.where(is_listed, share[:, 0], whole))
    share_size = clusters * count
    received = trade(
        jnp.concatenate(
            [
                carry(received[:, :piece]),
                jnp.broadcast_to(share.reshape(1, share_size), (members, share_size)),
            ],
            axis=1,
        ),
        "sub",
    )
    images = (
        live
        * (products.reshape(count, 6, slots) + six_faces(from_carriers(received[:, :piece]), low, high))
    ).reshape(count, width)
    parts = received[:, piece:].reshape(members, clusters, count)
    energy_raw = parts[:basis_parts, :4].reshape(count, count)
    image_coarse = parts[basis_parts : basis_parts + 6].transpose(1, 0, 2).reshape(coarse, count)
    image_weighted = parts[basis_parts + 6 : basis_parts + 12].transpose(1, 0, 2).reshape(coarse, count)
    start_sums = parts[basis_parts + 12, 0][:, None]
    listed = parts[basis_parts + 13, :, 24:48].reshape(clusters, 6, 4)[:, :, :3]
    start_weighted = dot(spread, listed.transpose(0, 2, 1).reshape(18 * clusters, 1))
    energy_inverse = spd_inverse(0.5 * (energy_raw + energy_raw.T))
    amount = dot(energy_inverse, start_sums)

    mixed = dot(amount.T, jnp.concatenate([basis, images], axis=1))
    solution = mixed[:, :width]
    shift = dot(coarse_inverse, dot(image_coarse, amount))
    residual = start - mixed[:, width:] + dot(nearby(shift).T, cols)
    weighted_residual = start_weighted - dot(image_weighted, amount) + dot(weighted_matrix, shift)
    amounts = dot(coarse_inverse, weighted_residual)
    search = weights * residual - dot(nearby(amounts).T, cols)
    weighted_images = weights * images
    parts_mixed = jnp.concatenate([cols, basis], axis=0)
    weighted_inverse = dot(coarse_inverse, weighted_matrix)
    by_shift = dot(energy_inverse, image_weighted.T)
    by_amounts = dot(energy_inverse, image_coarse.T)

    sums_row = padded_row(
        dot_t(jnp.concatenate([products, 0.5 * residual], axis=0), weights * residual)
    )
    received = everyone(
        jnp.concatenate([sums_row, weights[0, : 4 * slots]]), "sub"
    )
    all_weights = received[:, LANES:].reshape(slots_of, slots)
    totals = jnp.sum(
        everyone(jnp.sum(received[:, :LANES], axis=0), "clu"), axis=0, keepdims=True
    )
    rho = totals[:, count : count + 1]
    coeff = dot(energy_inverse, totals[:, :count].T) - dot(by_amounts, amounts)
    deflated_search = search - dot(coeff.T, basis)
    direction = deflated_search
    for iteration in range(ITERS):
        last = iteration + 1 == ITERS
        product = flat_live * jnp.dot(
            direction.astype(jnp.bfloat16), local_op, preferred_element_type=jnp.float32
        )
        faces = product.reshape(6, slots)
        low, high = rims(faces[None])
        tests = [both_cols, direction]
        if not last:
            tests += [weights * residual, weighted_images]
        sums = dot_t(product, jnp.concatenate(tests, axis=0))
        if not last:
            beside = jnp.concatenate([jnp.zeros((1, 4 * slots), jnp.float32), low, high], axis=1)
            square = jnp.sum(weights * product * (product + beside), axis=1, keepdims=True)
            sums = jnp.concatenate([sums, square], axis=1)
        received = everyone(
            jnp.concatenate([product[0, : 4 * slots], padded_row(sums)]), "sub"
        )
        all_faces = received[:, : 4 * slots].reshape(slots_of, slots)
        all_partners = dot(route, all_faces)
        inner = lax.dynamic_slice_in_dim(all_partners, 4 * sub_index, 4, 0)
        assembled = (live * (faces + jnp.concatenate([inner, low, high], axis=0))).reshape(1, width)
        sums = jnp.sum(received[:, 4 * slots :], axis=0, keepdims=True)
        if not last:
            cross = jnp.sum(
                jnp.sum(all_weights * all_faces * all_partners, axis=0, keepdims=True),
                axis=1,
                keepdims=True,
            )
            lane = lax.broadcasted_iota(jnp.int32, sums.shape, 1)
            sums = sums + jnp.where(lane == 38 + count, cross, 0.0)
        gathered = everyone(sums[0], "clu")
        pair = dot(
            spread,
            gathered[:, :36].reshape(clusters, 2, 18).transpose(0, 2, 1).reshape(18 * clusters, 2),
        )
        totals = jnp.sum(gathered, axis=0, keepdims=True)
        step = rho / totals[:, 36:37]
        shifts = dot(coarse_inverse, pair)
        shift = shifts[:, :1]
        if last:
            image = assembled - dot(nearby(shift).T, cols)
            solution = solution + step * direction
            residual = residual - step * image
            break
        turned = shifts[:, 1:] - dot(weighted_inverse, shift)
        coeff_change = (
            dot(energy_inverse, totals[:, 38 : 38 + count].T)
            - dot(by_shift, shift)
            - dot(by_amounts, turned)
        )
        near = nearby(jnp.concatenate([shift, turned], axis=1))
        mixed = dot(
            jnp.concatenate([near, jnp.concatenate([jnp.zeros_like(coeff_change), coeff_change], axis=1)], axis=0).T,
            parts_mixed,
        )
        image = assembled - mixed[:1]
        cross = totals[:, 37:38] - dot(shift.T, weighted_residual)
        weighted_shift = dot(weighted_matrix, shift)
        square = totals[:, 38 + count : 39 + count] - dot(shift.T, 2.0 * pair[:, 1:] - weighted_shift)
        rho_next = rho - step * (2.0 * cross - step * square)
        weighted_residual = weighted_residual - step * (pair[:, 1:] - weighted_shift)
        solution = solution + step * direction
        residual = residual - step * image
        deflated_search = deflated_search - step * (weights * image - mixed[1:])
        direction = deflated_search + rho_next / rho * direction
        rho = rho_next
    return (solution.reshape(1, 1, 6, slots), residual.reshape(1, 1, 6, slots))


def solution(mesh):
    return jax.shard_map(
        local,
        mesh=mesh,
        in_specs=(
            P("clu", "sub", None, None),
            P("clu", "sub", None),
            P("clu", "sub", None),
            P("clu", "sub", None, None),
            P("clu", "sub", None, None),
            P("clu", "sub", None, None, None),
            P("clu", "sub", None, None, None),
        ),
        out_specs=(P("clu", "sub", None, None), P("clu", "sub", None, None)),
        check_vma=False,
    )
```

time: 1800 us -> 325 us (0.18)
  blocking collectives: 1240 us -> 12.9 us
  waiting for transfers between devices: 356 us -> 113 us
  starting transfers between devices: 66.7 us -> 103 us
  other arithmetic: 45.4 us -> 9.77 us
    psum x13 -> x0, blocking collectives: 1240 us -> none  [the longest x4 379 us: precondition(): lax.psum((local_dot(current, search), local_dot(deflated, search)), ('sub...]
    psum x1 -> x0, waiting for transfers between devices: 259 us -> none  [local(): lax.psum((gram_pad, coarse_terms(rigid_cols, combined, clu_index, cluster...]
    all_to_all x5 -> x13, starting transfers between devices: 36.1 us -> 76.7 us  [the longest x9 52.8 us: everyone(): lax.all_to_all(sent, axis, split_axis=0, concat_axis=0, tiled=True)[:, 0, :]]
    another operation x17 -> x0, other arithmetic: 30.5 us -> none  [the longest x6 16 us: spd_solve(): factor_low = jnp.linalg.cholesky(matrix)]
    all_to_all x5 -> x13, waiting for transfers between devices: 97.3 us -> 105 us  [the longest x9 65.8 us: everyone(): lax.all_to_all(sent, axis, split_axis=0, concat_axis=0, tiled=True)[:, 0, :]]
    dot_general x41 -> x57, matrix products: 37.9 us -> 33.1 us  [the longest x45 16.4 us: dot(): jnp.dot(first, second, precision=precise, preferred_element_type=jnp.floa...]
  transfers between devices with their start and end apart: 16 -> 23, of which waited for: 6 -> 18; matrix products, arithmetic and copies ran while one was open for 1% -> 2% of each run, Pallas kernels for 0% -> 0%
where the time goes in v1:
time: 325 us; the launch traced here: 323 us
  waiting for transfers between devices  113 us (35%)
  starting transfers between devices  103 us (32%)
  matrix products  33.1 us (10%)
  local copies, waits for them, and re-layouts  23.1 us (7%)
  Pallas kernels  16.2 us (5%)
  blocking collectives  12.9 us (4%)
  between operations  11.3 us (3%)
  other arithmetic  9.77 us (3%)
    all_to_all x9, waiting for transfers between devices, everyone(): lax.all_to_all(sent, axis, split_axis=0, concat_axis=0, tiled=True)[:, 0, :]  65.8 us
    all_to_all x9, starting transfers between devices, everyone(): lax.all_to_all(sent, axis, split_axis=0, concat_axis=0, tiled=True)[:, 0, :]  52.8 us
    all_to_all x4, waiting for transfers between devices, trade(): lax.all_to_all(rows[:, None, :], axis, split_axis=0, concat_axis=0, tiled...  39.3 us
    all_to_all x4, starting transfers between devices, trade(): lax.all_to_all(rows[:, None, :], axis, split_axis=0, concat_axis=0, tiled...  23.9 us
    dot_general x45, matrix products, dot(): jnp.dot(first, second, precision=precise, preferred_element_type=jnp.floa...  16.4 us
    ppermute x5, starting transfers between devices, rims(): low = lax.ppermute(values[:, 5, :], 'clu', forward)  16.4 us
    pallas_call x2, Pallas kernels, spd_inverse(): pl.pallas_call(invert, out_shape=jax.ShapeDtypeStruct((size, size), jnp.f...  16.2 us
    all_to_all x1, blocking collectives, everyone(): lax.all_to_all(sent, axis, split_axis=0, concat_axis=0, tiled=True)[:, 0, :]  12.9 us
  transfers between devices with their start and end apart: 23, of which 18 were waited for; matrix products, arithmetic and copies ran while one was open for 2% of the time, Pallas kernels for 0%

profile of v1, /device:TPU:1, one launch (start us, length us, event | category | flops | bytes accessed | tf_op | source)
XLA Modules:
  0.0 322.9 jit_solution(4772559294990989920)
XLA Ops:
  5.4 1.3 copy.138
  6.7 10.5 %all-to-all-start = ((f32[32,1,4224]{2,1,0:T(1,128)}), f32[32,1,4224]{2,1,0:T(1,128)S(1)}, u32[]{:S(2)}, u32[]{:S(2)}) async-start(f32[32,1,4224]{2,1,0:T(1,128)} %copy.138), calls=%async_computation | async-start | bytes 1081344 | tf_op jit(solution)/shard_map/all_to_all | solution.py:37
  17.3 4.8 %collective-permute-start = (f32[72,256]{1,0:T(8,128)S(1)}, f32[72,256]{1,0:T(8,128)S(1)}, u32[]{:S(2)}, u32[]{:S(2)}) collective-permute-start(f32[72,256]{1,0:T(8,128)S(1)} %get-tuple-element.34), channel_id=1, source_target_pairs={{0,1},{1,2},{2,3},{3,4},{4,5},{5,6},{6,7},{7,8},{8,9},{9,10},{10,1... | collective-permute-start | bytes 221192 | tf_op jit(solution)/shard_map/ppermute | solution.py:44
  22.2 1.9 collective-permute-start.1
  24.6 3.6 %collective-permute-done.1 = f32[72,256]{1,0:T(8,128)S(1)} collective-permute-done((f32[72,256]{1,0:T(8,128)S(1)}, f32[72,256]{1,0:T(8,128)S(1)}, u32[]{:S(2)}, u32[]{:S(2)}) %collective-permute-start.1) | collective-permute-done | bytes 73760 | tf_op jit(solution)/shard_map/ppermute | solution.py:45
  28.2 5.7 %all-to-all-done = f32[32,1,4224]{2,1,0:T(1,128)S(1)} async-done(((f32[32,1,4224]{2,1,0:T(1,128)}), f32[32,1,4224]{2,1,0:T(1,128)S(1)}, u32[]{:S(2)}, u32[]{:S(2)}) %all-to-all-start) | async-done | bytes 540704 | tf_op jit(solution)/shard_map/all_to_all | solution.py:37
  36.1 1.1 broadcast_in_dim.175
  37.2 5.3 %all-to-all-start.1 = ((f32[32,1,3968]{2,1,0:T(1,128)}), f32[32,1,3968]{2,1,0:T(1,128)S(1)}, u32[]{:S(2)}, u32[]{:S(2)}) async-start(f32[32,1,3968]{2,1,0:T(1,128)} %broadcast_in_dim.175), calls=%async_computation.1 | async-start | bytes 1015808 | tf_op jit(solution)/shard_map/all_to_all | solution.py:37
  43.1 14.2 %all-to-all-done.1 = f32[32,1,3968]{2,1,0:T(1,128)S(1)} async-done(((f32[32,1,3968]{2,1,0:T(1,128)}), f32[32,1,3968]{2,1,0:T(1,128)S(1)}, u32[]{:S(2)}, u32[]{:S(2)}) %all-to-all-start.1) | async-done | bytes 507936 | tf_op jit(solution)/shard_map/all_to_all | solution.py:37
  58.4 14.0 %all-to-all-start.2 = ((f32[16,1,1920]{2,1,0:T(1,128)}), f32[16,1,1920]{2,1,0:T(1,128)S(1)}, u32[]{:S(2)}, u32[]{:S(2)}) async-start(f32[16,1,1920]{2,1,0:T(1,128)} %broadcast_in_dim.178), calls=%async_computation.2 | async-start | bytes 245760 | tf_op jit(solution)/shard_map/all_to_all | solution.py:33
  72.8 8.6 %all-to-all-done.2 = f32[16,1,1920]{2,1,0:T(1,128)S(1)} async-done(((f32[16,1,1920]{2,1,0:T(1,128)}), f32[16,1,1920]{2,1,0:T(1,128)S(1)}, u32[]{:S(2)}, u32[]{:S(2)}) %all-to-all-start.2) | async-done | bytes 122912 | tf_op jit(solution)/shard_map/all_to_all | solution.py:33
  84.0 9.5 %shard_map.86 = f32[96,96]{1,0:T(8,128)} custom-call(f32[96,96]{1,0:T(8,128)} %copy.189.matrix_ref), custom_call_target="tpu_custom_call" | custom-call | flops 1769472 | bytes 73728 | tf_op jit(solution)/shard_map/pallas_call | solution.py:72
  95.2 3.3 %fusion.8 = f32[64,1536]{1,0:T(8,128)S(1)} fusion(bf16[1,1,1536,1536]{3,2,1,0:T(8,128)(2,1)} %param.7, f32[1536]{0:T(1024)S(1)} %get-tuple-element.26, f32[65,1536]{1,0:T(8,128)S(1)} %convolution_subtract_fusion), kind=kOutput, calls=%fused_computation.9 | convolution fusion | flops 302088192 | bytes 5316608 | tf_op jit(solution)/shard_map/dot_general | solution.py:198
  101.5 4.2 %all-to-all-start.3 = ((f32[32,1,2304]{2,1,0:T(1,128)}), f32[32,1,2304]{2,1,0:T(1,128)S(1)}, u32[]{:S(2)}, u32[]{:S(2)}) async-start(f32[32,1,2304]{2,1,0:T(1,128)} %copy.150), calls=%async_computation.3 | async-start | bytes 589824 | tf_op jit(solution)/shard_map/all_to_all | solution.py:37
  105.7 12.8 %all-to-all-done.3 = f32[32,1,2304]{2,1,0:T(1,128)S(1)} async-done(((f32[32,1,2304]{2,1,0:T(1,128)}), f32[32,1,2304]{2,1,0:T(1,128)S(1)}, u32[]{:S(2)}, u32[]{:S(2)}) %all-to-all-start.3) | async-done | bytes 294944 | tf_op jit(solution)/shard_map/all_to_all | solution.py:37
  119.3 4.9 %all-to-all-start.4 = ((f32[16,1,256]{2,1,0:T(1,128)}), f32[16,1,256]{2,1,0:T(1,128)S(1)}, u32[]{:S(2)}, u32[]{:S(2)}) async-start(f32[16,1,256]{2,1,0:T(1,128)} %broadcast_in_dim.181), calls=%async_computation.4 | async-start | bytes 32768 | tf_op jit(solution)/shard_map/all_to_all | solution.py:33
  124.8 6.8 %all-to-all-done.4 = f32[16,1,256]{2,1,0:T(1,128)S(1)} async-done(((f32[16,1,256]{2,1,0:T(1,128)}), f32[16,1,256]{2,1,0:T(1,128)S(1)}, u32[]{:S(2)}, u32[]{:S(2)}) %all-to-all-start.4) | async-done | bytes 16416 | tf_op jit(solution)/shard_map/all_to_all | solution.py:33
  133.0 3.9 %all-to-all-start.5 = ((f32[32,1,3072]{2,1,0:T(1,128)}), f32[32,1,3072]{2,1,0:T(1,128)S(1)}, u32[]{:S(2)}, u32[]{:S(2)}) async-start(f32[32,1,3072]{2,1,0:T(1,128)} %broadcast_in_dim.184), calls=%async_computation.5 | async-start | bytes 786432 | tf_op jit(solution)/shard_map/all_to_all | solution.py:37
  137.2 2.4 collective-permute-start.3
  139.6 3.4 %collective-permute-start.2 = (f32[64,256]{1,0:T(8,128)S(1)}, f32[64,256]{1,0:T(8,128)S(1)}, u32[]{:S(2)}, u32[]{:S(2)}) collective-permute-start(f32[64,256]{1,0:T(8,128)S(1)} %bitcast.494), channel_id=1, source_target_pairs={{0,1},{1,2},{2,3},{3,4},{4,5},{5,6},{6,7},{7,8},{8,9},{9,10},{10,1... | collective-permute-start | bytes 196616 | tf_op jit(solution)/shard_map/ppermute | solution.py:44
  144.2 6.7 %all-to-all-done.5 = f32[32,1,3072]{2,1,0:T(1,128)S(1)} async-done(((f32[32,1,3072]{2,1,0:T(1,128)}), f32[32,1,3072]{2,1,0:T(1,128)S(1)}, u32[]{:S(2)}, u32[]{:S(2)}) %all-to-all-start.5) | async-done | bytes 393248 | tf_op jit(solution)/shard_map/all_to_all | solution.py:37
  152.9 6.7 %shard_map.87 = f32[64,64]{1,0:T(8,128)} custom-call(f32[64,64]{1,0:T(8,128)} %fusion.112.matrix_ref), custom_call_target="tpu_custom_call" | custom-call | flops 524288 | bytes 32768 | tf_op jit(solution)/shard_map/pallas_call | solution.py:72
  163.8 4.8 %all-to-all-start.6 = ((f32[32,1,1152]{2,1,0:T(1,128)}), f32[32,1,1152]{2,1,0:T(1,128)S(1)}, u32[]{:S(2)}, u32[]{:S(2)}) async-start(f32[32,1,1152]{2,1,0:T(1,128)} %broadcast_in_dim.187), calls=%async_computation.6 | async-start | bytes 294912 | tf_op jit(solution)/shard_map/all_to_all | solution.py:33
  169.1 9.0 %all-to-all-done.6 = f32[32,1,1152]{2,1,0:T(1,128)S(1)} async-done(((f32[32,1,1152]{2,1,0:T(1,128)}), f32[32,1,1152]{2,1,0:T(1,128)S(1)}, u32[]{:S(2)}, u32[]{:S(2)}) %all-to-all-start.6) | async-done | bytes 147488 | tf_op jit(solution)/shard_map/all_to_all | solution.py:33
  178.8 6.3 %all-to-all-start.7 = ((f32[16,1,128]{2,1,0:T(1,128)}), f32[16,1,128]{2,1,0:T(1,128)S(1)}, u32[]{:S(2)}, u32[]{:S(2)}) async-start(f32[16,1,128]{2,1,0:T(1,128)} %broadcast_in_dim.188), calls=%async_computation.7 | async-start | bytes 16384 | tf_op jit(solution)/shard_map/all_to_all | solution.py:33
  185.3 6.8 %all-to-all-done.7 = f32[16,1,128]{2,1,0:T(1,128)S(1)} async-done(((f32[16,1,128]{2,1,0:T(1,128)}), f32[16,1,128]{2,1,0:T(1,128)S(1)}, u32[]{:S(2)}, u32[]{:S(2)}) %all-to-all-start.7) | async-done | bytes 8224 | tf_op jit(solution)/shard_map/all_to_all | solution.py:33
  192.8 3.1 fusion.11
  196.0 2.7 collective-permute-start.4
  198.7 1.9 collective-permute-start.5
  201.8 1.8 collective-permute-done.5
  205.7 3.9 %all-to-all-start.8 = ((f32[32,1,1152]{2,1,0:T(1,128)}), f32[32,1,1152]{2,1,0:T(1,128)S(1)}, u32[]{:S(2)}, u32[]{:S(2)}) async-start(f32[32,1,1152]{2,1,0:T(1,128)} %broadcast_in_dim.191), calls=%async_computation.8 | async-start | bytes 294912 | tf_op jit(solution)/shard_map/all_to_all | solution.py:33
  210.6 8.6 %all-to-all-done.8 = f32[32,1,1152]{2,1,0:T(1,128)S(1)} async-done(((f32[32,1,1152]{2,1,0:T(1,128)}), f32[32,1,1152]{2,1,0:T(1,128)S(1)}, u32[]{:S(2)}, u32[]{:S(2)}) %all-to-all-start.8) | async-done | bytes 147488 | tf_op jit(solution)/shard_map/all_to_all | solution.py:33
  221.6 4.8 %all-to-all-start.9 = ((f32[16,1,128]{2,1,0:T(1,128)}), f32[16,1,128]{2,1,0:T(1,128)S(1)}, u32[]{:S(2)}, u32[]{:S(2)}) async-start(f32[16,1,128]{2,1,0:T(1,128)} %broadcast_in_dim.194), calls=%async_computation.9 | async-start | bytes 16384 | tf_op jit(solution)/shard_map/all_to_all | solution.py:33
  226.4 7.0 %all-to-all-done.9 = f32[16,1,128]{2,1,0:T(1,128)S(1)} async-done(((f32[16,1,128]{2,1,0:T(1,128)}), f32[16,1,128]{2,1,0:T(1,128)S(1)}, u32[]{:S(2)}, u32[]{:S(2)}) %all-to-all-start.9) | async-done | bytes 8224 | tf_op jit(solution)/shard_map/all_to_all | solution.py:33
  242.1 3.1 fusion.14
  245.2 2.7 collective-permute-start.6
  248.0 1.9 collective-permute-start.7
  251.0 1.8 collective-permute-done.7
  254.3 12.9 %all_to_all.70 = f32[32,1,1152]{2,1,0:T(1,128)S(1)} all-to-all(f32[32,1,1152]{2,1,0:T(1,128)S(1)} %broadcast_in_dim.197), channel_id=1, replica_groups=mesh['sub'=32,'clu'=16] {'sub'}, dimensions={0} | all-to-all | bytes 294912 | tf_op jit(solution)/shard_map/all_to_all | solution.py:33
  269.4 4.6 %all-to-all-start.11 = ((f32[16,1,128]{2,1,0:T(1,128)}), f32[16,1,128]{2,1,0:T(1,128)S(1)}, u32[]{:S(2)}, u32[]{:S(2)}) async-start(f32[16,1,128]{2,1,0:T(1,128)} %broadcast_in_dim.199), calls=%async_computation.11 | async-start | bytes 16384 | tf_op jit(solution)/shard_map/all_to_all | solution.py:33
  274.0 7.0 %all-to-all-done.11 = f32[16,1,128]{2,1,0:T(1,128)S(1)} async-done(((f32[16,1,128]{2,1,0:T(1,128)}), f32[16,1,128]{2,1,0:T(1,128)S(1)}, u32[]{:S(2)}, u32[]{:S(2)}) %all-to-all-start.11) | async-done | bytes 8224 | tf_op jit(solution)/shard_map/all_to_all | solution.py:33
  288.2 3.1 fusion.17
  292.4 3.9 %all-to-all-start.12 = ((f32[32,1,1152]{2,1,0:T(1,128)}), f32[32,1,1152]{2,1,0:T(1,128)S(1)}, u32[]{:S(2)}, u32[]{:S(2)}) async-start(f32[32,1,1152]{2,1,0:T(1,128)} %broadcast_in_dim.201), calls=%async_computation.12 | async-start | bytes 294912 | tf_op jit(solution)/shard_map/all_to_all | solution.py:33
  296.3 2.7 collective-permute-start.8
  299.0 1.9 collective-permute-start.9
  301.0 4.8 %all-to-all-done.12 = f32[32,1,1152]{2,1,0:T(1,128)S(1)} async-done(((f32[32,1,1152]{2,1,0:T(1,128)}), f32[32,1,1152]{2,1,0:T(1,128)S(1)}, u32[]{:S(2)}, u32[]{:S(2)}) %all-to-all-start.12) | async-done | bytes 147488 | tf_op jit(solution)/shard_map/all_to_all | solution.py:33
  306.8 5.6 %all-to-all-start.13 = ((f32[16,1,128]{2,1,0:T(1,128)}), f32[16,1,128]{2,1,0:T(1,128)S(1)}, u32[]{:S(2)}, u32[]{:S(2)}) async-start(f32[16,1,128]{2,1,0:T(1,128)} %broadcast_in_dim.202), calls=%async_computation.13 | async-start | bytes 16384 | tf_op jit(solution)/shard_map/all_to_all | solution.py:33
  312.5 7.0 %all-to-all-done.13 = f32[16,1,128]{2,1,0:T(1,128)S(1)} async-done(((f32[16,1,128]{2,1,0:T(1,128)}), f32[16,1,128]{2,1,0:T(1,128)S(1)}, u32[]{:S(2)}, u32[]{:S(2)}) %all-to-all-start.13) | async-done | bytes 8224 | tf_op jit(solution)/shard_map/all_to_all | solution.py:33
  (309 shorter events, 52.1 us)
Async XLA Ops:
  0.6 33.2 %copy-start.7 = (s32[1,1,4]{2,1,0:T(1,128)S(1)}, s32[1,1,4]{2,1,0:T(1,128)}, u32[]{:S(2)}) copy-start(s32[1,1,4]{2,1,0:T(1,128)} %param.8) | copy-start | bytes 52
  0.6 16.6 %copy-start.4 = (f32[1,1,6,256]{3,1,2,0:T(1,128)S(1)}, f32[1,1,6,256]{3,1,2,0:T(1,128)}, u32[]{:S(2)}) copy-start(f32[1,1,6,256]{3,1,2,0:T(1,128)} %param.11) | copy-start | bytes 18436
  0.7 16.6 %copy-start.5 = (f32[1,1,6,256]{3,1,2,0:T(1,128)S(1)}, f32[1,1,6,256]{3,1,2,0:T(1,128)}, u32[]{:S(2)}) copy-start(f32[1,1,6,256]{3,1,2,0:T(1,128)} %param.10) | copy-start | bytes 18436
  0.7 16.6 %copy-start.1 = (bf16[1,1,64,6,256]{4,2,3,1,0:T(8,128)(2,1)S(1)}, bf16[1,1,64,6,256]{4,2,3,1,0:T(8,128)(2,1)}, u32[]{:S(2)}) copy-start(bf16[1,1,64,6,256]{4,2,3,1,0:T(8,128)(2,1)} %param.13) | copy-start | bytes 589828
  0.7 23.5 %copy-start.6 = (s32[1,1,6]{2,1,0:T(1,128)S(1)}, s32[1,1,6]{2,1,0:T(1,128)}, u32[]{:S(2)}) copy-start(s32[1,1,6]{2,1,0:T(1,128)} %param.9) | copy-start | bytes 76
  4.2 30.7 %copy-start.3 = (f32[1,1,6,6,256]{4,1,3,2,0:T(1,128)S(1)}, f32[1,1,6,6,256]{4,1,3,2,0:T(1,128)}, u32[]{:S(2)}) copy-start(f32[1,1,6,6,256]{4,1,3,2,0:T(1,128)} %param.12) | copy-start | bytes 110596
  6.7 27.1 %all-to-all-start = ((f32[32,1,4224]{2,1,0:T(1,128)}), f32[32,1,4224]{2,1,0:T(1,128)S(1)}, u32[]{:S(2)}, u32[]{:S(2)}) async-start(f32[32,1,4224]{2,1,0:T(1,128)} %copy.138), calls=%async_computation | async-start | bytes 1081344 | tf_op jit(solution)/shard_map/all_to_all | solution.py:37
  17.3 7.2 %collective-permute-start = (f32[72,256]{1,0:T(8,128)S(1)}, f32[72,256]{1,0:T(8,128)S(1)}, u32[]{:S(2)}, u32[]{:S(2)}) collective-permute-start(f32[72,256]{1,0:T(8,128)S(1)} %get-tuple-element.34), channel_id=1, source_target_pairs={{0,1},{1,2},{2,3},{3,4},{4,5},{5,6},{6,7},{7,8},{8,9},{9,10},{10,1... | collective-permute-start | bytes 221192 | tf_op jit(solution)/shard_map/ppermute | solution.py:44
  22.2 6.0 %collective-permute-start.1 = (f32[72,256]{1,0:T(8,128)S(1)}, f32[72,256]{1,0:T(8,128)S(1)}, u32[]{:S(2)}, u32[]{:S(2)}) collective-permute-start(f32[72,256]{1,0:T(8,128)S(1)} %get-tuple-element.35), channel_id=1, source_target_pairs={{1,0},{2,1},{3,2},{4,3},{5,4},{6,5},{7,6},{8,7},{9,8},{10,9},{11,1... | collective-permute-start | bytes 221192 | tf_op jit(solution)/shard_map/ppermute | solution.py:45
  37.2 20.1 %all-to-all-start.1 = ((f32[32,1,3968]{2,1,0:T(1,128)}), f32[32,1,3968]{2,1,0:T(1,128)S(1)}, u32[]{:S(2)}, u32[]{:S(2)}) async-start(f32[32,1,3968]{2,1,0:T(1,128)} %broadcast_in_dim.175), calls=%async_computation.1 | async-start | bytes 1015808 | tf_op jit(solution)/shard_map/all_to_all | solution.py:37
  58.4 23.0 %all-to-all-start.2 = ((f32[16,1,1920]{2,1,0:T(1,128)}), f32[16,1,1920]{2,1,0:T(1,128)S(1)}, u32[]{:S(2)}, u32[]{:S(2)}) async-start(f32[16,1,1920]{2,1,0:T(1,128)} %broadcast_in_dim.178), calls=%async_computation.2 | async-start | bytes 245760 | tf_op jit(solution)/shard_map/all_to_all | solution.py:33
  101.5 17.0 %all-to-all-start.3 = ((f32[32,1,2304]{2,1,0:T(1,128)}), f32[32,1,2304]{2,1,0:T(1,128)S(1)}, u32[]{:S(2)}, u32[]{:S(2)}) async-start(f32[32,1,2304]{2,1,0:T(1,128)} %copy.150), calls=%async_computation.3 | async-start | bytes 589824 | tf_op jit(solution)/shard_map/all_to_all | solution.py:37
  119.3 12.3 %all-to-all-start.4 = ((f32[16,1,256]{2,1,0:T(1,128)}), f32[16,1,256]{2,1,0:T(1,128)S(1)}, u32[]{:S(2)}, u32[]{:S(2)}) async-start(f32[16,1,256]{2,1,0:T(1,128)} %broadcast_in_dim.181), calls=%async_computation.4 | async-start | bytes 32768 | tf_op jit(solution)/shard_map/all_to_all | solution.py:33
  124.2 36.6 %copy-start = (f32[96,96]{1,0:T(8,128)S(1)}, f32[96,96]{1,0:T(8,128)}, u32[]{:S(2)}) copy-start(f32[96,96]{1,0:T(8,128)} %shard_map.86) | copy-start | bytes 110596
  133.0 17.8 %all-to-all-start.5 = ((f32[32,1,3072]{2,1,0:T(1,128)}), f32[32,1,3072]{2,1,0:T(1,128)S(1)}, u32[]{:S(2)}, u32[]{:S(2)}) async-start(f32[32,1,3072]{2,1,0:T(1,128)} %broadcast_in_dim.184), calls=%async_computation.5 | async-start | bytes 786432 | tf_op jit(solution)/shard_map/all_to_all | solution.py:37
  137.2 5.9 %collective-permute-start.3 = (f32[64,256]{1,0:T(8,128)S(1)}, f32[64,256]{1,0:T(8,128)S(1)}, u32[]{:S(2)}, u32[]{:S(2)}) collective-permute-start(f32[64,256]{1,0:T(8,128)S(1)} %bitcast.492), channel_id=1, source_target_pairs={{1,0},{2,1},{3,2},{4,3},{5,4},{6,5},{7,6},{8,7},{9,8},{10,9},{11,1... | collective-permute-start | bytes 196616 | tf_op jit(solution)/shard_map/ppermute | solution.py:45
  139.6 4.5 %collective-permute-start.2 = (f32[64,256]{1,0:T(8,128)S(1)}, f32[64,256]{1,0:T(8,128)S(1)}, u32[]{:S(2)}, u32[]{:S(2)}) collective-permute-start(f32[64,256]{1,0:T(8,128)S(1)} %bitcast.494), channel_id=1, source_target_pairs={{0,1},{1,2},{2,3},{3,4},{4,5},{5,6},{6,7},{7,8},{8,9},{9,10},{10,1... | collective-permute-start | bytes 196616 | tf_op jit(solution)/shard_map/ppermute | solution.py:44
  159.7 25.5 %copy-start.2 = (f32[64,64]{1,0:T(8,128)S(1)}, f32[64,64]{1,0:T(8,128)}, u32[]{:S(2)}) copy-start(f32[64,64]{1,0:T(8,128)} %shard_map.87) | copy-start | bytes 49156
  163.8 14.3 %all-to-all-start.6 = ((f32[32,1,1152]{2,1,0:T(1,128)}), f32[32,1,1152]{2,1,0:T(1,128)S(1)}, u32[]{:S(2)}, u32[]{:S(2)}) async-start(f32[32,1,1152]{2,1,0:T(1,128)} %broadcast_in_dim.187), calls=%async_computation.6 | async-start | bytes 294912 | tf_op jit(solution)/shard_map/all_to_all | solution.py:33
  178.8 13.4 %all-to-all-start.7 = ((f32[16,1,128]{2,1,0:T(1,128)}), f32[16,1,128]{2,1,0:T(1,128)S(1)}, u32[]{:S(2)}, u32[]{:S(2)}) async-start(f32[16,1,128]{2,1,0:T(1,128)} %broadcast_in_dim.188), calls=%async_computation.7 | async-start | bytes 16384 | tf_op jit(solution)/shard_map/all_to_all | solution.py:33
  196.0 5.8 %collective-permute-start.4 = (f32[1,256]{1,0:T(1,128)S(1)}, f32[1,256]{1,0:T(1,128)S(1)}, u32[]{:S(2)}, u32[]{:S(2)}) collective-permute-start(f32[1,256]{1,0:T(1,128)S(1)} %get-tuple-element.51), channel_id=1, source_target_pairs={{0,1},{1,2},{2,3},{3,4},{4,5},{5,6},{6,7},{7,8},{8,9},{9,10},{10,1... | collective-permute-start | bytes 3080 | tf_op jit(solution)/shard_map/ppermute | solution.py:44
  198.7 4.9 %collective-permute-start.5 = (f32[1,256]{1,0:T(1,128)S(1)}, f32[1,256]{1,0:T(1,128)S(1)}, u32[]{:S(2)}, u32[]{:S(2)}) collective-permute-start(f32[1,256]{1,0:T(1,128)S(1)} %get-tuple-element.52), channel_id=1, source_target_pairs={{1,0},{2,1},{3,2},{4,3},{5,4},{6,5},{7,6},{8,7},{9,8},{10,9},{11,1... | collective-permute-start | bytes 3080 | tf_op jit(solution)/shard_map/ppermute | solution.py:45
  205.7 13.6 %all-to-all-start.8 = ((f32[32,1,1152]{2,1,0:T(1,128)}), f32[32,1,1152]{2,1,0:T(1,128)S(1)}, u32[]{:S(2)}, u32[]{:S(2)}) async-start(f32[32,1,1152]{2,1,0:T(1,128)} %broadcast_in_dim.191), calls=%async_computation.8 | async-start | bytes 294912 | tf_op jit(solution)/shard_map/all_to_all | solution.py:33
  221.6 11.8 %all-to-all-start.9 = ((f32[16,1,128]{2,1,0:T(1,128)}), f32[16,1,128]{2,1,0:T(1,128)S(1)}, u32[]{:S(2)}, u32[]{:S(2)}) async-start(f32[16,1,128]{2,1,0:T(1,128)} %broadcast_in_dim.194), calls=%async_computation.9 | async-start | bytes 16384 | tf_op jit(solution)/shard_map/all_to_all | solution.py:33
  245.2 5.8 %collective-permute-start.6 = (f32[1,256]{1,0:T(1,128)S(1)}, f32[1,256]{1,0:T(1,128)S(1)}, u32[]{:S(2)}, u32[]{:S(2)}) collective-permute-start(f32[1,256]{1,0:T(1,128)S(1)} %get-tuple-element.49), channel_id=1, source_target_pairs={{0,1},{1,2},{2,3},{3,4},{4,5},{5,6},{6,7},{7,8},{8,9},{9,10},{10,1... | collective-permute-start | bytes 3080 | tf_op jit(solution)/shard_map/ppermute | solution.py:44
  248.0 4.9 %collective-permute-start.7 = (f32[1,256]{1,0:T(1,128)S(1)}, f32[1,256]{1,0:T(1,128)S(1)}, u32[]{:S(2)}, u32[]{:S(2)}) collective-permute-start(f32[1,256]{1,0:T(1,128)S(1)} %get-tuple-element.50), channel_id=1, source_target_pairs={{1,0},{2,1},{3,2},{4,3},{5,4},{6,5},{7,6},{8,7},{9,8},{10,9},{11,1... | collective-permute-start | bytes 3080 | tf_op jit(solution)/shard_map/ppermute | solution.py:45
  269.4 11.6 %all-to-all-start.11 = ((f32[16,1,128]{2,1,0:T(1,128)}), f32[16,1,128]{2,1,0:T(1,128)S(1)}, u32[]{:S(2)}, u32[]{:S(2)}) async-start(f32[16,1,128]{2,1,0:T(1,128)} %broadcast_in_dim.199), calls=%async_computation.11 | async-start | bytes 16384 | tf_op jit(solution)/shard_map/all_to_all | solution.py:33
  292.4 13.3 %all-to-all-start.12 = ((f32[32,1,1152]{2,1,0:T(1,128)}), f32[32,1,1152]{2,1,0:T(1,128)S(1)}, u32[]{:S(2)}, u32[]{:S(2)}) async-start(f32[32,1,1152]{2,1,0:T(1,128)} %broadcast_in_dim.201), calls=%async_computation.12 | async-start | bytes 294912 | tf_op jit(solution)/shard_map/all_to_all | solution.py:33
  296.3 16.1 %collective-permute-start.8 = (f32[1,256]{1,0:T(1,128)S(1)}, f32[1,256]{1,0:T(1,128)S(1)}, u32[]{:S(2)}, u32[]{:S(2)}) collective-permute-start(f32[1,256]{1,0:T(1,128)S(1)} %get-tuple-element.47), channel_id=1, source_target_pairs={{0,1},{1,2},{2,3},{3,4},{4,5},{5,6},{6,7},{7,8},{8,9},{9,10},{10,1... | collective-permute-start | bytes 3080 | tf_op jit(solution)/shard_map/ppermute | solution.py:44
  299.0 13.4 %collective-permute-start.9 = (f32[1,256]{1,0:T(1,128)S(1)}, f32[1,256]{1,0:T(1,128)S(1)}, u32[]{:S(2)}, u32[]{:S(2)}) collective-permute-start(f32[1,256]{1,0:T(1,128)S(1)} %get-tuple-element.48), channel_id=1, source_target_pairs={{1,0},{2,1},{3,2},{4,3},{5,4},{6,5},{7,6},{8,7},{9,8},{10,9},{11,1... | collective-permute-start | bytes 3080 | tf_op jit(solution)/shard_map/ppermute | solution.py:45
  306.8 12.7 %all-to-all-start.13 = ((f32[16,1,128]{2,1,0:T(1,128)}), f32[16,1,128]{2,1,0:T(1,128)S(1)}, u32[]{:S(2)}, u32[]{:S(2)}) async-start(f32[16,1,128]{2,1,0:T(1,128)} %broadcast_in_dim.202), calls=%async_computation.13 | async-start | bytes 16384 | tf_op jit(solution)/shard_map/all_to_all | solution.py:33

commit v2 on v1

--- a/solution.py
+++ b/solution.py
@@ -1,3 +1,5 @@
+import functools
+
 import jax
 import jax.numpy as jnp
 from jax import lax
@@ -57,13 +59,23 @@
     row_lanes = lax.broadcasted_iota(jnp.int32, (1, size), 1)
     column_rows = lax.broadcasted_iota(jnp.int32, (size, 1), 0)
     values = matrix_ref[...]
-    for k in range(size):
-        pivot_row = values[k : k + 1, :]
-        reciprocal = 1.0 / pivot_row[:, k : k + 1]
-        scaled_row = jnp.where(row_lanes == k, 1.0, pivot_row) * reciprocal
-        column = jnp.where(column_rows == k, -1.0, values[:, k : k + 1])
-        kept = jnp.where((rows == k) | (lanes == k), 0.0, values)
-        values = kept - column * scaled_row
+    for k in range(0, size, 2):
+        first, second = values[k : k + 1, :], values[k + 1 : k + 2, :]
+        across = second[:, k : k + 1]
+        first_part = 1.0 / first[:, k : k + 1]
+        ratio = across * first_part
+        second_part = 1.0 / (second[:, k + 1 : k + 2] - ratio * across)
+        mixed_part = ratio * second_part
+        here, after = row_lanes == k, row_lanes == k + 1
+        first = jnp.where(here, 1.0, jnp.where(after, 0.0, first))
+        second = jnp.where(after, 1.0, jnp.where(here, 0.0, second))
+        first_scaled = (first_part + ratio * mixed_part) * first - mixed_part * second
+        second_scaled = second_part * second - mixed_part * first
+        here, after = column_rows == k, column_rows == k + 1
+        first_column = jnp.where(here, -1.0, jnp.where(after, 0.0, values[:, k : k + 1]))
+        second_column = jnp.where(after, -1.0, jnp.where(here, 0.0, values[:, k + 1 : k + 2]))
+        kept = jnp.where((rows // 2 == k // 2) | (lanes // 2 == k // 2), 0.0, values)
+        values = kept - first_column * first_scaled - second_column * second_scaled
     inverse_ref[...] = values
 
 
@@ -76,6 +88,126 @@
         out_specs=pl.BlockSpec(memory_space=pltpu.VMEM),
         cost_estimate=pl.CostEstimate(flops=2 * size**3, bytes_accessed=8 * size**2, transcendentals=size),
     )(matrix)
+
+
+PARTS = 4
+VMEM = pl.BlockSpec(memory_space=pltpu.VMEM)
+
+
+def lane_sum(values):
+    return jnp.sum(values, axis=1, keepdims=True)
+
+
+def row_sum(values):
+    return jnp.sum(values, axis=0, keepdims=True)
+
+
+def advance(count, gathered, image_sum, state, state_out, weighted, rho, weighted_out, rho_out, refs, again):
+    spread, mask, by_coarse, by_weighted, by_products, cols, basis, weights = refs
+    coarse = weighted.shape[0]
+    near = cols.shape[0]
+    values = gathered[:, :LANES]
+    high = values.astype(jnp.bfloat16)
+    rest = values - high.astype(jnp.float32)
+    middle = rest.astype(jnp.bfloat16)
+    low = (rest - middle.astype(jnp.float32)).astype(jnp.bfloat16)
+    lifted = (
+        jnp.dot(high, spread[...], preferred_element_type=jnp.float32)
+        + jnp.dot(middle, spread[...], preferred_element_type=jnp.float32)
+        + jnp.dot(low, spread[...], preferred_element_type=jnp.float32)
+    )
+    lifted = row_sum(lifted * mask[...])
+    coarse_row = lifted[:, :LANES] + lifted[:, LANES : 2 * LANES] + lifted[:, 2 * LANES : 3 * LANES]
+    weighted_row = (
+        lifted[:, 3 * LANES : 4 * LANES] + lifted[:, 4 * LANES : 5 * LANES] + lifted[:, 5 * LANES :]
+    )
+    totals = row_sum(values)
+    step = rho[...] / totals[:, 36:37]
+    from_coarse = lane_sum(by_coarse[...] * coarse_row)
+    from_weighted = lane_sum(by_weighted[...] * weighted_row)
+    shift = from_coarse[:coarse]
+    weighted_shift = from_coarse[coarse : 2 * coarse]
+    near_shift = from_coarse[2 * coarse : 2 * coarse + near]
+    image = image_sum[...] - row_sum(cols[...] * near_shift)
+    direction = state[0:1, :]
+    state_out[1:2, :] = state[1:2, :] + step * direction
+    state_out[2:3, :] = state[2:3, :] - step * image
+    if not again:
+        return
+    near_turned = from_coarse[2 * coarse + near : 2 * coarse + 2 * near] + from_weighted[coarse : coarse + near]
+    coeff_change = (
+        from_coarse[2 * coarse + 2 * near :]
+        + from_weighted[coarse + near :]
+        + lane_sum(by_products[...] * totals)
+    )
+    found_weighted = from_weighted[:coarse]
+    cross = totals[:, 37:38] - row_sum(shift * weighted[...])
+    square = lane_sum(row_sum(gathered[:, LANES:])) - row_sum(shift * (2.0 * found_weighted - weighted_shift))
+    rho_next = rho[...] - step * (2.0 * cross - step * square)
+    weighted_out[...] = weighted[...] - step * (found_weighted - weighted_shift)
+    rho_out[...] = rho_next
+    change = weights[...] * image - row_sum(cols[...] * near_turned) - row_sum(basis[...] * coeff_change)
+    deflated = state[3:4, :] - step * change
+    state_out[3:4, :] = deflated
+    state_out[0:1, :] = deflated + (rho_next / rho[...]) * direction
+
+
+def apply(count, operator, held, arrived, state, tests, images, weights, live, product, sums):
+    rows = held.shape[0] // PARTS
+    direction = state[0:1, :]
+    rounded = jnp.broadcast_to(direction, (16, direction.shape[1])).astype(jnp.bfloat16)
+    total = None
+    for part in range(PARTS):
+        pltpu.make_async_copy(
+            operator.at[pl.ds(part * rows, rows)], held.at[pl.ds(part * rows, rows)], arrived.at[part]
+        ).wait()
+        piece = jnp.dot(
+            rounded[:, part * rows : (part + 1) * rows],
+            held[part * rows : (part + 1) * rows, :],
+            preferred_element_type=jnp.float32,
+        )
+        total = piece if total is None else total + piece
+    found = live[...] * total[0:1, :]
+    product[...] = found
+    column = jnp.concatenate([lane_sum(tests[...] * found), lane_sum(images[...] * found)], axis=0)
+    size = column.shape[0]
+    rows_of = lax.broadcasted_iota(jnp.int32, (size, LANES), 0)
+    lanes_of = lax.broadcasted_iota(jnp.int32, (size, LANES), 1)
+    lane = lax.broadcasted_iota(jnp.int32, (1, LANES), 1)
+    row = row_sum(jnp.where(rows_of == lanes_of, column, 0.0))
+    row = row + jnp.where(lane == 36, lane_sum(direction * found), 0.0)
+    sums[...] = row + jnp.where(lane == 37, lane_sum(weights[...] * state[2:3, :] * found), 0.0)
+
+
+def fetch(operator, held, arrived):
+    rows = held.shape[0] // PARTS
+    for part in range(PARTS):
+        pltpu.make_async_copy(
+            operator.at[pl.ds(part * rows, rows)], held.at[pl.ds(part * rows, rows)], arrived.at[part]
+        ).start()
+
+
+def step_kernel(count, again, *refs):
+    if not again:
+        gathered, image_sum, state, weighted, rho, *rest = refs
+        advance(count, gathered, image_sum, state, rest[-1], weighted, rho, None, None, rest[:-1], False)
+        return
+    gathered, image_sum, state, weighted, rho = refs[:5]
+    shared = refs[5:13]
+    operator, tests, images, live = refs[13:17]
+    state_out, weighted_out, rho_out, product, sums, held, arrived = refs[17:]
+    fetch(operator, held, arrived)
+    advance(count, gathered, image_sum, state, state_out, weighted, rho, weighted_out, rho_out, shared, True)
+    apply(count, operator, held, arrived, state_out, tests, images, shared[-1], live, product, sums)
+
+
+def first_kernel(count, state, operator, tests, images, weights, live, product, sums, held, arrived):
+    fetch(operator, held, arrived)
+    apply(count, operator, held, arrived, state, tests, images, weights, live, product, sums)
+
+
+def shape_of(*dims):
+    return jax.ShapeDtypeStruct(dims, jnp.float32)
 
 
 def local(dual_ops, neighbors, face_counts, load_terms, precond_terms, rigid_terms, recycled_terms):
@@ -258,10 +390,43 @@
     amounts = dot(coarse_inverse, weighted_residual)
     search = weights * residual - dot(nearby(amounts).T, cols)
     weighted_images = weights * images
-    parts_mixed = jnp.concatenate([cols, basis], axis=0)
-    weighted_inverse = dot(coarse_inverse, weighted_matrix)
+    near_rows = lax.broadcasted_iota(jnp.int32, (24, coarse), 0)
+    near_lanes = lax.broadcasted_iota(jnp.int32, (24, coarse), 1)
+    near_select = ((near_lanes == 6 * clu_index + near_rows - 6) & (near_rows < 18)).astype(jnp.float32)
+    weighted_inverse = dot(weighted_matrix, coarse_inverse)
+    twice = dot(coarse_inverse, weighted_inverse)
+    both_near = dot(near_select, jnp.concatenate([coarse_inverse, twice], axis=1))
     by_shift = dot(energy_inverse, image_weighted.T)
     by_amounts = dot(energy_inverse, image_coarse.T)
+    weighted_coeff = -dot(by_amounts, coarse_inverse)
+    coarse_coeff = dot(by_amounts, twice) - dot(by_shift, coarse_inverse)
+    lane_pad = ((0, 0), (0, LANES - coarse))
+    by_coarse = jnp.pad(
+        jnp.concatenate(
+            [coarse_inverse, weighted_inverse, both_near[:, :coarse], -both_near[:, coarse:], coarse_coeff],
+            axis=0,
+        ),
+        lane_pad,
+    )
+    by_weighted = jnp.pad(
+        jnp.concatenate(
+            [jnp.eye(coarse, dtype=jnp.float32), both_near[:, :coarse], weighted_coeff], axis=0
+        ),
+        lane_pad,
+    )
+    by_products = jnp.pad(energy_inverse, ((0, 0), (40, LANES - 40 - count)))
+    lift_rows = lax.broadcasted_iota(jnp.int32, (LANES, 6 * LANES), 0)
+    lift_lanes = lax.broadcasted_iota(jnp.int32, (LANES, 6 * LANES), 1)
+    lift = (
+        (lift_rows // 6 == lift_lanes // LANES) & (lift_rows % 6 == (lift_lanes % LANES) % 6)
+    ).astype(jnp.bfloat16)
+    mask_rows = lax.broadcasted_iota(jnp.int32, (clusters, 6 * LANES), 0)
+    mask_lanes = lax.broadcasted_iota(jnp.int32, (clusters, 6 * LANES), 1)
+    lift_mask = (
+        mask_rows + (mask_lanes // LANES) % 3 - 1 == (mask_lanes % LANES) // 6
+    ).astype(jnp.float32)
+    padded_cols = jnp.pad(cols, ((0, 6), (0, 0)))
+    tests = jnp.pad(both_cols, ((0, 4), (0, 0)))
 
     sums_row = padded_row(
         dot_t(jnp.concatenate([products, 0.5 * residual], axis=0), weights * residual)
@@ -276,74 +441,69 @@
     rho = totals[:, count : count + 1]
     coeff = dot(energy_inverse, totals[:, :count].T) - dot(by_amounts, amounts)
     deflated_search = search - dot(coeff.T, basis)
-    direction = deflated_search
+    state = jnp.concatenate([deflated_search, solution, residual, deflated_search], axis=0)
+    shared = (lift, lift_mask, by_coarse, by_weighted, by_products, padded_cols, basis, weights)
+    scratch = [pltpu.VMEM(local_op.shape, jnp.bfloat16), pltpu.SemaphoreType.DMA((PARTS,))]
+    params = pltpu.CompilerParams(vmem_limit_bytes=24 * 2**20)
+    anywhere = pl.BlockSpec(memory_space=pl.ANY)
+    cost = pl.CostEstimate(
+        flops=2 * width * width, bytes_accessed=2 * width * width + 4 * 300 * width, transcendentals=0
+    )
+    product, sums = pl.pallas_call(
+        functools.partial(first_kernel, count),
+        out_shape=(shape_of(1, width), shape_of(1, LANES)),
+        in_specs=[VMEM, anywhere, VMEM, VMEM, VMEM, VMEM],
+        out_specs=(VMEM, VMEM),
+        scratch_shapes=scratch,
+        compiler_params=params,
+        cost_estimate=cost,
+    )(state, local_op, tests, weighted_images, weights, flat_live)
     for iteration in range(ITERS):
         last = iteration + 1 == ITERS
-        product = flat_live * jnp.dot(
-            direction.astype(jnp.bfloat16), local_op, preferred_element_type=jnp.float32
-        )
         faces = product.reshape(6, slots)
         low, high = rims(faces[None])
-        tests = [both_cols, direction]
-        if not last:
-            tests += [weights * residual, weighted_images]
-        sums = dot_t(product, jnp.concatenate(tests, axis=0))
+        sent = [product[0, : 4 * slots], sums[0]]
         if not last:
             beside = jnp.concatenate([jnp.zeros((1, 4 * slots), jnp.float32), low, high], axis=1)
-            square = jnp.sum(weights * product * (product + beside), axis=1, keepdims=True)
-            sums = jnp.concatenate([sums, square], axis=1)
-        received = everyone(
-            jnp.concatenate([product[0, : 4 * slots], padded_row(sums)]), "sub"
-        )
+            square = weights * product * (product + beside)
+            sent.append(jnp.sum(square.reshape(width // LANES, LANES), axis=0))
+        received = everyone(jnp.concatenate(sent), "sub")
         all_faces = received[:, : 4 * slots].reshape(slots_of, slots)
         all_partners = dot(route, all_faces)
         inner = lax.dynamic_slice_in_dim(all_partners, 4 * sub_index, 4, 0)
         assembled = (live * (faces + jnp.concatenate([inner, low, high], axis=0))).reshape(1, width)
-        sums = jnp.sum(received[:, 4 * slots :], axis=0, keepdims=True)
+        sums = jnp.sum(received[:, 4 * slots :], axis=0)
         if not last:
-            cross = jnp.sum(
-                jnp.sum(all_weights * all_faces * all_partners, axis=0, keepdims=True),
-                axis=1,
-                keepdims=True,
-            )
-            lane = lax.broadcasted_iota(jnp.int32, sums.shape, 1)
-            sums = sums + jnp.where(lane == 38 + count, cross, 0.0)
-        gathered = everyone(sums[0], "clu")
-        pair = dot(
-            spread,
-            gathered[:, :36].reshape(clusters, 2, 18).transpose(0, 2, 1).reshape(18 * clusters, 2),
-        )
-        totals = jnp.sum(gathered, axis=0, keepdims=True)
-        step = rho / totals[:, 36:37]
-        shifts = dot(coarse_inverse, pair)
-        shift = shifts[:, :1]
+            cross = jnp.sum(all_weights * all_faces * all_partners, axis=0)
+            cross = jnp.sum(cross.reshape(slots // LANES, LANES), axis=0)
+            sums = sums + jnp.concatenate([jnp.zeros((LANES,), jnp.float32), cross])
+        gathered = everyone(sums, "clu")
+        ahead = (gathered, assembled, state, weighted_residual, rho)
         if last:
-            image = assembled - dot(nearby(shift).T, cols)
-            solution = solution + step * direction
-            residual = residual - step * image
+            state = pl.pallas_call(
+                functools.partial(step_kernel, count, False),
+                out_shape=shape_of(4, width),
+                in_specs=[VMEM] * 13,
+                out_specs=VMEM,
+                compiler_params=params,
+            )(*ahead, *shared)
             break
-        turned = shifts[:, 1:] - dot(weighted_inverse, shift)
-        coeff_change = (
-            dot(energy_inverse, totals[:, 38 : 38 + count].T)
-            - dot(by_shift, shift)
-            - dot(by_amounts, turned)
-        )
-        near = nearby(jnp.concatenate([shift, turned], axis=1))
-        mixed = dot(
-            jnp.concatenate([near, jnp.concatenate([jnp.zeros_like(coeff_change), coeff_change], axis=1)], axis=0).T,
-            parts_mixed,
-        )
-        image = assembled - mixed[:1]
-        cross = totals[:, 37:38] - dot(shift.T, weighted_residual)
-        weighted_shift = dot(weighted_matrix, shift)
-        square = totals[:, 38 + count : 39 + count] - dot(shift.T, 2.0 * pair[:, 1:] - weighted_shift)
-        rho_next = rho - step * (2.0 * cross - step * square)
-        weighted_residual = weighted_residual - step * (pair[:, 1:] - weighted_shift)
-        solution = solution + step * direction
-        residual = residual - step * image
-        deflated_search = deflated_search - step * (weights * image - mixed[1:])
-        direction = deflated_search + rho_next / rho * direction
-        rho = rho_next
+        state, weighted_residual, rho, product, sums = pl.pallas_call(
+            functools.partial(step_kernel, count, True),
+            out_shape=(
+                shape_of(4, width),
+                shape_of(coarse, 1),
+                shape_of(1, 1),
+                shape_of(1, width),
+                shape_of(1, LANES),
+            ),
+            in_specs=[VMEM] * 13 + [anywhere, VMEM, VMEM, VMEM],
+            out_specs=(VMEM,) * 5,
+            scratch_shapes=scratch,
+            compiler_params=params,
+            cost_estimate=cost,
+        )(*ahead, *shared, local_op, tests, weighted_images, flat_live)
+    solution, residual = state[1], state[2]
     return (solution.reshape(1, 1, 6, slots), residual.reshape(1, 1, 6, slots))
 
 

time: 325 us -> 331 us (1.018)
  Pallas kernels: 16.2 us -> 32.6 us
  matrix products: 33.1 us -> 20 us
  between operations: 11.3 us -> 2.53 us
  local copies, waits for them, and re-layouts: 23.1 us -> 30.5 us
    pallas_call x0 -> x4, Pallas kernels: none -> 9.95 us  [the longest x2 7.03 us: local(): pl.pallas_call(functools.partial(step_kernel, count, True), out_shape=(sh...]
    dot_general x3 -> x0, matrix products: 9.19 us -> none  [local(): jnp.dot(direction.astype(jnp.bfloat16), local_op, preferred_element_type=...]
    all_to_all x4, waiting for transfers between devices: 39.3 us -> 48.2 us  [trade(): lax.all_to_all(rows[:, None, :], axis, split_axis=0, concat_axis=0, tiled...]
    ppermute x5, starting transfers between devices: 10.1 us -> 17.9 us  [rims(): high = lax.ppermute(values[:, 4, :], 'clu', backward)]
    ppermute x5, waiting for transfers between devices: 7.27 us -> 0.01 us  [rims(): high = lax.ppermute(values[:, 4, :], 'clu', backward)]
    unnamed x39 -> x92, local copies, waits for them, and re-layouts: 2.29 us -> 9.52 us
    pallas_call x2, Pallas kernels: 16.2 us -> 22.6 us  [spd_inverse(): pl.pallas_call(invert, out_shape=jax.ShapeDtypeStruct((size, size), jnp.f...]
    all_to_all x4, starting transfers between devices: 23.9 us -> 19.1 us  [trade(): lax.all_to_all(rows[:, None, :], axis, split_axis=0, concat_axis=0, tiled...]
  transfers between devices with their start and end apart: 23 -> 23, of which waited for: 18 -> 15; matrix products, arithmetic and copies ran while one was open for 2% -> 5% of each run, Pallas kernels for 0% -> 0%
where the time goes in v2:
time: 331 us; the launch traced here: 328 us
  waiting for transfers between devices  116 us (35%)
  starting transfers between devices  105 us (32%)
  Pallas kernels  32.6 us (10%)
  local copies, waits for them, and re-layouts  30.5 us (9%)
  matrix products  20 us (6%)
  blocking collectives  14 us (4%)
  other arithmetic  7.62 us (2%)
    all_to_all x9, waiting for transfers between devices, everyone(): lax.all_to_all(sent, axis, split_axis=0, concat_axis=0, tiled=True)[:, 0, :]  66.8 us
    all_to_all x9, starting transfers between devices, everyone(): lax.all_to_all(sent, axis, split_axis=0, concat_axis=0, tiled=True)[:, 0, :]  53.3 us
    all_to_all x4, waiting for transfers between devices, trade(): lax.all_to_all(rows[:, None, :], axis, split_axis=0, concat_axis=0, tiled...  48.2 us
    pallas_call x2, Pallas kernels, spd_inverse(): pl.pallas_call(invert, out_shape=jax.ShapeDtypeStruct((size, size), jnp.f...  22.6 us
    all_to_all x4, starting transfers between devices, trade(): lax.all_to_all(rows[:, None, :], axis, split_axis=0, concat_axis=0, tiled...  19.1 us
    ppermute x5, starting transfers between devices, rims(): high = lax.ppermute(values[:, 4, :], 'clu', backward)  17.9 us
    ppermute x5, starting transfers between devices, rims(): low = lax.ppermute(values[:, 5, :], 'clu', forward)  15.1 us
    dot_general x31, matrix products, dot(): jnp.dot(first, second, precision=precise, preferred_element_type=jnp.floa...  14 us
  transfers between devices with their start and end apart: 23, of which 15 were waited for; matrix products, arithmetic and copies ran while one was open for 5% of the time, Pallas kernels for 0%

profile of v2, /device:TPU:1, one launch (start us, length us, event | category | flops | bytes accessed | tf_op | source)
XLA Modules:
  0.0 328.5 jit_solution(11148083257140327681)
XLA Ops:
  3.3 8.8 %collective-permute-start.1 = (f32[72,256]{1,0:T(8,128)S(1)}, f32[72,256]{1,0:T(8,128)S(1)}, u32[]{:S(2)}, u32[]{:S(2)}) collective-permute-start(f32[72,256]{1,0:T(8,128)S(1)} %get-tuple-element.51), channel_id=1, source_target_pairs={{1,0},{2,1},{3,2},{4,3},{5,4},{6,5},{7,6},{8,7},{9,8},{10,9},{11,1... | collective-permute-start | bytes 221192 | tf_op jit(solution)/shard_map/ppermute | solution.py:47
  12.1 1.9 collective-permute-start
  17.9 1.4 copy.144
  19.3 6.3 %all-to-all-start = ((f32[32,1,4224]{2,1,0:T(1,128)}), f32[32,1,4224]{2,1,0:T(1,128)S(1)}, u32[]{:S(2)}, u32[]{:S(2)}) async-start(f32[32,1,4224]{2,1,0:T(1,128)} %copy.144), calls=%async_computation | async-start | bytes 1081344 | tf_op jit(solution)/shard_map/all_to_all | solution.py:39
  28.3 14.9 %all-to-all-done = f32[32,1,4224]{2,1,0:T(1,128)S(1)} async-done(((f32[32,1,4224]{2,1,0:T(1,128)}), f32[32,1,4224]{2,1,0:T(1,128)S(1)}, u32[]{:S(2)}, u32[]{:S(2)}) %all-to-all-start) | async-done | bytes 540704 | tf_op jit(solution)/shard_map/all_to_all | solution.py:39
  45.4 1.2 broadcast_in_dim.67
  46.6 4.4 %all-to-all-start.1 = ((f32[32,1,3968]{2,1,0:T(1,128)}), f32[32,1,3968]{2,1,0:T(1,128)S(1)}, u32[]{:S(2)}, u32[]{:S(2)}) async-start(f32[32,1,3968]{2,1,0:T(1,128)} %broadcast_in_dim.67), calls=%async_computation.1 | async-start | bytes 1015808 | tf_op jit(solution)/shard_map/all_to_all | solution.py:39
  52.3 15.2 %all-to-all-done.1 = f32[32,1,3968]{2,1,0:T(1,128)S(1)} async-done(((f32[32,1,3968]{2,1,0:T(1,128)}), f32[32,1,3968]{2,1,0:T(1,128)S(1)}, u32[]{:S(2)}, u32[]{:S(2)}) %all-to-all-start.1) | async-done | bytes 507936 | tf_op jit(solution)/shard_map/all_to_all | solution.py:39
  68.3 12.0 %all-to-all-start.2 = ((f32[16,1,1920]{2,1,0:T(1,128)}), f32[16,1,1920]{2,1,0:T(1,128)S(1)}, u32[]{:S(2)}, u32[]{:S(2)}) async-start(f32[16,1,1920]{2,1,0:T(1,128)} %broadcast_in_dim.70), calls=%async_computation.2 | async-start | bytes 245760 | tf_op jit(solution)/shard_map/all_to_all | solution.py:35
  80.9 8.3 %all-to-all-done.2 = f32[16,1,1920]{2,1,0:T(1,128)S(1)} async-done(((f32[16,1,1920]{2,1,0:T(1,128)}), f32[16,1,1920]{2,1,0:T(1,128)S(1)}, u32[]{:S(2)}, u32[]{:S(2)}) %all-to-all-start.2) | async-done | bytes 122912 | tf_op jit(solution)/shard_map/all_to_all | solution.py:35
  91.9 13.5 %shard_map.86 = f32[96,96]{1,0:T(8,128)} custom-call(f32[96,96]{1,0:T(8,128)} %copy.189.matrix_ref), custom_call_target="tpu_custom_call" | custom-call | flops 1769472 | bytes 73728 | tf_op jit(solution)/shard_map/pallas_call | solution.py:84
  107.7 3.3 convolution_multiply_fusion
  113.6 4.3 %all-to-all-start.3 = ((f32[32,1,2304]{2,1,0:T(1,128)}), f32[32,1,2304]{2,1,0:T(1,128)S(1)}, u32[]{:S(2)}, u32[]{:S(2)}) async-start(f32[32,1,2304]{2,1,0:T(1,128)} %copy.156), calls=%async_computation.3 | async-start | bytes 589824 | tf_op jit(solution)/shard_map/all_to_all | solution.py:39
  118.0 1.9 collective-permute-start.3
  119.9 3.6 %collective-permute-start.2 = (f32[64,256]{1,0:T(8,128)S(1)}, f32[64,256]{1,0:T(8,128)S(1)}, u32[]{:S(2)}, u32[]{:S(2)}) collective-permute-start(f32[64,256]{1,0:T(8,128)S(1)} %bitcast.364), channel_id=1, source_target_pairs={{0,1},{1,2},{2,3},{3,4},{4,5},{5,6},{6,7},{7,8},{8,9},{9,10},{10,1... | collective-permute-start | bytes 196616 | tf_op jit(solution)/shard_map/ppermute | solution.py:46
  125.1 5.6 %all-to-all-done.3 = f32[32,1,2304]{2,1,0:T(1,128)S(1)} async-done(((f32[32,1,2304]{2,1,0:T(1,128)}), f32[32,1,2304]{2,1,0:T(1,128)S(1)}, u32[]{:S(2)}, u32[]{:S(2)}) %all-to-all-start.3) | async-done | bytes 294944 | tf_op jit(solution)/shard_map/all_to_all | solution.py:39
  131.4 4.9 %all-to-all-start.4 = ((f32[16,1,256]{2,1,0:T(1,128)}), f32[16,1,256]{2,1,0:T(1,128)S(1)}, u32[]{:S(2)}, u32[]{:S(2)}) async-start(f32[16,1,256]{2,1,0:T(1,128)} %broadcast_in_dim.73), calls=%async_computation.4 | async-start | bytes 32768 | tf_op jit(solution)/shard_map/all_to_all | solution.py:35
  136.9 6.8 %all-to-all-done.4 = f32[16,1,256]{2,1,0:T(1,128)S(1)} async-done(((f32[16,1,256]{2,1,0:T(1,128)}), f32[16,1,256]{2,1,0:T(1,128)S(1)}, u32[]{:S(2)}, u32[]{:S(2)}) %all-to-all-start.4) | async-done | bytes 16416 | tf_op jit(solution)/shard_map/all_to_all | solution.py:35
  145.1 4.1 %all-to-all-start.5 = ((f32[32,1,3072]{2,1,0:T(1,128)}), f32[32,1,3072]{2,1,0:T(1,128)S(1)}, u32[]{:S(2)}, u32[]{:S(2)}) async-start(f32[32,1,3072]{2,1,0:T(1,128)} %broadcast_in_dim.148), calls=%async_computation.5 | async-start | bytes 786432 | tf_op jit(solution)/shard_map/all_to_all | solution.py:39
  150.3 12.6 %all-to-all-done.5 = f32[32,1,3072]{2,1,0:T(1,128)S(1)} async-done(((f32[32,1,3072]{2,1,0:T(1,128)}), f32[32,1,3072]{2,1,0:T(1,128)S(1)}, u32[]{:S(2)}, u32[]{:S(2)}) %all-to-all-start.5) | async-done | bytes 393248 | tf_op jit(solution)/shard_map/all_to_all | solution.py:39
  165.2 9.1 %shard_map.87 = f32[64,64]{1,0:T(8,128)} custom-call(f32[64,64]{1,0:T(8,128)} %fusion.88.matrix_ref), custom_call_target="tpu_custom_call" | custom-call | flops 524288 | bytes 32768 | tf_op jit(solution)/shard_map/pallas_call | solution.py:84
  182.4 4.9 %all-to-all-start.6 = ((f32[32,1,1152]{2,1,0:T(1,128)}), f32[32,1,1152]{2,1,0:T(1,128)S(1)}, u32[]{:S(2)}, u32[]{:S(2)}) async-start(f32[32,1,1152]{2,1,0:T(1,128)} %broadcast_in_dim.151), calls=%async_computation.6 | async-start | bytes 294912 | tf_op jit(solution)/shard_map/all_to_all | solution.py:35
  187.7 9.0 %all-to-all-done.6 = f32[32,1,1152]{2,1,0:T(1,128)S(1)} async-done(((f32[32,1,1152]{2,1,0:T(1,128)}), f32[32,1,1152]{2,1,0:T(1,128)S(1)}, u32[]{:S(2)}, u32[]{:S(2)}) %all-to-all-start.6) | async-done | bytes 147488 | tf_op jit(solution)/shard_map/all_to_all | solution.py:35
  197.4 6.3 %all-to-all-start.7 = ((f32[16,1,128]{2,1,0:T(1,128)}), f32[16,1,128]{2,1,0:T(1,128)S(1)}, u32[]{:S(2)}, u32[]{:S(2)}) async-start(f32[16,1,128]{2,1,0:T(1,128)} %broadcast_in_dim.152), calls=%async_computation.7 | async-start | bytes 16384 | tf_op jit(solution)/shard_map/all_to_all | solution.py:35
  203.9 6.8 %all-to-all-done.7 = f32[16,1,128]{2,1,0:T(1,128)S(1)} async-done(((f32[16,1,128]{2,1,0:T(1,128)}), f32[16,1,128]{2,1,0:T(1,128)S(1)}, u32[]{:S(2)}, u32[]{:S(2)}) %all-to-all-start.7) | async-done | bytes 8224 | tf_op jit(solution)/shard_map/all_to_all | solution.py:35
  211.4 2.3 copy-done
  213.7 2.0 shard_map.88
  215.8 2.6 collective-permute-start.5
  218.4 3.0 collective-permute-start.4
  222.9 3.9 %all-to-all-start.8 = ((f32[32,1,1280]{2,1,0:T(1,128)}), f32[32,1,1280]{2,1,0:T(1,128)S(1)}, u32[]{:S(2)}, u32[]{:S(2)}) async-start(f32[32,1,1280]{2,1,0:T(1,128)} %broadcast_in_dim.154), calls=%async_computation.8 | async-start | bytes 327680 | tf_op jit(solution)/shard_map/all_to_all | solution.py:35
  227.6 10.3 %all-to-all-done.8 = f32[32,1,1280]{2,1,0:T(1,128)S(1)} async-done(((f32[32,1,1280]{2,1,0:T(1,128)}), f32[32,1,1280]{2,1,0:T(1,128)S(1)}, u32[]{:S(2)}, u32[]{:S(2)}) %all-to-all-start.8) | async-done | bytes 163872 | tf_op jit(solution)/shard_map/all_to_all | solution.py:35
  239.1 6.1 %all-to-all-start.9 = ((f32[16,1,256]{2,1,0:T(1,128)}), f32[16,1,256]{2,1,0:T(1,128)S(1)}, u32[]{:S(2)}, u32[]{:S(2)}) async-start(f32[16,1,256]{2,1,0:T(1,128)} %broadcast_in_dim.155), calls=%async_computation.9 | async-start | bytes 32768 | tf_op jit(solution)/shard_map/all_to_all | solution.py:35
  245.2 7.3 %all-to-all-done.9 = f32[16,1,256]{2,1,0:T(1,128)S(1)} async-done(((f32[16,1,256]{2,1,0:T(1,128)}), f32[16,1,256]{2,1,0:T(1,128)S(1)}, u32[]{:S(2)}, u32[]{:S(2)}) %all-to-all-start.9) | async-done | bytes 16416 | tf_op jit(solution)/shard_map/all_to_all | solution.py:35
  252.5 2.3 copy-done.1
  254.8 3.5 %shard_map.89 = (f32[4,1536]{1,0:T(4,128)S(1)}, f32[96,1]{1,0:T(8,128)S(1)}, f32[1,1]{1,0:T(1,128)}, f32[1,1536]{1,0:T(1,128)S(1)}, f32[1,128]{1,0:T(1,128)S(1)}) custom-call(f32[16,256]{1,0:T(8,128)S(1)} %bitcast.298, f32[1,1536]{1,0:T(1,128)S(1)} %add_select_fusion.7.refs_1_, f32[4,1536]{1,0:T(4,128)S(1)} %pad_maximum_fusion.15.state.refs_2_, ...), custom_call_target="tpu_custom_call" | custom-call | flops 4718592 | bytes 6561792 | tf_op jit(solution)/shard_map/pallas_call | solution.py:491
  258.4 2.3 collective-permute-start.7
  260.7 3.3 collective-permute-start.6
  264.8 14.0 %all_to_all.70 = f32[32,1,1280]{2,1,0:T(1,128)S(1)} all-to-all(f32[32,1,1280]{2,1,0:T(1,128)S(1)} %broadcast_in_dim.156), channel_id=1, replica_groups=mesh['sub'=32,'clu'=16] {'sub'}, dimensions={0} | all-to-all | bytes 327680 | tf_op jit(solution)/shard_map/all_to_all | solution.py:35
  279.9 6.5 %all-to-all-start.11 = ((f32[16,1,256]{2,1,0:T(1,128)}), f32[16,1,256]{2,1,0:T(1,128)S(1)}, u32[]{:S(2)}, u32[]{:S(2)}) async-start(f32[16,1,256]{2,1,0:T(1,128)} %broadcast_in_dim.157), calls=%async_computation.11 | async-start | bytes 32768 | tf_op jit(solution)/shard_map/all_to_all | solution.py:35
  286.4 7.3 %all-to-all-done.11 = f32[16,1,256]{2,1,0:T(1,128)S(1)} async-done(((f32[16,1,256]{2,1,0:T(1,128)}), f32[16,1,256]{2,1,0:T(1,128)S(1)}, u32[]{:S(2)}, u32[]{:S(2)}) %all-to-all-start.11) | async-done | bytes 16416 | tf_op jit(solution)/shard_map/all_to_all | solution.py:35
  293.7 2.3 copy-done.2
  296.0 3.5 %shard_map.90 = (f32[4,1536]{1,0:T(4,128)S(1)}, f32[96,1]{1,0:T(8,128)S(1)}, f32[1,1]{1,0:T(1,128)}, f32[1,1536]{1,0:T(1,128)S(1)}, f32[1,128]{1,0:T(1,128)S(1)}) custom-call(f32[16,256]{1,0:T(8,128)S(1)} %bitcast.297, f32[1,1536]{1,0:T(1,128)S(1)} %add_select_fusion.6.refs_1_, f32[4,1536]{1,0:T(4,128)S(1)} %get-tuple-element.18.refs_2_, ...), custom_call_target="tpu_custom_call" | custom-call | flops 4718592 | bytes 6561792 | tf_op jit(solution)/shard_map/pallas_call | solution.py:491
  300.3 3.9 %all-to-all-start.12 = ((f32[32,1,1152]{2,1,0:T(1,128)}), f32[32,1,1152]{2,1,0:T(1,128)S(1)}, u32[]{:S(2)}, u32[]{:S(2)}) async-start(f32[32,1,1152]{2,1,0:T(1,128)} %broadcast_in_dim.158), calls=%async_computation.12 | async-start | bytes 294912 | tf_op jit(solution)/shard_map/all_to_all | solution.py:35
  304.2 2.3 collective-permute-start.9
  306.5 3.3 collective-permute-start.8
  309.8 4.4 %all-to-all-done.12 = f32[32,1,1152]{2,1,0:T(1,128)S(1)} async-done(((f32[32,1,1152]{2,1,0:T(1,128)}), f32[32,1,1152]{2,1,0:T(1,128)S(1)}, u32[]{:S(2)}, u32[]{:S(2)}) %all-to-all-start.12) | async-done | bytes 147488 | tf_op jit(solution)/shard_map/all_to_all | solution.py:35
  314.9 5.0 %all-to-all-start.13 = ((f32[16,1,128]{2,1,0:T(1,128)}), f32[16,1,128]{2,1,0:T(1,128)S(1)}, u32[]{:S(2)}, u32[]{:S(2)}) async-start(f32[16,1,128]{2,1,0:T(1,128)} %broadcast_in_dim.159), calls=%async_computation.13 | async-start | bytes 16384 | tf_op jit(solution)/shard_map/all_to_all | solution.py:35
  320.3 6.6 %all-to-all-done.13 = f32[16,1,128]{2,1,0:T(1,128)S(1)} async-done(((f32[16,1,128]{2,1,0:T(1,128)}), f32[16,1,128]{2,1,0:T(1,128)S(1)}, u32[]{:S(2)}, u32[]{:S(2)}) %all-to-all-start.13) | async-done | bytes 8224 | tf_op jit(solution)/shard_map/all_to_all | solution.py:35
  (335 shorter events, 47.3 us)
Async XLA Ops:
  0.6 26.6 %copy-start.4 = (bf16[1,1,64,6,256]{4,2,3,1,0:T(8,128)(2,1)S(1)}, bf16[1,1,64,6,256]{4,2,3,1,0:T(8,128)(2,1)}, u32[]{:S(2)}) copy-start(bf16[1,1,64,6,256]{4,2,3,1,0:T(8,128)(2,1)} %param.13) | copy-start | bytes 589828
  0.6 26.7 %copy-start.9 = (f32[1,1,6,256]{3,1,2,0:T(1,128)S(1)}, f32[1,1,6,256]{3,1,2,0:T(1,128)}, u32[]{:S(2)}) copy-start(f32[1,1,6,256]{3,1,2,0:T(1,128)} %param.11) | copy-start | bytes 18436
  0.7 42.5 %copy-start.28 = (s32[1,1,4]{2,1,0:T(1,128)S(1)}, s32[1,1,4]{2,1,0:T(1,128)}, u32[]{:S(2)}) copy-start(s32[1,1,4]{2,1,0:T(1,128)} %param.8) | copy-start | bytes 52
  0.7 25.0 %copy-start.27 = (s32[1,1,6]{2,1,0:T(1,128)S(1)}, s32[1,1,6]{2,1,0:T(1,128)}, u32[]{:S(2)}) copy-start(s32[1,1,6]{2,1,0:T(1,128)} %param.9) | copy-start | bytes 76
  1.7 41.8 %copy-start.8 = (f32[1,1,6,6,256]{4,1,3,2,0:T(1,128)S(1)}, f32[1,1,6,6,256]{4,1,3,2,0:T(1,128)}, u32[]{:S(2)}) copy-start(f32[1,1,6,6,256]{4,1,3,2,0:T(1,128)} %param.12) | copy-start | bytes 110596
  3.3 24.9 %collective-permute-start.1 = (f32[72,256]{1,0:T(8,128)S(1)}, f32[72,256]{1,0:T(8,128)S(1)}, u32[]{:S(2)}, u32[]{:S(2)}) collective-permute-start(f32[72,256]{1,0:T(8,128)S(1)} %get-tuple-element.51), channel_id=1, source_target_pairs={{1,0},{2,1},{3,2},{4,3},{5,4},{6,5},{7,6},{8,7},{9,8},{10,9},{11,1... | collective-permute-start | bytes 221192 | tf_op jit(solution)/shard_map/ppermute | solution.py:47
  12.1 16.1 %collective-permute-start = (f32[72,256]{1,0:T(8,128)S(1)}, f32[72,256]{1,0:T(8,128)S(1)}, u32[]{:S(2)}, u32[]{:S(2)}) collective-permute-start(f32[72,256]{1,0:T(8,128)S(1)} %get-tuple-element.50), channel_id=1, source_target_pairs={{0,1},{1,2},{2,3},{3,4},{4,5},{5,6},{6,7},{7,8},{8,9},{9,10},{10,1... | collective-permute-start | bytes 221192 | tf_op jit(solution)/shard_map/ppermute | solution.py:46
  17.9 26.8 %copy-start.13 = (f32[1,1,6,256]{3,1,2,0:T(1,128)S(1)}, f32[1,1,6,256]{3,1,2,0:T(1,128)}, u32[]{:S(2)}) copy-start(f32[1,1,6,256]{3,1,2,0:T(1,128)} %param.10) | copy-start | bytes 18436
  19.3 23.9 %all-to-all-start = ((f32[32,1,4224]{2,1,0:T(1,128)}), f32[32,1,4224]{2,1,0:T(1,128)S(1)}, u32[]{:S(2)}, u32[]{:S(2)}) async-start(f32[32,1,4224]{2,1,0:T(1,128)} %copy.144), calls=%async_computation | async-start | bytes 1081344 | tf_op jit(solution)/shard_map/all_to_all | solution.py:39
  25.6 21.0 %copy-start.14 = (s32[128]{0:T(128)}, s32[128]{0:T(128)S(1)}, u32[]{:S(2)}) copy-start(s32[128]{0:T(128)S(1)} %get-tuple-element.88) | copy-start | bytes 1540
  25.6 21.0 %copy-start.17 = (s32[128]{0:T(128)}, s32[128]{0:T(128)S(1)}, u32[]{:S(2)}) copy-start(s32[128]{0:T(128)S(1)} %get-tuple-element.89) | copy-start | bytes 1540
  25.6 21.0 %copy-start.20 = (pred[128]{0:T(512)(128)(4,1)}, pred[128]{0:T(512)(128)(4,1)S(1)}, u32[]{:S(2)}) copy-start(pred[128]{0:T(512)(128)(4,1)S(1)} %compare_and_fusion.1) | copy-start | bytes 388
  25.9 64.5 %copy-start.25 = (s32[288]{0:T(512)}, s32[288]{0:T(512)S(1)}, u32[]{:S(2)}) copy-start(s32[288]{0:T(512)S(1)} %fusion.139) | copy-start | bytes 3460
  46.6 20.9 %all-to-all-start.1 = ((f32[32,1,3968]{2,1,0:T(1,128)}), f32[32,1,3968]{2,1,0:T(1,128)S(1)}, u32[]{:S(2)}, u32[]{:S(2)}) async-start(f32[32,1,3968]{2,1,0:T(1,128)} %broadcast_in_dim.67), calls=%async_computation.1 | async-start | bytes 1015808 | tf_op jit(solution)/shard_map/all_to_all | solution.py:39
  68.3 21.0 %all-to-all-start.2 = ((f32[16,1,1920]{2,1,0:T(1,128)}), f32[16,1,1920]{2,1,0:T(1,128)S(1)}, u32[]{:S(2)}, u32[]{:S(2)}) async-start(f32[16,1,1920]{2,1,0:T(1,128)} %broadcast_in_dim.70), calls=%async_computation.2 | async-start | bytes 245760 | tf_op jit(solution)/shard_map/all_to_all | solution.py:35
  110.9 25.3 %copy-start.11 = (f32[128]{0:T(128)S(1)}, f32[128]{0:T(128)}, u32[]{:S(2)}) copy-start(f32[128]{0:T(128)} %copy-done.10) | copy-start | bytes 1540
  111.0 25.3 %copy-start.15 = (s32[128]{0:T(128)S(1)}, s32[128]{0:T(128)}, u32[]{:S(2)}) copy-start(s32[128]{0:T(128)} %copy-done.14) | copy-start | bytes 1540
  111.0 25.3 %copy-start.18 = (s32[128]{0:T(128)S(1)}, s32[128]{0:T(128)}, u32[]{:S(2)}) copy-start(s32[128]{0:T(128)} %copy-done.17) | copy-start | bytes 1540
  111.0 25.3 %copy-start.21 = (pred[128]{0:T(512)(128)(4,1)S(1)}, pred[128]{0:T(512)(128)(4,1)}, u32[]{:S(2)}) copy-start(pred[128]{0:T(512)(128)(4,1)} %copy-done.20) | copy-start | bytes 388
  112.1 37.1 %copy-start.29 = (s32[24]{0:T(128)S(1)}, s32[24]{0:T(128)}, u32[]{:S(2)}) copy-start(s32[24]{0:T(128)} %add_add_fusion) | copy-start | bytes 292
  112.1 37.1 %copy-start.30 = (pred[24]{0:T(512)(128)(4,1)S(1)}, pred[24]{0:T(512)(128)(4,1)}, u32[]{:S(2)}) copy-start(pred[24]{0:T(512)(128)(4,1)} %iota_compare_fusion.19) | copy-start | bytes 76
  113.6 17.1 %all-to-all-start.3 = ((f32[32,1,2304]{2,1,0:T(1,128)}), f32[32,1,2304]{2,1,0:T(1,128)S(1)}, u32[]{:S(2)}, u32[]{:S(2)}) async-start(f32[32,1,2304]{2,1,0:T(1,128)} %copy.156), calls=%async_computation.3 | async-start | bytes 589824 | tf_op jit(solution)/shard_map/all_to_all | solution.py:39
  117.8 46.3 %copy-start.26 = (s32[288]{0:T(512)S(1)}, s32[288]{0:T(512)}, u32[]{:S(2)}) copy-start(s32[288]{0:T(512)} %copy-done.25) | copy-start | bytes 3460
  118.0 32.2 %collective-permute-start.3 = (f32[64,256]{1,0:T(8,128)S(1)}, f32[64,256]{1,0:T(8,128)S(1)}, u32[]{:S(2)}, u32[]{:S(2)}) collective-permute-start(f32[64,256]{1,0:T(8,128)S(1)} %bitcast.362), channel_id=1, source_target_pairs={{1,0},{2,1},{3,2},{4,3},{5,4},{6,5},{7,6},{8,7},{9,8},{10,9},{11,1... | collective-permute-start | bytes 196616 | tf_op jit(solution)/shard_map/ppermute | solution.py:47
  119.9 30.3 %collective-permute-start.2 = (f32[64,256]{1,0:T(8,128)S(1)}, f32[64,256]{1,0:T(8,128)S(1)}, u32[]{:S(2)}, u32[]{:S(2)}) collective-permute-start(f32[64,256]{1,0:T(8,128)S(1)} %bitcast.364), channel_id=1, source_target_pairs={{0,1},{1,2},{2,3},{3,4},{4,5},{5,6},{6,7},{7,8},{8,9},{9,10},{10,1... | collective-permute-start | bytes 196616 | tf_op jit(solution)/shard_map/ppermute | solution.py:46
  131.4 12.3 %all-to-all-start.4 = ((f32[16,1,256]{2,1,0:T(1,128)}), f32[16,1,256]{2,1,0:T(1,128)S(1)}, u32[]{:S(2)}, u32[]{:S(2)}) async-start(f32[16,1,256]{2,1,0:T(1,128)} %broadcast_in_dim.73), calls=%async_computation.4 | async-start | bytes 32768 | tf_op jit(solution)/shard_map/all_to_all | solution.py:35
  145.1 17.8 %all-to-all-start.5 = ((f32[32,1,3072]{2,1,0:T(1,128)}), f32[32,1,3072]{2,1,0:T(1,128)S(1)}, u32[]{:S(2)}, u32[]{:S(2)}) async-start(f32[32,1,3072]{2,1,0:T(1,128)} %broadcast_in_dim.148), calls=%async_computation.5 | async-start | bytes 786432 | tf_op jit(solution)/shard_map/all_to_all | solution.py:39
  150.3 31.3 %copy-start.24 = (f32[1,1024]{1,0:T(1,128)S(1)}, f32[1,1024]{1,0:T(1,128)}, u32[]{:S(2)}) copy-start(f32[1,1024]{1,0:T(1,128)} %slice.337) | copy-start | bytes 12292
  174.3 36.4 %copy-start.5 = (f32[64,64]{1,0:T(8,128)S(1)}, f32[64,64]{1,0:T(8,128)}, u32[]{:S(2)}) copy-start(f32[64,64]{1,0:T(8,128)} %shard_map.87) | copy-start | bytes 49156
  179.9 47.1 %copy-start.7 = (f32[96,96]{1,0:T(8,128)S(1)}, f32[96,96]{1,0:T(8,128)}, u32[]{:S(2)}) copy-start(f32[96,96]{1,0:T(8,128)} %fusion.77) | copy-start | bytes 110596
  179.9 47.1 %copy-start.23 = (f32[24,96]{1,0:T(8,128)S(1)}, f32[24,96]{1,0:T(8,128)}, u32[]{:S(2)}) copy-start(f32[24,96]{1,0:T(8,128)} %get-tuple-element.65) | copy-start | bytes 27652
  182.4 14.3 %all-to-all-start.6 = ((f32[32,1,1152]{2,1,0:T(1,128)}), f32[32,1,1152]{2,1,0:T(1,128)S(1)}, u32[]{:S(2)}, u32[]{:S(2)}) async-start(f32[32,1,1152]{2,1,0:T(1,128)} %broadcast_in_dim.151), calls=%async_computation.6 | async-start | bytes 294912 | tf_op jit(solution)/shard_map/all_to_all | solution.py:35
  187.4 50.6 %copy-start.12 = (f32[128]{0:T(128)S(1)}, f32[128]{0:T(128)}, u32[]{:S(2)}) copy-start(f32[128]{0:T(128)} %copy-done.10) | copy-start | bytes 1540
  187.4 50.6 %copy-start.16 = (s32[128]{0:T(128)S(1)}, s32[128]{0:T(128)}, u32[]{:S(2)}) copy-start(s32[128]{0:T(128)} %copy-done.14) | copy-start | bytes 1540
  187.4 50.6 %copy-start.19 = (s32[128]{0:T(128)S(1)}, s32[128]{0:T(128)}, u32[]{:S(2)}) copy-start(s32[128]{0:T(128)} %copy-done.17) | copy-start | bytes 1540
  187.4 50.6 %copy-start.22 = (pred[128]{0:T(512)(128)(4,1)S(1)}, pred[128]{0:T(512)(128)(4,1)}, u32[]{:S(2)}) copy-start(pred[128]{0:T(512)(128)(4,1)} %copy-done.20) | copy-start | bytes 388
  197.4 13.3 %all-to-all-start.7 = ((f32[16,1,128]{2,1,0:T(1,128)}), f32[16,1,128]{2,1,0:T(1,128)S(1)}, u32[]{:S(2)}, u32[]{:S(2)}) async-start(f32[16,1,128]{2,1,0:T(1,128)} %broadcast_in_dim.152), calls=%async_computation.7 | async-start | bytes 16384 | tf_op jit(solution)/shard_map/all_to_all | solution.py:35
  215.8 6.0 %collective-permute-start.5 = (f32[1,256]{1,0:T(1,128)S(1)}, f32[1,256]{1,0:T(1,128)S(1)}, u32[]{:S(2)}, u32[]{:S(2)}) collective-permute-start(f32[1,256]{1,0:T(1,128)S(1)} %get-tuple-element.72), channel_id=1, source_target_pairs={{1,0},{2,1},{3,2},{4,3},{5,4},{6,5},{7,6},{8,7},{9,8},{10,9},{11,1... | collective-permute-start | bytes 3080 | tf_op jit(solution)/shard_map/ppermute | solution.py:47
  218.4 3.7 %collective-permute-start.4 = (f32[1,256]{1,0:T(1,128)S(1)}, f32[1,256]{1,0:T(1,128)S(1)}, u32[]{:S(2)}, u32[]{:S(2)}) collective-permute-start(f32[1,256]{1,0:T(1,128)S(1)} %get-tuple-element.71), channel_id=1, source_target_pairs={{0,1},{1,2},{2,3},{3,4},{4,5},{5,6},{6,7},{7,8},{8,9},{9,10},{10,1... | collective-permute-start | bytes 3080 | tf_op jit(solution)/shard_map/ppermute | solution.py:46
  222.9 15.0 %all-to-all-start.8 = ((f32[32,1,1280]{2,1,0:T(1,128)}), f32[32,1,1280]{2,1,0:T(1,128)S(1)}, u32[]{:S(2)}, u32[]{:S(2)}) async-start(f32[32,1,1280]{2,1,0:T(1,128)} %broadcast_in_dim.154), calls=%async_computation.8 | async-start | bytes 327680 | tf_op jit(solution)/shard_map/all_to_all | solution.py:35
  239.1 13.4 %all-to-all-start.9 = ((f32[16,1,256]{2,1,0:T(1,128)}), f32[16,1,256]{2,1,0:T(1,128)S(1)}, u32[]{:S(2)}, u32[]{:S(2)}) async-start(f32[16,1,256]{2,1,0:T(1,128)} %broadcast_in_dim.155), calls=%async_computation.9 | async-start | bytes 32768 | tf_op jit(solution)/shard_map/all_to_all | solution.py:35
  258.4 5.6 %collective-permute-start.7 = (f32[1,256]{1,0:T(1,128)S(1)}, f32[1,256]{1,0:T(1,128)S(1)}, u32[]{:S(2)}, u32[]{:S(2)}) collective-permute-start(f32[1,256]{1,0:T(1,128)S(1)} %get-tuple-element.70), channel_id=1, source_target_pairs={{1,0},{2,1},{3,2},{4,3},{5,4},{6,5},{7,6},{8,7},{9,8},{10,9},{11,1... | collective-permute-start | bytes 3080 | tf_op jit(solution)/shard_map/ppermute | solution.py:47
  260.7 4.0 %collective-permute-start.6 = (f32[1,256]{1,0:T(1,128)S(1)}, f32[1,256]{1,0:T(1,128)S(1)}, u32[]{:S(2)}, u32[]{:S(2)}) collective-permute-start(f32[1,256]{1,0:T(1,128)S(1)} %get-tuple-element.69), channel_id=1, source_target_pairs={{0,1},{1,2},{2,3},{3,4},{4,5},{5,6},{6,7},{7,8},{8,9},{9,10},{10,1... | collective-permute-start | bytes 3080 | tf_op jit(solution)/shard_map/ppermute | solution.py:46
  279.9 13.8 %all-to-all-start.11 = ((f32[16,1,256]{2,1,0:T(1,128)}), f32[16,1,256]{2,1,0:T(1,128)S(1)}, u32[]{:S(2)}, u32[]{:S(2)}) async-start(f32[16,1,256]{2,1,0:T(1,128)} %broadcast_in_dim.157), calls=%async_computation.11 | async-start | bytes 32768 | tf_op jit(solution)/shard_map/all_to_all | solution.py:35
  300.3 13.9 %all-to-all-start.12 = ((f32[32,1,1152]{2,1,0:T(1,128)}), f32[32,1,1152]{2,1,0:T(1,128)S(1)}, u32[]{:S(2)}, u32[]{:S(2)}) async-start(f32[32,1,1152]{2,1,0:T(1,128)} %broadcast_in_dim.158), calls=%async_computation.12 | async-start | bytes 294912 | tf_op jit(solution)/shard_map/all_to_all | solution.py:35
  304.2 16.0 %collective-permute-start.9 = (f32[1,256]{1,0:T(1,128)S(1)}, f32[1,256]{1,0:T(1,128)S(1)}, u32[]{:S(2)}, u32[]{:S(2)}) collective-permute-start(f32[1,256]{1,0:T(1,128)S(1)} %get-tuple-element.68), channel_id=1, source_target_pairs={{1,0},{2,1},{3,2},{4,3},{5,4},{6,5},{7,6},{8,7},{9,8},{10,9},{11,1... | collective-permute-start | bytes 3080 | tf_op jit(solution)/shard_map/ppermute | solution.py:47
  306.5 13.7 %collective-permute-start.8 = (f32[1,256]{1,0:T(1,128)S(1)}, f32[1,256]{1,0:T(1,128)S(1)}, u32[]{:S(2)}, u32[]{:S(2)}) collective-permute-start(f32[1,256]{1,0:T(1,128)S(1)} %get-tuple-element.67), channel_id=1, source_target_pairs={{0,1},{1,2},{2,3},{3,4},{4,5},{5,6},{6,7},{7,8},{8,9},{9,10},{10,1... | collective-permute-start | bytes 3080 | tf_op jit(solution)/shard_map/ppermute | solution.py:46
  314.9 12.1 %all-to-all-start.13 = ((f32[16,1,128]{2,1,0:T(1,128)}), f32[16,1,128]{2,1,0:T(1,128)S(1)}, u32[]{:S(2)}, u32[]{:S(2)}) async-start(f32[16,1,128]{2,1,0:T(1,128)} %broadcast_in_dim.159), calls=%async_computation.13 | async-start | bytes 16384 | tf_op jit(solution)/shard_map/all_to_all | solution.py:35
  (6 other events, 35.5 us)

commit v3 on v2

--- a/solution.py
+++ b/solution.py
@@ -54,29 +54,39 @@
 
 def invert(matrix_ref, inverse_ref):
     size = matrix_ref.shape[0]
-    rows = lax.broadcasted_iota(jnp.int32, (size, size), 0)
-    lanes = lax.broadcasted_iota(jnp.int32, (size, size), 1)
-    row_lanes = lax.broadcasted_iota(jnp.int32, (1, size), 1)
-    column_rows = lax.broadcasted_iota(jnp.int32, (size, 1), 0)
-    values = matrix_ref[...]
+    lane = lax.broadcasted_iota(jnp.int32, (8, size), 1)
+    row = lax.broadcasted_iota(jnp.int32, (8, 1), 0)
+    tiles = [matrix_ref[8 * t : 8 * t + 8, :] for t in range(size // 8)]
     for k in range(0, size, 2):
-        first, second = values[k : k + 1, :], values[k + 1 : k + 2, :]
-        across = second[:, k : k + 1]
-        first_part = 1.0 / first[:, k : k + 1]
+        home, at = divmod(k, 8)
+
+        def spread_out(values, place):
+            return jnp.broadcast_to(values[:, place : place + 1], (8, size))
+
+        first = jnp.broadcast_to(tiles[home][at : at + 1, :], (8, size))
+        second = jnp.broadcast_to(tiles[home][at + 1 : at + 2, :], (8, size))
+        across = spread_out(second, k)
+        first_part = 1.0 / spread_out(first, k)
         ratio = across * first_part
-        second_part = 1.0 / (second[:, k + 1 : k + 2] - ratio * across)
+        second_part = 1.0 / (spread_out(second, k + 1) - ratio * across)
         mixed_part = ratio * second_part
-        here, after = row_lanes == k, row_lanes == k + 1
-        first = jnp.where(here, 1.0, jnp.where(after, 0.0, first))
-        second = jnp.where(after, 1.0, jnp.where(here, 0.0, second))
+        here, after = lane == k, lane == k + 1
+        either = here | after
+        first = jnp.where(either, jnp.where(here, 1.0, 0.0), first)
+        second = jnp.where(either, jnp.where(after, 1.0, 0.0), second)
         first_scaled = (first_part + ratio * mixed_part) * first - mixed_part * second
         second_scaled = second_part * second - mixed_part * first
-        here, after = column_rows == k, column_rows == k + 1
-        first_column = jnp.where(here, -1.0, jnp.where(after, 0.0, values[:, k : k + 1]))
-        second_column = jnp.where(after, -1.0, jnp.where(here, 0.0, values[:, k + 1 : k + 2]))
-        kept = jnp.where((rows // 2 == k // 2) | (lanes // 2 == k // 2), 0.0, values)
-        values = kept - first_column * first_scaled - second_column * second_scaled
-    inverse_ref[...] = values
+        for t, tile in enumerate(tiles):
+            first_column, second_column = tile[:, k : k + 1], tile[:, k + 1 : k + 2]
+            kept = jnp.where(either, 0.0, tile)
+            if t == home:
+                pivots = (row == at) | (row == at + 1)
+                first_column = jnp.where(pivots, jnp.where(row == at, -1.0, 0.0), first_column)
+                second_column = jnp.where(pivots, jnp.where(row == at + 1, -1.0, 0.0), second_column)
+                kept = jnp.where(pivots, 0.0, kept)
+            tiles[t] = kept - first_column * first_scaled - second_column * second_scaled
+    for t, tile in enumerate(tiles):
+        inverse_ref[8 * t : 8 * t + 8, :] = tile
 
 
 def spd_inverse(matrix):
@@ -122,7 +132,8 @@
         lifted[:, 3 * LANES : 4 * LANES] + lifted[:, 4 * LANES : 5 * LANES] + lifted[:, 5 * LANES :]
     )
     totals = row_sum(values)
-    step = rho[...] / totals[:, 36:37]
+    rho_now = rho[:, count : count + 1]
+    step = rho_now / totals[:, 36:37]
     from_coarse = lane_sum(by_coarse[...] * coarse_row)
     from_weighted = lane_sum(by_weighted[...] * weighted_row)
     shift = from_coarse[:coarse]
@@ -130,10 +141,14 @@
     near_shift = from_coarse[2 * coarse : 2 * coarse + near]
     image = image_sum[...] - row_sum(cols[...] * near_shift)
     direction = state[0:1, :]
-    state_out[1:2, :] = state[1:2, :] + step * direction
-    state_out[2:3, :] = state[2:3, :] - step * image
+    solution = state[1:2, :] + step * direction
+    residual = state[2:3, :] - step * image
     if not again:
+        state_out[0][...] = solution
+        state_out[1][...] = residual
         return
+    state_out[1:2, :] = solution
+    state_out[2:3, :] = residual
     near_turned = from_coarse[2 * coarse + near : 2 * coarse + 2 * near] + from_weighted[coarse : coarse + near]
     coeff_change = (
         from_coarse[2 * coarse + 2 * near :]
@@ -143,13 +158,13 @@
     found_weighted = from_weighted[:coarse]
     cross = totals[:, 37:38] - row_sum(shift * weighted[...])
     square = lane_sum(row_sum(gathered[:, LANES:])) - row_sum(shift * (2.0 * found_weighted - weighted_shift))
-    rho_next = rho[...] - step * (2.0 * cross - step * square)
+    rho_next = rho_now - step * (2.0 * cross - step * square)
     weighted_out[...] = weighted[...] - step * (found_weighted - weighted_shift)
-    rho_out[...] = rho_next
+    rho_out[...] = jnp.broadcast_to(rho_next, rho_out.shape)
     change = weights[...] * image - row_sum(cols[...] * near_turned) - row_sum(basis[...] * coeff_change)
     deflated = state[3:4, :] - step * change
     state_out[3:4, :] = deflated
-    state_out[0:1, :] = deflated + (rho_next / rho[...]) * direction
+    state_out[0:1, :] = deflated + (rho_next / rho_now) * direction
 
 
 def apply(count, operator, held, arrived, state, tests, images, weights, live, product, sums):
@@ -190,7 +205,8 @@
 def step_kernel(count, again, *refs):
     if not again:
         gathered, image_sum, state, weighted, rho, *rest = refs
-        advance(count, gathered, image_sum, state, rest[-1], weighted, rho, None, None, rest[:-1], False)
+        outs = rest[-2:]
+        advance(count, gathered, image_sum, state, outs, weighted, rho, None, None, rest[:-2], False)
         return
     gathered, image_sum, state, weighted, rho = refs[:5]
     shared = refs[5:13]
@@ -255,10 +271,12 @@
 
     few = jnp.concatenate([load[None], precond_terms[0, 0][None], rigid], axis=0)
     few_count = few.shape[0]
-    low, high = rims(jnp.concatenate([few, recycled], axis=0))
     direct = dot(onehot.T, few[:, :4].transpose(1, 0, 2).reshape(4, few_count * slots))
     ids = jnp.broadcast_to(padded_row(neighbor_ids.astype(jnp.float32))[None], (members, LANES))
-    received = trade(jnp.concatenate([to_carriers(recycled), direct, ids], axis=1), "sub")
+    first_blocks = jnp.concatenate([to_carriers(recycled), direct, ids], axis=1)
+    few_later, first_blocks = lax.optimization_barrier((few, first_blocks))
+    received = trade(first_blocks, "sub")
+    few_low, few_high = rims(few_later)
     table = received[:, piece + few_count * slots :][:, :4]
     slots_of = 4 * members
     row_member = (lax.broadcasted_iota(jnp.int32, (slots_of, slots_of), 0) // 4).astype(jnp.float32)
@@ -272,7 +290,7 @@
 
     few_inner = dot(onehot, received[:, piece : piece + few_count * slots])
     few_inner = few_inner.reshape(4, few_count, slots).transpose(1, 0, 2)
-    few_copy = six_faces(few_inner, low[:few_count], high[:few_count])
+    few_copy = six_faces(few_inner, few_low, few_high)
     demand = (live * (load + few_copy[0])).reshape(1, width)
     weights = (0.5 * live * (few[1] + few_copy[1])).reshape(1, width)
     face_index = jnp.arange(6, dtype=jnp.int32)
@@ -298,15 +316,15 @@
     )
     sums_size = sums.size
     sums_row = padded_row(sums)
-    received = trade(
-        jnp.concatenate(
-            [carry(received[:, :piece]), jnp.broadcast_to(sums_row[None], (members, sums_row.shape[0]))],
-            axis=1,
-        ),
-        "sub",
-    )
+    second_blocks = jnp.concatenate(
+        [carry(received[:, :piece]), jnp.broadcast_to(sums_row[None], (members, sums_row.shape[0]))],
+        axis=1,
+    )
+    recycled_later, second_blocks = lax.optimization_barrier((recycled, second_blocks))
+    received = trade(second_blocks, "sub")
+    low, high = rims(recycled_later)
     basis_raw = (
-        live * (recycled + six_faces(from_carriers(received[:, :piece]), low[few_count:], high[few_count:]))
+        live * (recycled + six_faces(from_carriers(received[:, :piece]), low, high))
     ).reshape(count, width)
     gathered = everyone(jnp.sum(received[:, piece:], axis=0), "clu")
     gathered = gathered[:, :sums_size].reshape(clusters, 18, 37 + count)
@@ -330,7 +348,6 @@
     products = flat_live * jnp.dot(
         basis.astype(jnp.bfloat16), local_op, preferred_element_type=jnp.float32
     )
-    low, high = rims(products.reshape(count, 6, slots))
     both_cols = jnp.concatenate([cols, weighted_cols], axis=0)
     grouped = both_cols.reshape(2, 3, 6, width).transpose(0, 2, 1, 3).reshape(12, 3, width)
     grouped = jnp.pad(grouped, ((0, 0), (0, 1), (0, 0))).reshape(48, width)
@@ -347,9 +364,10 @@
         ],
         axis=0,
     )
-    received = trade(
-        jnp.concatenate([to_carriers(products), shares], axis=1), "sub"
-    )
+    blocks = jnp.concatenate([to_carriers(products), shares], axis=1)
+    products_later, blocks = lax.optimization_barrier((products, blocks))
+    received = trade(blocks, "sub")
+    low, high = rims(products_later.reshape(count, 6, slots))
     share = everyone(jnp.sum(received[:, piece:], axis=0), "clu").reshape(clusters, 4, count)
     whole = jnp.pad(jnp.sum(share, axis=0), ((0, clusters - 4), (0, 0)))
     beside = jnp.pad(share[:, :3], ((1, 1), (0, 0), (0, 0)))
@@ -390,6 +408,21 @@
     amounts = dot(coarse_inverse, weighted_residual)
     search = weights * residual - dot(nearby(amounts).T, cols)
     weighted_images = weights * images
+    sums_row = padded_row(
+        dot_t(jnp.concatenate([products, 0.5 * residual], axis=0), weights * residual)
+    )
+    received = everyone(
+        jnp.concatenate([sums_row, weights[0, : 4 * slots]]), "sub"
+    )
+    all_weights = received[:, LANES:].reshape(slots_of, slots)
+    to_clusters = jnp.sum(received[:, :LANES], axis=0)
+    totals = jnp.sum(everyone(to_clusters, "clu"), axis=0, keepdims=True)
+    rho = totals
+    (to_clusters, weighted_matrix, coarse_inverse, energy_inverse, image_weighted, image_coarse) = (
+        lax.optimization_barrier(
+            (to_clusters, weighted_matrix, coarse_inverse, energy_inverse, image_weighted, image_coarse)
+        )
+    )
     near_rows = lax.broadcasted_iota(jnp.int32, (24, coarse), 0)
     near_lanes = lax.broadcasted_iota(jnp.int32, (24, coarse), 1)
     near_select = ((near_lanes == 6 * clu_index + near_rows - 6) & (near_rows < 18)).astype(jnp.float32)
@@ -428,23 +461,11 @@
     padded_cols = jnp.pad(cols, ((0, 6), (0, 0)))
     tests = jnp.pad(both_cols, ((0, 4), (0, 0)))
 
-    sums_row = padded_row(
-        dot_t(jnp.concatenate([products, 0.5 * residual], axis=0), weights * residual)
-    )
-    received = everyone(
-        jnp.concatenate([sums_row, weights[0, : 4 * slots]]), "sub"
-    )
-    all_weights = received[:, LANES:].reshape(slots_of, slots)
-    totals = jnp.sum(
-        everyone(jnp.sum(received[:, :LANES], axis=0), "clu"), axis=0, keepdims=True
-    )
-    rho = totals[:, count : count + 1]
     coeff = dot(energy_inverse, totals[:, :count].T) - dot(by_amounts, amounts)
     deflated_search = search - dot(coeff.T, basis)
     state = jnp.concatenate([deflated_search, solution, residual, deflated_search], axis=0)
     shared = (lift, lift_mask, by_coarse, by_weighted, by_products, padded_cols, basis, weights)
     scratch = [pltpu.VMEM(local_op.shape, jnp.bfloat16), pltpu.SemaphoreType.DMA((PARTS,))]
-    params = pltpu.CompilerParams(vmem_limit_bytes=24 * 2**20)
     anywhere = pl.BlockSpec(memory_space=pl.ANY)
     cost = pl.CostEstimate(
         flops=2 * width * width, bytes_accessed=2 * width * width + 4 * 300 * width, transcendentals=0
@@ -455,7 +476,6 @@
         in_specs=[VMEM, anywhere, VMEM, VMEM, VMEM, VMEM],
         out_specs=(VMEM, VMEM),
         scratch_shapes=scratch,
-        compiler_params=params,
         cost_estimate=cost,
     )(state, local_op, tests, weighted_images, weights, flat_live)
     for iteration in range(ITERS):
@@ -480,12 +500,11 @@
         gathered = everyone(sums, "clu")
         ahead = (gathered, assembled, state, weighted_residual, rho)
         if last:
-            state = pl.pallas_call(
+            solution, residual = pl.pallas_call(
                 functools.partial(step_kernel, count, False),
-                out_shape=shape_of(4, width),
+                out_shape=(shape_of(1, width), shape_of(1, width)),
                 in_specs=[VMEM] * 13,
-                out_specs=VMEM,
-                compiler_params=params,
+                out_specs=(VMEM, VMEM),
             )(*ahead, *shared)
             break
         state, weighted_residual, rho, product, sums = pl.pallas_call(
@@ -493,17 +512,15 @@
             out_shape=(
                 shape_of(4, width),
                 shape_of(coarse, 1),
-                shape_of(1, 1),
+                shape_of(1, LANES),
                 shape_of(1, width),
                 shape_of(1, LANES),
             ),
             in_specs=[VMEM] * 13 + [anywhere, VMEM, VMEM, VMEM],
             out_specs=(VMEM,) * 5,
             scratch_shapes=scratch,
-            compiler_params=params,
             cost_estimate=cost,
         )(*ahead, *shared, local_op, tests, weighted_images, flat_live)
-    solution, residual = state[1], state[2]
     return (solution.reshape(1, 1, 6, slots), residual.reshape(1, 1, 6, slots))
 
 

time: 331 us -> 327 us (0.988)
  waiting for transfers between devices: 116 us -> 104 us
  other arithmetic: 7.62 us -> 17.1 us
  starting transfers between devices: 105 us -> 111 us
  local copies, waits for them, and re-layouts: 30.5 us -> 26.7 us
    pallas_call x2, Pallas kernels: 22.6 us -> 16.2 us  [spd_inverse(): pl.pallas_call(invert, out_shape=jax.ShapeDtypeStruct((size, size), jnp.f...]
    all_to_all x9, waiting for transfers between devices: 66.8 us -> 60.7 us  [everyone(): lax.all_to_all(sent, axis, split_axis=0, concat_axis=0, tiled=True)[:, 0, :]]
    all_to_all x4, waiting for transfers between devices: 48.2 us -> 42.7 us  [trade(): lax.all_to_all(rows[:, None, :], axis, split_axis=0, concat_axis=0, tiled...]
    unnamed x92 -> x60, local copies, waits for them, and re-layouts: 9.52 us -> 4.19 us
    mul x3, other arithmetic: 0.05 us -> 3.91 us  [local(): live * (faces + jnp.concatenate([inner, low, high], axis=0))]
    ppermute x5 -> x6, starting transfers between devices: 15.1 us -> 18.8 us  [rims(): low = lax.ppermute(values[:, 5, :], 'clu', forward)]
    ppermute x5 -> x6, starting transfers between devices: 17.9 us -> 20.6 us  [rims(): high = lax.ppermute(values[:, 4, :], 'clu', backward)]
  transfers between devices with their start and end apart: 23 -> 25, of which waited for: 15 -> 14; matrix products, arithmetic and copies ran while one was open for 5% -> 6% of each run, Pallas kernels for 0% -> 0%
where the time goes in v3:
time: 327 us; the launch traced here: 325 us
  starting transfers between devices  111 us (34%)
  waiting for transfers between devices  104 us (32%)
  Pallas kernels  32.8 us (10%)
  local copies, waits for them, and re-layouts  26.7 us (8%)
  other arithmetic  17.1 us (5%)
  matrix products  17 us (5%)
  blocking collectives  14 us (4%)
    all_to_all x9, waiting for transfers between devices, everyone(): lax.all_to_all(sent, axis, split_axis=0, concat_axis=0, tiled=True)[:, 0, :]  60.7 us
    all_to_all x9, starting transfers between devices, everyone(): lax.all_to_all(sent, axis, split_axis=0, concat_axis=0, tiled=True)[:, 0, :]  52.4 us
    all_to_all x4, waiting for transfers between devices, trade(): lax.all_to_all(rows[:, None, :], axis, split_axis=0, concat_axis=0, tiled...  42.7 us
    ppermute x6, starting transfers between devices, rims(): high = lax.ppermute(values[:, 4, :], 'clu', backward)  20.6 us
    all_to_all x4, starting transfers between devices, trade(): lax.all_to_all(rows[:, None, :], axis, split_axis=0, concat_axis=0, tiled...  18.9 us
    ppermute x6, starting transfers between devices, rims(): low = lax.ppermute(values[:, 5, :], 'clu', forward)  18.8 us
    pallas_call x2, Pallas kernels, spd_inverse(): pl.pallas_call(invert, out_shape=jax.ShapeDtypeStruct((size, size), jnp.f...  16.2 us
    all_to_all x1, blocking collectives, everyone(): lax.all_to_all(sent, axis, split_axis=0, concat_axis=0, tiled=True)[:, 0, :]  14 us
  transfers between devices with their start and end apart: 25, of which 14 were waited for; matrix products, arithmetic and copies ran while one was open for 6% of the time, Pallas kernels for 0%

profile of v3, /device:TPU:1, one launch (start us, length us, event | category | flops | bytes accessed | tf_op | source)
XLA Modules:
  0.0 324.6 jit_solution(7717233181272913724)
XLA Ops:
  5.4 8.8 %collective-permute-start.1 = (f32[8,256]{1,0:T(8,128)S(1)}, f32[8,256]{1,0:T(8,128)S(1)}, u32[]{:S(2)}, u32[]{:S(2)}) collective-permute-start(f32[8,256]{1,0:T(8,128)S(1)} %get-tuple-element.89), channel_id=1, source_target_pairs={{1,0},{2,1},{3,2},{4,3},{5,4},{6,5},{7,6},{8,7},{9,8},{10,9},{11,1... | collective-permute-start | bytes 24584 | tf_op jit(solution)/shard_map/ppermute | solution.py:47
  14.2 1.9 collective-permute-start
  16.1 1.4 copy.149
  17.5 6.3 %all-to-all-start = ((f32[32,1,4224]{2,1,0:T(1,128)}), f32[32,1,4224]{2,1,0:T(1,128)S(1)}, u32[]{:S(2)}, u32[]{:S(2)}) async-start(f32[32,1,4224]{2,1,0:T(1,128)} %copy.149), calls=%async_computation | async-start | bytes 1081344 | tf_op jit(solution)/shard_map/all_to_all | solution.py:39
  24.4 17.0 %all-to-all-done = f32[32,1,4224]{2,1,0:T(1,128)S(1)} async-done(((f32[32,1,4224]{2,1,0:T(1,128)}), f32[32,1,4224]{2,1,0:T(1,128)S(1)}, u32[]{:S(2)}, u32[]{:S(2)}) %all-to-all-start) | async-done | bytes 540704 | tf_op jit(solution)/shard_map/all_to_all | solution.py:39
  44.7 4.4 %all-to-all-start.1 = ((f32[32,1,3968]{2,1,0:T(1,128)}), f32[32,1,3968]{2,1,0:T(1,128)S(1)}, u32[]{:S(2)}, u32[]{:S(2)}) async-start(f32[32,1,3968]{2,1,0:T(1,128)} %broadcast_in_dim.67), calls=%async_computation.1 | async-start | bytes 1015808 | tf_op jit(solution)/shard_map/all_to_all | solution.py:39
  49.2 2.3 collective-permute-start.3
  51.5 3.9 %collective-permute-start.2 = (f32[64,256]{1,0:T(8,128)S(1)}, f32[64,256]{1,0:T(8,128)S(1)}, u32[]{:S(2)}, u32[]{:S(2)}) collective-permute-start(f32[64,256]{1,0:T(8,128)S(1)} %get-tuple-element.76), channel_id=1, source_target_pairs={{0,1},{1,2},{2,3},{3,4},{4,5},{5,6},{6,7},{7,8},{8,9},{9,10},{10,1... | collective-permute-start | bytes 196616 | tf_op jit(solution)/shard_map/ppermute | solution.py:46
  56.8 8.8 %all-to-all-done.1 = f32[32,1,3968]{2,1,0:T(1,128)S(1)} async-done(((f32[32,1,3968]{2,1,0:T(1,128)}), f32[32,1,3968]{2,1,0:T(1,128)S(1)}, u32[]{:S(2)}, u32[]{:S(2)}) %all-to-all-start.1) | async-done | bytes 507936 | tf_op jit(solution)/shard_map/all_to_all | solution.py:39
  66.4 11.9 %all-to-all-start.2 = ((f32[16,1,1920]{2,1,0:T(1,128)}), f32[16,1,1920]{2,1,0:T(1,128)S(1)}, u32[]{:S(2)}, u32[]{:S(2)}) async-start(f32[16,1,1920]{2,1,0:T(1,128)} %broadcast_in_dim.70), calls=%async_computation.2 | async-start | bytes 245760 | tf_op jit(solution)/shard_map/all_to_all | solution.py:35
  79.0 8.3 %all-to-all-done.2 = f32[16,1,1920]{2,1,0:T(1,128)S(1)} async-done(((f32[16,1,1920]{2,1,0:T(1,128)}), f32[16,1,1920]{2,1,0:T(1,128)S(1)}, u32[]{:S(2)}, u32[]{:S(2)}) %all-to-all-start.2) | async-done | bytes 122912 | tf_op jit(solution)/shard_map/all_to_all | solution.py:35
  89.9 9.7 %shard_map.86 = f32[96,96]{1,0:T(8,128)} custom-call(f32[96,96]{1,0:T(8,128)} %copy.196.matrix_ref), custom_call_target="tpu_custom_call" | custom-call | flops 1769472 | bytes 73728 | tf_op jit(solution)/shard_map/pallas_call | solution.py:94
  101.3 3.4 %convolution_multiply_fusion = f32[64,1536]{1,0:T(8,128)S(1)} fusion(f32[1536]{0:T(1024)S(1)} %get-tuple-element.68, bf16[1,1,1536,1536]{3,2,1,0:T(8,128)(2,1)} %param.7, f32[65,1536]{1,0:T(8,128)S(1)} %convolution_subtract_fusion), kind=kOutput, calls=%fused_computation.1 | convolution fusion | flops 302088192 | bytes 5316608 | tf_op jit(solution)/shard_map/dot_general | solution.py:348
  107.8 4.3 %all-to-all-start.3 = ((f32[32,1,2304]{2,1,0:T(1,128)}), f32[32,1,2304]{2,1,0:T(1,128)S(1)}, u32[]{:S(2)}, u32[]{:S(2)}) async-start(f32[32,1,2304]{2,1,0:T(1,128)} %copy.162), calls=%async_computation.3 | async-start | bytes 589824 | tf_op jit(solution)/shard_map/all_to_all | solution.py:39
  112.7 12.1 %all-to-all-done.3 = f32[32,1,2304]{2,1,0:T(1,128)S(1)} async-done(((f32[32,1,2304]{2,1,0:T(1,128)}), f32[32,1,2304]{2,1,0:T(1,128)S(1)}, u32[]{:S(2)}, u32[]{:S(2)}) %all-to-all-start.3) | async-done | bytes 294944 | tf_op jit(solution)/shard_map/all_to_all | solution.py:39
  125.6 4.9 %all-to-all-start.4 = ((f32[16,1,256]{2,1,0:T(1,128)}), f32[16,1,256]{2,1,0:T(1,128)S(1)}, u32[]{:S(2)}, u32[]{:S(2)}) async-start(f32[16,1,256]{2,1,0:T(1,128)} %broadcast_in_dim.73), calls=%async_computation.4 | async-start | bytes 32768 | tf_op jit(solution)/shard_map/all_to_all | solution.py:35
  131.1 6.8 %all-to-all-done.4 = f32[16,1,256]{2,1,0:T(1,128)S(1)} async-done(((f32[16,1,256]{2,1,0:T(1,128)}), f32[16,1,256]{2,1,0:T(1,128)S(1)}, u32[]{:S(2)}, u32[]{:S(2)}) %all-to-all-start.4) | async-done | bytes 16416 | tf_op jit(solution)/shard_map/all_to_all | solution.py:35
  139.3 3.9 %all-to-all-start.5 = ((f32[32,1,3072]{2,1,0:T(1,128)}), f32[32,1,3072]{2,1,0:T(1,128)S(1)}, u32[]{:S(2)}, u32[]{:S(2)}) async-start(f32[32,1,3072]{2,1,0:T(1,128)} %broadcast_in_dim.148), calls=%async_computation.5 | async-start | bytes 786432 | tf_op jit(solution)/shard_map/all_to_all | solution.py:39
  145.0 2.4 collective-permute-start.5
  147.4 3.4 %collective-permute-start.4 = (f32[64,256]{1,0:T(8,128)S(1)}, f32[64,256]{1,0:T(8,128)S(1)}, u32[]{:S(2)}, u32[]{:S(2)}) collective-permute-start(f32[64,256]{1,0:T(8,128)S(1)} %bitcast.359), channel_id=1, source_target_pairs={{0,1},{1,2},{2,3},{3,4},{4,5},{5,6},{6,7},{7,8},{8,9},{9,10},{10,1... | collective-permute-start | bytes 196616 | tf_op jit(solution)/shard_map/ppermute | solution.py:46
  152.4 4.8 %all-to-all-done.5 = f32[32,1,3072]{2,1,0:T(1,128)S(1)} async-done(((f32[32,1,3072]{2,1,0:T(1,128)}), f32[32,1,3072]{2,1,0:T(1,128)S(1)}, u32[]{:S(2)}, u32[]{:S(2)}) %all-to-all-start.5) | async-done | bytes 393248 | tf_op jit(solution)/shard_map/all_to_all | solution.py:39
  158.8 6.5 %shard_map.87 = f32[64,64]{1,0:T(8,128)} custom-call(f32[64,64]{1,0:T(8,128)} %fusion.83.matrix_ref), custom_call_target="tpu_custom_call" | custom-call | flops 524288 | bytes 32768 | tf_op jit(solution)/shard_map/pallas_call | solution.py:94
  170.6 4.8 %all-to-all-start.6 = ((f32[32,1,1152]{2,1,0:T(1,128)}), f32[32,1,1152]{2,1,0:T(1,128)S(1)}, u32[]{:S(2)}, u32[]{:S(2)}) async-start(f32[32,1,1152]{2,1,0:T(1,128)} %broadcast_in_dim.151), calls=%async_computation.6 | async-start | bytes 294912 | tf_op jit(solution)/shard_map/all_to_all | solution.py:35
  176.7 8.3 %all-to-all-done.6 = f32[32,1,1152]{2,1,0:T(1,128)S(1)} async-done(((f32[32,1,1152]{2,1,0:T(1,128)}), f32[32,1,1152]{2,1,0:T(1,128)S(1)}, u32[]{:S(2)}, u32[]{:S(2)}) %all-to-all-start.6) | async-done | bytes 147488 | tf_op jit(solution)/shard_map/all_to_all | solution.py:35
  186.2 7.1 %all-to-all-start.7 = ((f32[16,1,128]{2,1,0:T(1,128)}), f32[16,1,128]{2,1,0:T(1,128)S(1)}, u32[]{:S(2)}, u32[]{:S(2)}) async-start(f32[16,1,128]{2,1,0:T(1,128)} %broadcast_in_dim.152), calls=%async_computation.7 | async-start | bytes 16384 | tf_op jit(solution)/shard_map/all_to_all | solution.py:35
  194.4 5.9 %all-to-all-done.7 = f32[16,1,128]{2,1,0:T(1,128)S(1)} async-done(((f32[16,1,128]{2,1,0:T(1,128)}), f32[16,1,128]{2,1,0:T(1,128)S(1)}, u32[]{:S(2)}, u32[]{:S(2)}) %all-to-all-start.7) | async-done | bytes 8224 | tf_op jit(solution)/shard_map/all_to_all | solution.py:35
  201.6 4.5 %shard_map.88 = (f32[1,1536]{1,0:T(1,128)}, f32[1,128]{1,0:T(1,128)}) custom-call(f32[4,1536]{1,0:T(4,128)} %pad_maximum_fusion.11.state.refs_2_, bf16[1536,1536]{1,0:T(8,128)(2,1)} %bitcast.293, f32[40,1536]{1,0:T(8,128)} %pad.76.tests.refs_14_, f32[64,1536]{1,0:T(8,128)} %get-tuple-element.66.images.refs_15_, f32[1,1536]{1,0:T(1,128)} %copy-done.4, ...), custom_call_target="tpu_custom_call" | custom-call | flops 4718592 | bytes 6561792 | tf_op jit(solution)/shard_map/pallas_call | solution.py:473
  206.9 2.5 collective-permute-start.7
  209.4 3.0 collective-permute-start.6
  216.8 3.9 %all-to-all-start.8 = ((f32[32,1,1280]{2,1,0:T(1,128)}), f32[32,1,1280]{2,1,0:T(1,128)S(1)}, u32[]{:S(2)}, u32[]{:S(2)}) async-start(f32[32,1,1280]{2,1,0:T(1,128)} %broadcast_in_dim.154), calls=%async_computation.8 | async-start | bytes 327680 | tf_op jit(solution)/shard_map/all_to_all | solution.py:35
  221.5 10.4 %all-to-all-done.8 = f32[32,1,1280]{2,1,0:T(1,128)S(1)} async-done(((f32[32,1,1280]{2,1,0:T(1,128)}), f32[32,1,1280]{2,1,0:T(1,128)S(1)}, u32[]{:S(2)}, u32[]{:S(2)}) %all-to-all-start.8) | async-done | bytes 163872 | tf_op jit(solution)/shard_map/all_to_all | solution.py:35
  233.0 4.4 %all-to-all-start.9 = ((f32[16,1,256]{2,1,0:T(1,128)}), f32[16,1,256]{2,1,0:T(1,128)S(1)}, u32[]{:S(2)}, u32[]{:S(2)}) async-start(f32[16,1,256]{2,1,0:T(1,128)} %broadcast_in_dim.155), calls=%async_computation.9 | async-start | bytes 32768 | tf_op jit(solution)/shard_map/all_to_all | solution.py:35
  237.4 1.3 add_select_fusion.7.refs_1_
  238.7 6.0 %all-to-all-done.9 = f32[16,1,256]{2,1,0:T(1,128)S(1)} async-done(((f32[16,1,256]{2,1,0:T(1,128)}), f32[16,1,256]{2,1,0:T(1,128)S(1)}, u32[]{:S(2)}, u32[]{:S(2)}) %all-to-all-start.9) | async-done | bytes 16416 | tf_op jit(solution)/shard_map/all_to_all | solution.py:35
  245.3 4.9 %shard_map.89 = (f32[4,1536]{1,0:T(4,128)}, f32[96,1]{1,0:T(8,128)}, f32[1,128]{1,0:T(1,128)}, f32[1,1536]{1,0:T(1,128)}, f32[1,128]{1,0:T(1,128)}) custom-call(f32[16,256]{1,0:T(8,128)} %bitcast.354, f32[1,1536]{1,0:T(1,128)} %add_select_fusion.7.refs_1_, f32[4,1536]{1,0:T(4,128)} %pad_maximum_fusion.11.state.refs_2_, f32[96,1]{1,0:T(8,128)} %copy.176.refs_3_, ...), custom_call_target="tpu_custom_call" | custom-call | flops 4718592 | bytes 6561792 | tf_op jit(solution)/shard_map/pallas_call | solution.py:510
  251.0 2.3 collective-permute-start.9
  253.3 3.3 %collective-permute-start.8 = (f32[1,256]{1,0:T(1,128)S(1)}, f32[1,256]{1,0:T(1,128)S(1)}, u32[]{:S(2)}, u32[]{:S(2)}) collective-permute-start(f32[1,256]{1,0:T(1,128)S(1)} %get-tuple-element.96), channel_id=1, source_target_pairs={{0,1},{1,2},{2,3},{3,4},{4,5},{5,6},{6,7},{7,8},{8,9},{9,10},{10,1... | collective-permute-start | bytes 3080 | tf_op jit(solution)/shard_map/ppermute | solution.py:46
  258.7 14.0 %all_to_all.70 = f32[32,1,1280]{2,1,0:T(1,128)S(1)} all-to-all(f32[32,1,1280]{2,1,0:T(1,128)S(1)} %broadcast_in_dim.156), channel_id=1, replica_groups=mesh['sub'=32,'clu'=16] {'sub'}, dimensions={0} | all-to-all | bytes 327680 | tf_op jit(solution)/shard_map/all_to_all | solution.py:35
  273.8 6.5 %all-to-all-start.11 = ((f32[16,1,256]{2,1,0:T(1,128)}), f32[16,1,256]{2,1,0:T(1,128)S(1)}, u32[]{:S(2)}, u32[]{:S(2)}) async-start(f32[16,1,256]{2,1,0:T(1,128)} %broadcast_in_dim.157), calls=%async_computation.11 | async-start | bytes 32768 | tf_op jit(solution)/shard_map/all_to_all | solution.py:35
  281.6 6.0 %all-to-all-done.11 = f32[16,1,256]{2,1,0:T(1,128)S(1)} async-done(((f32[16,1,256]{2,1,0:T(1,128)}), f32[16,1,256]{2,1,0:T(1,128)S(1)}, u32[]{:S(2)}, u32[]{:S(2)}) %all-to-all-start.11) | async-done | bytes 16416 | tf_op jit(solution)/shard_map/all_to_all | solution.py:35
  288.2 4.9 %shard_map.90 = (f32[4,1536]{1,0:T(4,128)}, f32[96,1]{1,0:T(8,128)}, f32[1,128]{1,0:T(1,128)}, f32[1,1536]{1,0:T(1,128)}, f32[1,128]{1,0:T(1,128)}) custom-call(f32[16,256]{1,0:T(8,128)} %bitcast.353, f32[1,1536]{1,0:T(1,128)} %add_select_fusion.6.refs_1_, f32[4,1536]{1,0:T(4,128)} %get-tuple-element.42.refs_2_, f32[96,1]{1,0:T(8,128)} %get-tuple-element.43.refs_3_, ...), custom_call_target="tpu_custom_call" | custom-call | flops 4718592 | bytes 6561792 | tf_op jit(solution)/shard_map/pallas_call | solution.py:510
  295.2 3.9 %all-to-all-start.12 = ((f32[32,1,1152]{2,1,0:T(1,128)}), f32[32,1,1152]{2,1,0:T(1,128)S(1)}, u32[]{:S(2)}, u32[]{:S(2)}) async-start(f32[32,1,1152]{2,1,0:T(1,128)} %broadcast_in_dim.158), calls=%async_computation.12 | async-start | bytes 294912 | tf_op jit(solution)/shard_map/all_to_all | solution.py:35
  299.8 2.3 collective-permute-start.11
  302.1 3.3 %collective-permute-start.10 = (f32[1,256]{1,0:T(1,128)S(1)}, f32[1,256]{1,0:T(1,128)S(1)}, u32[]{:S(2)}, u32[]{:S(2)}) collective-permute-start(f32[1,256]{1,0:T(1,128)S(1)} %get-tuple-element.94), channel_id=1, source_target_pairs={{0,1},{1,2},{2,3},{3,4},{4,5},{5,6},{6,7},{7,8},{8,9},{9,10},{10,1... | collective-permute-start | bytes 3080 | tf_op jit(solution)/shard_map/ppermute | solution.py:46
  305.3 3.7 %all-to-all-done.12 = f32[32,1,1152]{2,1,0:T(1,128)S(1)} async-done(((f32[32,1,1152]{2,1,0:T(1,128)}), f32[32,1,1152]{2,1,0:T(1,128)S(1)}, u32[]{:S(2)}, u32[]{:S(2)}) %all-to-all-start.12) | async-done | bytes 147488 | tf_op jit(solution)/shard_map/all_to_all | solution.py:35
  309.7 5.0 %all-to-all-start.13 = ((f32[16,1,128]{2,1,0:T(1,128)}), f32[16,1,128]{2,1,0:T(1,128)S(1)}, u32[]{:S(2)}, u32[]{:S(2)}) async-start(f32[16,1,128]{2,1,0:T(1,128)} %broadcast_in_dim.159), calls=%async_computation.13 | async-start | bytes 16384 | tf_op jit(solution)/shard_map/all_to_all | solution.py:35
  316.5 5.3 %all-to-all-done.13 = f32[16,1,128]{2,1,0:T(1,128)S(1)} async-done(((f32[16,1,128]{2,1,0:T(1,128)}), f32[16,1,128]{2,1,0:T(1,128)S(1)}, u32[]{:S(2)}, u32[]{:S(2)}) %all-to-all-start.13) | async-done | bytes 8224 | tf_op jit(solution)/shard_map/all_to_all | solution.py:35
  322.4 2.2 shard_map.91
  (303 shorter events, 55.6 us)
Async XLA Ops:
  0.6 41.1 %copy-start.7 = (f32[1,1,6,6,256]{4,1,3,2,0:T(1,128)S(1)}, f32[1,1,6,6,256]{4,1,3,2,0:T(1,128)}, u32[]{:S(2)}) copy-start(f32[1,1,6,6,256]{4,1,3,2,0:T(1,128)} %param.12) | copy-start | bytes 110596
  0.6 23.6 %copy-start.8 = (f32[1,1,6,256]{3,1,2,0:T(1,128)S(1)}, f32[1,1,6,256]{3,1,2,0:T(1,128)}, u32[]{:S(2)}) copy-start(f32[1,1,6,256]{3,1,2,0:T(1,128)} %param.11) | copy-start | bytes 18436
  0.7 23.5 %copy-start.2 = (bf16[1,1,64,6,256]{4,2,3,1,0:T(8,128)(2,1)S(1)}, bf16[1,1,64,6,256]{4,2,3,1,0:T(8,128)(2,1)}, u32[]{:S(2)}) copy-start(bf16[1,1,64,6,256]{4,2,3,1,0:T(8,128)(2,1)} %param.13) | copy-start | bytes 589828
  0.7 40.8 %copy-start.13 = (s32[1,1,4]{2,1,0:T(1,128)S(1)}, s32[1,1,4]{2,1,0:T(1,128)}, u32[]{:S(2)}) copy-start(s32[1,1,4]{2,1,0:T(1,128)} %param.8) | copy-start | bytes 52
  0.7 23.2 %copy-start.12 = (s32[1,1,6]{2,1,0:T(1,128)S(1)}, s32[1,1,6]{2,1,0:T(1,128)}, u32[]{:S(2)}) copy-start(s32[1,1,6]{2,1,0:T(1,128)} %param.9) | copy-start | bytes 76
  5.4 37.4 %copy-start.10 = (f32[1,1,6,256]{3,1,2,0:T(1,128)S(1)}, f32[1,1,6,256]{3,1,2,0:T(1,128)}, u32[]{:S(2)}) copy-start(f32[1,1,6,256]{3,1,2,0:T(1,128)} %param.10) | copy-start | bytes 18436
  5.4 18.9 %collective-permute-start.1 = (f32[8,256]{1,0:T(8,128)S(1)}, f32[8,256]{1,0:T(8,128)S(1)}, u32[]{:S(2)}, u32[]{:S(2)}) collective-permute-start(f32[8,256]{1,0:T(8,128)S(1)} %get-tuple-element.89), channel_id=1, source_target_pairs={{1,0},{2,1},{3,2},{4,3},{5,4},{6,5},{7,6},{8,7},{9,8},{10,9},{11,1... | collective-permute-start | bytes 24584 | tf_op jit(solution)/shard_map/ppermute | solution.py:47
  14.2 10.1 %collective-permute-start = (f32[8,256]{1,0:T(8,128)S(1)}, f32[8,256]{1,0:T(8,128)S(1)}, u32[]{:S(2)}, u32[]{:S(2)}) collective-permute-start(f32[8,256]{1,0:T(8,128)S(1)} %get-tuple-element.88), channel_id=1, source_target_pairs={{0,1},{1,2},{2,3},{3,4},{4,5},{5,6},{6,7},{7,8},{8,9},{9,10},{10,1... | collective-permute-start | bytes 24584 | tf_op jit(solution)/shard_map/ppermute | solution.py:46
  17.5 23.9 %all-to-all-start = ((f32[32,1,4224]{2,1,0:T(1,128)}), f32[32,1,4224]{2,1,0:T(1,128)S(1)}, u32[]{:S(2)}, u32[]{:S(2)}) async-start(f32[32,1,4224]{2,1,0:T(1,128)} %copy.149), calls=%async_computation | async-start | bytes 1081344 | tf_op jit(solution)/shard_map/all_to_all | solution.py:39
  44.7 20.9 %all-to-all-start.1 = ((f32[32,1,3968]{2,1,0:T(1,128)}), f32[32,1,3968]{2,1,0:T(1,128)S(1)}, u32[]{:S(2)}, u32[]{:S(2)}) async-start(f32[32,1,3968]{2,1,0:T(1,128)} %broadcast_in_dim.67), calls=%async_computation.1 | async-start | bytes 1015808 | tf_op jit(solution)/shard_map/all_to_all | solution.py:39
  49.2 6.7 %collective-permute-start.3 = (f32[64,256]{1,0:T(8,128)S(1)}, f32[64,256]{1,0:T(8,128)S(1)}, u32[]{:S(2)}, u32[]{:S(2)}) collective-permute-start(f32[64,256]{1,0:T(8,128)S(1)} %get-tuple-element.77), channel_id=1, source_target_pairs={{1,0},{2,1},{3,2},{4,3},{5,4},{6,5},{7,6},{8,7},{9,8},{10,9},{11,1... | collective-permute-start | bytes 196616 | tf_op jit(solution)/shard_map/ppermute | solution.py:47
  51.5 5.3 %collective-permute-start.2 = (f32[64,256]{1,0:T(8,128)S(1)}, f32[64,256]{1,0:T(8,128)S(1)}, u32[]{:S(2)}, u32[]{:S(2)}) collective-permute-start(f32[64,256]{1,0:T(8,128)S(1)} %get-tuple-element.76), channel_id=1, source_target_pairs={{0,1},{1,2},{2,3},{3,4},{4,5},{5,6},{6,7},{7,8},{8,9},{9,10},{10,1... | collective-permute-start | bytes 196616 | tf_op jit(solution)/shard_map/ppermute | solution.py:46
  55.5 120.9 %copy-start.4 = (f32[1,1536]{1,0:T(1,128)}, f32[1,1536]{1,0:T(1,128)S(1)}, u32[]{:S(2)}) copy-start(f32[1,1536]{1,0:T(1,128)S(1)} %get-tuple-element.101.weights.refs_12_) | copy-start | bytes 18436
  66.4 20.9 %all-to-all-start.2 = ((f32[16,1,1920]{2,1,0:T(1,128)}), f32[16,1,1920]{2,1,0:T(1,128)S(1)}, u32[]{:S(2)}, u32[]{:S(2)}) async-start(f32[16,1,1920]{2,1,0:T(1,128)} %broadcast_in_dim.70), calls=%async_computation.2 | async-start | bytes 245760 | tf_op jit(solution)/shard_map/all_to_all | solution.py:35
  101.2 67.0 %copy-start = (f32[64,1536]{1,0:T(8,128)}, f32[64,1536]{1,0:T(8,128)S(1)}, u32[]{:S(2)}) copy-start(f32[64,1536]{1,0:T(8,128)S(1)} %slice.295.refs_11_) | copy-start | bytes 1179652
  107.8 17.1 %all-to-all-start.3 = ((f32[32,1,2304]{2,1,0:T(1,128)}), f32[32,1,2304]{2,1,0:T(1,128)S(1)}, u32[]{:S(2)}, u32[]{:S(2)}) async-start(f32[32,1,2304]{2,1,0:T(1,128)} %copy.162), calls=%async_computation.3 | async-start | bytes 589824 | tf_op jit(solution)/shard_map/all_to_all | solution.py:39
  125.6 12.3 %all-to-all-start.4 = ((f32[16,1,256]{2,1,0:T(1,128)}), f32[16,1,256]{2,1,0:T(1,128)S(1)}, u32[]{:S(2)}, u32[]{:S(2)}) async-start(f32[16,1,256]{2,1,0:T(1,128)} %broadcast_in_dim.73), calls=%async_computation.4 | async-start | bytes 32768 | tf_op jit(solution)/shard_map/all_to_all | solution.py:35
  130.5 36.1 %copy-start.1 = (f32[96,96]{1,0:T(8,128)S(1)}, f32[96,96]{1,0:T(8,128)}, u32[]{:S(2)}) copy-start(f32[96,96]{1,0:T(8,128)} %shard_map.86) | copy-start | bytes 110596
  139.3 17.8 %all-to-all-start.5 = ((f32[32,1,3072]{2,1,0:T(1,128)}), f32[32,1,3072]{2,1,0:T(1,128)S(1)}, u32[]{:S(2)}, u32[]{:S(2)}) async-start(f32[32,1,3072]{2,1,0:T(1,128)} %broadcast_in_dim.148), calls=%async_computation.5 | async-start | bytes 786432 | tf_op jit(solution)/shard_map/all_to_all | solution.py:39
  145.0 7.2 %collective-permute-start.5 = (f32[64,256]{1,0:T(8,128)S(1)}, f32[64,256]{1,0:T(8,128)S(1)}, u32[]{:S(2)}, u32[]{:S(2)}) collective-permute-start(f32[64,256]{1,0:T(8,128)S(1)} %bitcast.357), channel_id=1, source_target_pairs={{1,0},{2,1},{3,2},{4,3},{5,4},{6,5},{7,6},{8,7},{9,8},{10,9},{11,1... | collective-permute-start | bytes 196616 | tf_op jit(solution)/shard_map/ppermute | solution.py:47
  147.4 4.8 %collective-permute-start.4 = (f32[64,256]{1,0:T(8,128)S(1)}, f32[64,256]{1,0:T(8,128)S(1)}, u32[]{:S(2)}, u32[]{:S(2)}) collective-permute-start(f32[64,256]{1,0:T(8,128)S(1)} %bitcast.359), channel_id=1, source_target_pairs={{0,1},{1,2},{2,3},{3,4},{4,5},{5,6},{6,7},{7,8},{8,9},{9,10},{10,1... | collective-permute-start | bytes 196616 | tf_op jit(solution)/shard_map/ppermute | solution.py:46
  165.3 28.1 %copy-start.3 = (f32[64,64]{1,0:T(8,128)S(1)}, f32[64,64]{1,0:T(8,128)}, u32[]{:S(2)}) copy-start(f32[64,64]{1,0:T(8,128)} %shard_map.87) | copy-start | bytes 49156
  170.6 14.3 %all-to-all-start.6 = ((f32[32,1,1152]{2,1,0:T(1,128)}), f32[32,1,1152]{2,1,0:T(1,128)S(1)}, u32[]{:S(2)}, u32[]{:S(2)}) async-start(f32[32,1,1152]{2,1,0:T(1,128)} %broadcast_in_dim.151), calls=%async_computation.6 | async-start | bytes 294912 | tf_op jit(solution)/shard_map/all_to_all | solution.py:35
  176.7 38.1 %copy-start.5 = (f32[1,1536]{1,0:T(1,128)S(1)}, f32[1,1536]{1,0:T(1,128)}, u32[]{:S(2)}) copy-start(f32[1,1536]{1,0:T(1,128)} %copy-done.4) | copy-start | bytes 18436
  186.2 14.1 %all-to-all-start.7 = ((f32[16,1,128]{2,1,0:T(1,128)}), f32[16,1,128]{2,1,0:T(1,128)S(1)}, u32[]{:S(2)}, u32[]{:S(2)}) async-start(f32[16,1,128]{2,1,0:T(1,128)} %broadcast_in_dim.152), calls=%async_computation.7 | async-start | bytes 16384 | tf_op jit(solution)/shard_map/all_to_all | solution.py:35
  200.3 45.0 %copy-start.11 = (f32[128]{0:T(128)}, f32[128]{0:T(128)S(1)}, u32[]{:S(2)}) copy-start(f32[128]{0:T(128)S(1)} %reduce_sum.133) | copy-start | bytes 1540
  206.9 7.9 %collective-permute-start.7 = (f32[1,256]{1,0:T(1,128)S(1)}, f32[1,256]{1,0:T(1,128)S(1)}, u32[]{:S(2)}, u32[]{:S(2)}) collective-permute-start(f32[1,256]{1,0:T(1,128)S(1)} %get-tuple-element.99), channel_id=1, source_target_pairs={{1,0},{2,1},{3,2},{4,3},{5,4},{6,5},{7,6},{8,7},{9,8},{10,9},{11,1... | collective-permute-start | bytes 3080 | tf_op jit(solution)/shard_map/ppermute | solution.py:47
  209.4 5.3 %collective-permute-start.6 = (f32[1,256]{1,0:T(1,128)S(1)}, f32[1,256]{1,0:T(1,128)S(1)}, u32[]{:S(2)}, u32[]{:S(2)}) collective-permute-start(f32[1,256]{1,0:T(1,128)S(1)} %get-tuple-element.98), channel_id=1, source_target_pairs={{0,1},{1,2},{2,3},{3,4},{4,5},{5,6},{6,7},{7,8},{8,9},{9,10},{10,1... | collective-permute-start | bytes 3080 | tf_op jit(solution)/shard_map/ppermute | solution.py:46
  213.3 43.9 %copy-start.6 = (f32[1,1536]{1,0:T(1,128)S(1)}, f32[1,1536]{1,0:T(1,128)}, u32[]{:S(2)}) copy-start(f32[1,1536]{1,0:T(1,128)} %copy-done.4) | copy-start | bytes 18436
  216.8 15.1 %all-to-all-start.8 = ((f32[32,1,1280]{2,1,0:T(1,128)}), f32[32,1,1280]{2,1,0:T(1,128)S(1)}, u32[]{:S(2)}, u32[]{:S(2)}) async-start(f32[32,1,1280]{2,1,0:T(1,128)} %broadcast_in_dim.154), calls=%async_computation.8 | async-start | bytes 327680 | tf_op jit(solution)/shard_map/all_to_all | solution.py:35
  233.0 11.7 %all-to-all-start.9 = ((f32[16,1,256]{2,1,0:T(1,128)}), f32[16,1,256]{2,1,0:T(1,128)S(1)}, u32[]{:S(2)}, u32[]{:S(2)}) async-start(f32[16,1,256]{2,1,0:T(1,128)} %broadcast_in_dim.155), calls=%async_computation.9 | async-start | bytes 32768 | tf_op jit(solution)/shard_map/all_to_all | solution.py:35
  251.0 6.3 %collective-permute-start.9 = (f32[1,256]{1,0:T(1,128)S(1)}, f32[1,256]{1,0:T(1,128)S(1)}, u32[]{:S(2)}, u32[]{:S(2)}) collective-permute-start(f32[1,256]{1,0:T(1,128)S(1)} %get-tuple-element.97), channel_id=1, source_target_pairs={{1,0},{2,1},{3,2},{4,3},{5,4},{6,5},{7,6},{8,7},{9,8},{10,9},{11,1... | collective-permute-start | bytes 3080 | tf_op jit(solution)/shard_map/ppermute | solution.py:47
  253.3 4.0 %collective-permute-start.8 = (f32[1,256]{1,0:T(1,128)S(1)}, f32[1,256]{1,0:T(1,128)S(1)}, u32[]{:S(2)}, u32[]{:S(2)}) collective-permute-start(f32[1,256]{1,0:T(1,128)S(1)} %get-tuple-element.96), channel_id=1, source_target_pairs={{0,1},{1,2},{2,3},{3,4},{4,5},{5,6},{6,7},{7,8},{8,9},{9,10},{10,1... | collective-permute-start | bytes 3080 | tf_op jit(solution)/shard_map/ppermute | solution.py:46
  273.8 13.8 %all-to-all-start.11 = ((f32[16,1,256]{2,1,0:T(1,128)}), f32[16,1,256]{2,1,0:T(1,128)S(1)}, u32[]{:S(2)}, u32[]{:S(2)}) async-start(f32[16,1,256]{2,1,0:T(1,128)} %broadcast_in_dim.157), calls=%async_computation.11 | async-start | bytes 32768 | tf_op jit(solution)/shard_map/all_to_all | solution.py:35
  295.2 13.9 %all-to-all-start.12 = ((f32[32,1,1152]{2,1,0:T(1,128)}), f32[32,1,1152]{2,1,0:T(1,128)S(1)}, u32[]{:S(2)}, u32[]{:S(2)}) async-start(f32[32,1,1152]{2,1,0:T(1,128)} %broadcast_in_dim.158), calls=%async_computation.12 | async-start | bytes 294912 | tf_op jit(solution)/shard_map/all_to_all | solution.py:35
  299.8 15.3 %collective-permute-start.11 = (f32[1,256]{1,0:T(1,128)S(1)}, f32[1,256]{1,0:T(1,128)S(1)}, u32[]{:S(2)}, u32[]{:S(2)}) collective-permute-start(f32[1,256]{1,0:T(1,128)S(1)} %get-tuple-element.95), channel_id=1, source_target_pairs={{1,0},{2,1},{3,2},{4,3},{5,4},{6,5},{7,6},{8,7},{9,8},{10,9},{11,1... | collective-permute-start | bytes 3080 | tf_op jit(solution)/shard_map/ppermute | solution.py:47
  302.1 13.0 %collective-permute-start.10 = (f32[1,256]{1,0:T(1,128)S(1)}, f32[1,256]{1,0:T(1,128)S(1)}, u32[]{:S(2)}, u32[]{:S(2)}) collective-permute-start(f32[1,256]{1,0:T(1,128)S(1)} %get-tuple-element.94), channel_id=1, source_target_pairs={{0,1},{1,2},{2,3},{3,4},{4,5},{5,6},{6,7},{7,8},{8,9},{9,10},{10,1... | collective-permute-start | bytes 3080 | tf_op jit(solution)/shard_map/ppermute | solution.py:46
  309.7 12.1 %all-to-all-start.13 = ((f32[16,1,128]{2,1,0:T(1,128)}), f32[16,1,128]{2,1,0:T(1,128)S(1)}, u32[]{:S(2)}, u32[]{:S(2)}) async-start(f32[16,1,128]{2,1,0:T(1,128)} %broadcast_in_dim.159), calls=%async_computation.13 | async-start | bytes 16384 | tf_op jit(solution)/shard_map/all_to_all | solution.py:35
  321.8 0.6 copy-start.9

commit v4 on v3

--- a/solution.py
+++ b/solution.py
@@ -466,7 +466,8 @@
     state = jnp.concatenate([deflated_search, solution, residual, deflated_search], axis=0)
     shared = (lift, lift_mask, by_coarse, by_weighted, by_products, padded_cols, basis, weights)
     scratch = [pltpu.VMEM(local_op.shape, jnp.bfloat16), pltpu.SemaphoreType.DMA((PARTS,))]
-    anywhere = pl.BlockSpec(memory_space=pl.ANY)
+    params = pltpu.CompilerParams(vmem_limit_bytes=52 * 2**20)
+    anywhere = pl.BlockSpec(memory_space=pltpu.HBM)
     cost = pl.CostEstimate(
         flops=2 * width * width, bytes_accessed=2 * width * width + 4 * 300 * width, transcendentals=0
     )
@@ -476,6 +477,7 @@
         in_specs=[VMEM, anywhere, VMEM, VMEM, VMEM, VMEM],
         out_specs=(VMEM, VMEM),
         scratch_shapes=scratch,
+        compiler_params=params,
         cost_estimate=cost,
     )(state, local_op, tests, weighted_images, weights, flat_live)
     for iteration in range(ITERS):
@@ -505,6 +507,7 @@
                 out_shape=(shape_of(1, width), shape_of(1, width)),
                 in_specs=[VMEM] * 13,
                 out_specs=(VMEM, VMEM),
+                compiler_params=params,
             )(*ahead, *shared)
             break
         state, weighted_residual, rho, product, sums = pl.pallas_call(
@@ -519,6 +522,7 @@
             in_specs=[VMEM] * 13 + [anywhere, VMEM, VMEM, VMEM],
             out_specs=(VMEM,) * 5,
             scratch_shapes=scratch,
+            compiler_params=params,
             cost_estimate=cost,
         )(*ahead, *shared, local_op, tests, weighted_images, flat_live)
     return (solution.reshape(1, 1, 6, slots), residual.reshape(1, 1, 6, slots))

time: 327 us -> 312 us (0.954)
  other arithmetic: 17.1 us -> 5.24 us
  waiting for transfers between devices: 104 us -> 112 us
  Pallas kernels: 32.8 us -> 26.6 us
  local copies, waits for them, and re-layouts: 26.7 us -> 20.9 us
    all_to_all x9, waiting for transfers between devices: 60.7 us -> 66.4 us  [everyone(): lax.all_to_all(sent, axis, split_axis=0, concat_axis=0, tiled=True)[:, 0, :]]
    mul x3, other arithmetic: 3.91 us -> 0.05 us  [local(): live * (faces + jnp.concatenate([inner, low, high], axis=0))]
  transfers between devices with their start and end apart: 25 -> 25, of which waited for: 14 -> 17; matrix products, arithmetic and copies ran while one was open for 6% -> 3% of each run, Pallas kernels for 0% -> 0%
where the time goes in v4:
time: 312 us; the launch traced here: 311 us
  starting transfers between devices  112 us (36%)
  waiting for transfers between devices  112 us (36%)
  Pallas kernels  26.6 us (9%)
  local copies, waits for them, and re-layouts  20.9 us (7%)
  matrix products  17.6 us (6%)
  blocking collectives  14 us (4%)
  other arithmetic  5.24 us (2%)
    all_to_all x9, waiting for transfers between devices, everyone(): lax.all_to_all(sent, axis, split_axis=0, concat_axis=0, tiled=True)[:, 0, :]  66.4 us
    all_to_all x9, starting transfers between devices, everyone(): lax.all_to_all(sent, axis, split_axis=0, concat_axis=0, tiled=True)[:, 0, :]  53.3 us
    all_to_all x4, waiting for transfers between devices, trade(): lax.all_to_all(rows[:, None, :], axis, split_axis=0, concat_axis=0, tiled...  43.2 us
    ppermute x6, starting transfers between devices, rims(): high = lax.ppermute(values[:, 4, :], 'clu', backward)  20.7 us
    all_to_all x4, starting transfers between devices, trade(): lax.all_to_all(rows[:, None, :], axis, split_axis=0, concat_axis=0, tiled...  18.8 us
    ppermute x6, starting transfers between devices, rims(): low = lax.ppermute(values[:, 5, :], 'clu', forward)  18.7 us
    pallas_call x2, Pallas kernels, spd_inverse(): pl.pallas_call(invert, out_shape=jax.ShapeDtypeStruct((size, size), jnp.f...  16.2 us
    all_to_all x1, blocking collectives, everyone(): lax.all_to_all(sent, axis, split_axis=0, concat_axis=0, tiled=True)[:, 0, :]  14 us
  transfers between devices with their start and end apart: 25, of which 17 were waited for; matrix products, arithmetic and copies ran while one was open for 3% of the time, Pallas kernels for 0%

profile of v4, /device:TPU:1, one launch (start us, length us, event | category | flops | bytes accessed | tf_op | source)
XLA Modules:
  0.0 310.6 jit_solution(18444971416966876389)
XLA Ops:
  4.3 1.1 fusion.136
  5.4 8.8 %collective-permute-start.1 = (f32[8,256]{1,0:T(8,128)S(1)}, f32[8,256]{1,0:T(8,128)S(1)}, u32[]{:S(2)}, u32[]{:S(2)}) collective-permute-start(f32[8,256]{1,0:T(8,128)S(1)} %get-tuple-element.89), channel_id=1, source_target_pairs={{1,0},{2,1},{3,2},{4,3},{5,4},{6,5},{7,6},{8,7},{9,8},{10,9},{11,1... | collective-permute-start | bytes 24584 | tf_op jit(solution)/shard_map/ppermute | solution.py:47
  14.2 1.9 collective-permute-start
  16.1 1.4 copy.149
  17.5 6.3 %all-to-all-start = ((f32[32,1,4224]{2,1,0:T(1,128)}), f32[32,1,4224]{2,1,0:T(1,128)S(1)}, u32[]{:S(2)}, u32[]{:S(2)}) async-start(f32[32,1,4224]{2,1,0:T(1,128)} %copy.149), calls=%async_computation | async-start | bytes 1081344 | tf_op jit(solution)/shard_map/all_to_all | solution.py:39
  24.4 17.0 %all-to-all-done = f32[32,1,4224]{2,1,0:T(1,128)S(1)} async-done(((f32[32,1,4224]{2,1,0:T(1,128)}), f32[32,1,4224]{2,1,0:T(1,128)S(1)}, u32[]{:S(2)}, u32[]{:S(2)}) %all-to-all-start) | async-done | bytes 540704 | tf_op jit(solution)/shard_map/all_to_all | solution.py:39
  43.6 1.2 broadcast_in_dim.67
  44.7 4.4 %all-to-all-start.1 = ((f32[32,1,3968]{2,1,0:T(1,128)}), f32[32,1,3968]{2,1,0:T(1,128)S(1)}, u32[]{:S(2)}, u32[]{:S(2)}) async-start(f32[32,1,3968]{2,1,0:T(1,128)} %broadcast_in_dim.67), calls=%async_computation.1 | async-start | bytes 1015808 | tf_op jit(solution)/shard_map/all_to_all | solution.py:39
  49.2 2.3 collective-permute-start.3
  51.5 3.9 %collective-permute-start.2 = (f32[64,256]{1,0:T(8,128)S(1)}, f32[64,256]{1,0:T(8,128)S(1)}, u32[]{:S(2)}, u32[]{:S(2)}) collective-permute-start(f32[64,256]{1,0:T(8,128)S(1)} %get-tuple-element.76), channel_id=1, source_target_pairs={{0,1},{1,2},{2,3},{3,4},{4,5},{5,6},{6,7},{7,8},{8,9},{9,10},{10,1... | collective-permute-start | bytes 196616 | tf_op jit(solution)/shard_map/ppermute | solution.py:46
  56.8 8.8 %all-to-all-done.1 = f32[32,1,3968]{2,1,0:T(1,128)S(1)} async-done(((f32[32,1,3968]{2,1,0:T(1,128)}), f32[32,1,3968]{2,1,0:T(1,128)S(1)}, u32[]{:S(2)}, u32[]{:S(2)}) %all-to-all-start.1) | async-done | bytes 507936 | tf_op jit(solution)/shard_map/all_to_all | solution.py:39
  66.4 11.9 %all-to-all-start.2 = ((f32[16,1,1920]{2,1,0:T(1,128)}), f32[16,1,1920]{2,1,0:T(1,128)S(1)}, u32[]{:S(2)}, u32[]{:S(2)}) async-start(f32[16,1,1920]{2,1,0:T(1,128)} %broadcast_in_dim.70), calls=%async_computation.2 | async-start | bytes 245760 | tf_op jit(solution)/shard_map/all_to_all | solution.py:35
  79.0 8.3 %all-to-all-done.2 = f32[16,1,1920]{2,1,0:T(1,128)S(1)} async-done(((f32[16,1,1920]{2,1,0:T(1,128)}), f32[16,1,1920]{2,1,0:T(1,128)S(1)}, u32[]{:S(2)}, u32[]{:S(2)}) %all-to-all-start.2) | async-done | bytes 122912 | tf_op jit(solution)/shard_map/all_to_all | solution.py:35
  90.5 9.7 %shard_map.86 = f32[96,96]{1,0:T(8,128)} custom-call(f32[96,96]{1,0:T(8,128)} %copy.196.matrix_ref), custom_call_target="tpu_custom_call" | custom-call | flops 1769472 | bytes 73728 | tf_op jit(solution)/shard_map/pallas_call | solution.py:94
  101.9 3.3 %convolution_multiply_fusion = f32[64,1536]{1,0:T(8,128)S(1)} fusion(f32[1536]{0:T(1024)S(1)} %get-tuple-element.68, bf16[1,1,1536,1536]{3,2,1,0:T(8,128)(2,1)} %param.7, f32[65,1536]{1,0:T(8,128)S(1)} %convolution_subtract_fusion), kind=kOutput, calls=%fused_computation.1 | convolution fusion | flops 302088192 | bytes 5316608 | tf_op jit(solution)/shard_map/dot_general | solution.py:348
  108.2 4.3 %all-to-all-start.3 = ((f32[32,1,2304]{2,1,0:T(1,128)}), f32[32,1,2304]{2,1,0:T(1,128)S(1)}, u32[]{:S(2)}, u32[]{:S(2)}) async-start(f32[32,1,2304]{2,1,0:T(1,128)} %copy.162), calls=%async_computation.3 | async-start | bytes 589824 | tf_op jit(solution)/shard_map/all_to_all | solution.py:39
  114.3 11.0 %all-to-all-done.3 = f32[32,1,2304]{2,1,0:T(1,128)S(1)} async-done(((f32[32,1,2304]{2,1,0:T(1,128)}), f32[32,1,2304]{2,1,0:T(1,128)S(1)}, u32[]{:S(2)}, u32[]{:S(2)}) %all-to-all-start.3) | async-done | bytes 294944 | tf_op jit(solution)/shard_map/all_to_all | solution.py:39
  126.1 4.9 %all-to-all-start.4 = ((f32[16,1,256]{2,1,0:T(1,128)}), f32[16,1,256]{2,1,0:T(1,128)S(1)}, u32[]{:S(2)}, u32[]{:S(2)}) async-start(f32[16,1,256]{2,1,0:T(1,128)} %broadcast_in_dim.73), calls=%async_computation.4 | async-start | bytes 32768 | tf_op jit(solution)/shard_map/all_to_all | solution.py:35
  131.6 6.8 %all-to-all-done.4 = f32[16,1,256]{2,1,0:T(1,128)S(1)} async-done(((f32[16,1,256]{2,1,0:T(1,128)}), f32[16,1,256]{2,1,0:T(1,128)S(1)}, u32[]{:S(2)}, u32[]{:S(2)}) %all-to-all-start.4) | async-done | bytes 16416 | tf_op jit(solution)/shard_map/all_to_all | solution.py:35
  139.8 3.9 %all-to-all-start.5 = ((f32[32,1,3072]{2,1,0:T(1,128)}), f32[32,1,3072]{2,1,0:T(1,128)S(1)}, u32[]{:S(2)}, u32[]{:S(2)}) async-start(f32[32,1,3072]{2,1,0:T(1,128)} %broadcast_in_dim.148), calls=%async_computation.5 | async-start | bytes 786432 | tf_op jit(solution)/shard_map/all_to_all | solution.py:39
  144.2 2.4 collective-permute-start.5
  146.6 3.4 %collective-permute-start.4 = (f32[64,256]{1,0:T(8,128)S(1)}, f32[64,256]{1,0:T(8,128)S(1)}, u32[]{:S(2)}, u32[]{:S(2)}) collective-permute-start(f32[64,256]{1,0:T(8,128)S(1)} %bitcast.365), channel_id=1, source_target_pairs={{0,1},{1,2},{2,3},{3,4},{4,5},{5,6},{6,7},{7,8},{8,9},{9,10},{10,1... | collective-permute-start | bytes 196616 | tf_op jit(solution)/shard_map/ppermute | solution.py:46
  151.1 6.4 %all-to-all-done.5 = f32[32,1,3072]{2,1,0:T(1,128)S(1)} async-done(((f32[32,1,3072]{2,1,0:T(1,128)}), f32[32,1,3072]{2,1,0:T(1,128)S(1)}, u32[]{:S(2)}, u32[]{:S(2)}) %all-to-all-start.5) | async-done | bytes 393248 | tf_op jit(solution)/shard_map/all_to_all | solution.py:39
  159.9 6.6 %shard_map.87 = f32[64,64]{1,0:T(8,128)} custom-call(f32[64,64]{1,0:T(8,128)} %fusion.83.matrix_ref), custom_call_target="tpu_custom_call" | custom-call | flops 524288 | bytes 32768 | tf_op jit(solution)/shard_map/pallas_call | solution.py:94
  171.1 4.8 %all-to-all-start.6 = ((f32[32,1,1152]{2,1,0:T(1,128)}), f32[32,1,1152]{2,1,0:T(1,128)S(1)}, u32[]{:S(2)}, u32[]{:S(2)}) async-start(f32[32,1,1152]{2,1,0:T(1,128)} %broadcast_in_dim.151), calls=%async_computation.6 | async-start | bytes 294912 | tf_op jit(solution)/shard_map/all_to_all | solution.py:35
  176.5 8.9 %all-to-all-done.6 = f32[32,1,1152]{2,1,0:T(1,128)S(1)} async-done(((f32[32,1,1152]{2,1,0:T(1,128)}), f32[32,1,1152]{2,1,0:T(1,128)S(1)}, u32[]{:S(2)}, u32[]{:S(2)}) %all-to-all-start.6) | async-done | bytes 147488 | tf_op jit(solution)/shard_map/all_to_all | solution.py:35
  186.6 6.3 %all-to-all-start.7 = ((f32[16,1,128]{2,1,0:T(1,128)}), f32[16,1,128]{2,1,0:T(1,128)S(1)}, u32[]{:S(2)}, u32[]{:S(2)}) async-start(f32[16,1,128]{2,1,0:T(1,128)} %broadcast_in_dim.152), calls=%async_computation.7 | async-start | bytes 16384 | tf_op jit(solution)/shard_map/all_to_all | solution.py:35
  194.0 5.9 %all-to-all-done.7 = f32[16,1,128]{2,1,0:T(1,128)S(1)} async-done(((f32[16,1,128]{2,1,0:T(1,128)}), f32[16,1,128]{2,1,0:T(1,128)S(1)}, u32[]{:S(2)}, u32[]{:S(2)}) %all-to-all-start.7) | async-done | bytes 8224 | tf_op jit(solution)/shard_map/all_to_all | solution.py:35
  200.7 2.8 shard_map.88
  203.6 2.6 collective-permute-start.7
  206.2 3.0 collective-permute-start.6
  210.7 3.9 %all-to-all-start.8 = ((f32[32,1,1280]{2,1,0:T(1,128)}), f32[32,1,1280]{2,1,0:T(1,128)S(1)}, u32[]{:S(2)}, u32[]{:S(2)}) async-start(f32[32,1,1280]{2,1,0:T(1,128)} %broadcast_in_dim.154), calls=%async_computation.8 | async-start | bytes 327680 | tf_op jit(solution)/shard_map/all_to_all | solution.py:35
  214.8 10.9 %all-to-all-done.8 = f32[32,1,1280]{2,1,0:T(1,128)S(1)} async-done(((f32[32,1,1280]{2,1,0:T(1,128)}), f32[32,1,1280]{2,1,0:T(1,128)S(1)}, u32[]{:S(2)}, u32[]{:S(2)}) %all-to-all-start.8) | async-done | bytes 163872 | tf_op jit(solution)/shard_map/all_to_all | solution.py:35
  226.8 6.1 %all-to-all-start.9 = ((f32[16,1,256]{2,1,0:T(1,128)}), f32[16,1,256]{2,1,0:T(1,128)S(1)}, u32[]{:S(2)}, u32[]{:S(2)}) async-start(f32[16,1,256]{2,1,0:T(1,128)} %broadcast_in_dim.155), calls=%async_computation.9 | async-start | bytes 32768 | tf_op jit(solution)/shard_map/all_to_all | solution.py:35
  233.0 7.3 %all-to-all-done.9 = f32[16,1,256]{2,1,0:T(1,128)S(1)} async-done(((f32[16,1,256]{2,1,0:T(1,128)}), f32[16,1,256]{2,1,0:T(1,128)S(1)}, u32[]{:S(2)}, u32[]{:S(2)}) %all-to-all-start.9) | async-done | bytes 16416 | tf_op jit(solution)/shard_map/all_to_all | solution.py:35
  240.3 3.3 %shard_map.89 = (f32[4,1536]{1,0:T(4,128)S(1)}, f32[96,1]{1,0:T(8,128)S(1)}, f32[1,128]{1,0:T(1,128)S(1)}, f32[1,1536]{1,0:T(1,128)S(1)}, f32[1,128]{1,0:T(1,128)S(1)}) custom-call(f32[16,256]{1,0:T(8,128)S(1)} %bitcast.294, f32[1,1536]{1,0:T(1,128)S(1)} %add_select_fusion.7.refs_1_, f32[4,1536]{1,0:T(4,128)S(1)} %pad_maximum_fusion.11.state.refs_2_, ...), custom_call_target="tpu_custom_call" | custom-call | flops 4718592 | bytes 6561792 | tf_op jit(solution)/shard_map/pallas_call | solution.py:513
  243.6 2.3 collective-permute-start.9
  246.0 3.3 %collective-permute-start.8 = (f32[1,256]{1,0:T(1,128)S(1)}, f32[1,256]{1,0:T(1,128)S(1)}, u32[]{:S(2)}, u32[]{:S(2)}) collective-permute-start(f32[1,256]{1,0:T(1,128)S(1)} %get-tuple-element.96), channel_id=1, source_target_pairs={{0,1},{1,2},{2,3},{3,4},{4,5},{5,6},{6,7},{7,8},{8,9},{9,10},{10,1... | collective-permute-start | bytes 3080 | tf_op jit(solution)/shard_map/ppermute | solution.py:46
  250.1 14.0 %all_to_all.70 = f32[32,1,1280]{2,1,0:T(1,128)S(1)} all-to-all(f32[32,1,1280]{2,1,0:T(1,128)S(1)} %broadcast_in_dim.156), channel_id=1, replica_groups=mesh['sub'=32,'clu'=16] {'sub'}, dimensions={0} | all-to-all | bytes 327680 | tf_op jit(solution)/shard_map/all_to_all | solution.py:35
  265.1 6.5 %all-to-all-start.11 = ((f32[16,1,256]{2,1,0:T(1,128)}), f32[16,1,256]{2,1,0:T(1,128)S(1)}, u32[]{:S(2)}, u32[]{:S(2)}) async-start(f32[16,1,256]{2,1,0:T(1,128)} %broadcast_in_dim.157), calls=%async_computation.11 | async-start | bytes 32768 | tf_op jit(solution)/shard_map/all_to_all | solution.py:35
  271.7 7.3 %all-to-all-done.11 = f32[16,1,256]{2,1,0:T(1,128)S(1)} async-done(((f32[16,1,256]{2,1,0:T(1,128)}), f32[16,1,256]{2,1,0:T(1,128)S(1)}, u32[]{:S(2)}, u32[]{:S(2)}) %all-to-all-start.11) | async-done | bytes 16416 | tf_op jit(solution)/shard_map/all_to_all | solution.py:35
  278.9 3.3 %shard_map.90 = (f32[4,1536]{1,0:T(4,128)S(1)}, f32[96,1]{1,0:T(8,128)S(1)}, f32[1,128]{1,0:T(1,128)S(1)}, f32[1,1536]{1,0:T(1,128)S(1)}, f32[1,128]{1,0:T(1,128)S(1)}) custom-call(f32[16,256]{1,0:T(8,128)S(1)} %bitcast.293, f32[1,1536]{1,0:T(1,128)S(1)} %add_select_fusion.6.refs_1_, f32[4,1536]{1,0:T(4,128)S(1)} %get-tuple-element.42.refs_2_, ...), custom_call_target="tpu_custom_call" | custom-call | flops 4718592 | bytes 6561792 | tf_op jit(solution)/shard_map/pallas_call | solution.py:513
  283.0 3.9 %all-to-all-start.12 = ((f32[32,1,1152]{2,1,0:T(1,128)}), f32[32,1,1152]{2,1,0:T(1,128)S(1)}, u32[]{:S(2)}, u32[]{:S(2)}) async-start(f32[32,1,1152]{2,1,0:T(1,128)} %broadcast_in_dim.158), calls=%async_computation.12 | async-start | bytes 294912 | tf_op jit(solution)/shard_map/all_to_all | solution.py:35
  286.9 2.3 collective-permute-start.11
  289.3 3.3 %collective-permute-start.10 = (f32[1,256]{1,0:T(1,128)S(1)}, f32[1,256]{1,0:T(1,128)S(1)}, u32[]{:S(2)}, u32[]{:S(2)}) collective-permute-start(f32[1,256]{1,0:T(1,128)S(1)} %get-tuple-element.94), channel_id=1, source_target_pairs={{0,1},{1,2},{2,3},{3,4},{4,5},{5,6},{6,7},{7,8},{8,9},{9,10},{10,1... | collective-permute-start | bytes 3080 | tf_op jit(solution)/shard_map/ppermute | solution.py:46
  292.5 4.4 %all-to-all-done.12 = f32[32,1,1152]{2,1,0:T(1,128)S(1)} async-done(((f32[32,1,1152]{2,1,0:T(1,128)}), f32[32,1,1152]{2,1,0:T(1,128)S(1)}, u32[]{:S(2)}, u32[]{:S(2)}) %all-to-all-start.12) | async-done | bytes 147488 | tf_op jit(solution)/shard_map/all_to_all | solution.py:35
  297.6 5.0 %all-to-all-start.13 = ((f32[16,1,128]{2,1,0:T(1,128)}), f32[16,1,128]{2,1,0:T(1,128)S(1)}, u32[]{:S(2)}, u32[]{:S(2)}) async-start(f32[16,1,128]{2,1,0:T(1,128)} %broadcast_in_dim.159), calls=%async_computation.13 | async-start | bytes 16384 | tf_op jit(solution)/shard_map/all_to_all | solution.py:35
  303.1 6.6 %all-to-all-done.13 = f32[16,1,128]{2,1,0:T(1,128)S(1)} async-done(((f32[16,1,128]{2,1,0:T(1,128)}), f32[16,1,128]{2,1,0:T(1,128)S(1)}, u32[]{:S(2)}, u32[]{:S(2)}) %all-to-all-start.13) | async-done | bytes 8224 | tf_op jit(solution)/shard_map/all_to_all | solution.py:35
  (313 shorter events, 40.5 us)
Async XLA Ops:
  0.6 41.1 %copy-start.5 = (f32[1,1,6,6,256]{4,1,3,2,0:T(1,128)S(1)}, f32[1,1,6,6,256]{4,1,3,2,0:T(1,128)}, u32[]{:S(2)}) copy-start(f32[1,1,6,6,256]{4,1,3,2,0:T(1,128)} %param.12) | copy-start | bytes 110596
  0.6 23.7 %copy-start.7 = (f32[1,1,6,256]{3,1,2,0:T(1,128)S(1)}, f32[1,1,6,256]{3,1,2,0:T(1,128)}, u32[]{:S(2)}) copy-start(f32[1,1,6,256]{3,1,2,0:T(1,128)} %param.11) | copy-start | bytes 18436
  0.7 23.5 %copy-start.1 = (bf16[1,1,64,6,256]{4,2,3,1,0:T(8,128)(2,1)S(1)}, bf16[1,1,64,6,256]{4,2,3,1,0:T(8,128)(2,1)}, u32[]{:S(2)}) copy-start(bf16[1,1,64,6,256]{4,2,3,1,0:T(8,128)(2,1)} %param.13) | copy-start | bytes 589828
  0.7 40.7 %copy-start.17 = (s32[1,1,4]{2,1,0:T(1,128)S(1)}, s32[1,1,4]{2,1,0:T(1,128)}, u32[]{:S(2)}) copy-start(s32[1,1,4]{2,1,0:T(1,128)} %param.8) | copy-start | bytes 52
  0.7 23.2 %copy-start.16 = (s32[1,1,6]{2,1,0:T(1,128)S(1)}, s32[1,1,6]{2,1,0:T(1,128)}, u32[]{:S(2)}) copy-start(s32[1,1,6]{2,1,0:T(1,128)} %param.9) | copy-start | bytes 76
  5.4 37.4 %copy-start.14 = (f32[1,1,6,256]{3,1,2,0:T(1,128)S(1)}, f32[1,1,6,256]{3,1,2,0:T(1,128)}, u32[]{:S(2)}) copy-start(f32[1,1,6,256]{3,1,2,0:T(1,128)} %param.10) | copy-start | bytes 18436
  5.4 19.0 %collective-permute-start.1 = (f32[8,256]{1,0:T(8,128)S(1)}, f32[8,256]{1,0:T(8,128)S(1)}, u32[]{:S(2)}, u32[]{:S(2)}) collective-permute-start(f32[8,256]{1,0:T(8,128)S(1)} %get-tuple-element.89), channel_id=1, source_target_pairs={{1,0},{2,1},{3,2},{4,3},{5,4},{6,5},{7,6},{8,7},{9,8},{10,9},{11,1... | collective-permute-start | bytes 24584 | tf_op jit(solution)/shard_map/ppermute | solution.py:47
  14.2 10.1 %collective-permute-start = (f32[8,256]{1,0:T(8,128)S(1)}, f32[8,256]{1,0:T(8,128)S(1)}, u32[]{:S(2)}, u32[]{:S(2)}) collective-permute-start(f32[8,256]{1,0:T(8,128)S(1)} %get-tuple-element.88), channel_id=1, source_target_pairs={{0,1},{1,2},{2,3},{3,4},{4,5},{5,6},{6,7},{7,8},{8,9},{9,10},{10,1... | collective-permute-start | bytes 24584 | tf_op jit(solution)/shard_map/ppermute | solution.py:46
  17.5 23.9 %all-to-all-start = ((f32[32,1,4224]{2,1,0:T(1,128)}), f32[32,1,4224]{2,1,0:T(1,128)S(1)}, u32[]{:S(2)}, u32[]{:S(2)}) async-start(f32[32,1,4224]{2,1,0:T(1,128)} %copy.149), calls=%async_computation | async-start | bytes 1081344 | tf_op jit(solution)/shard_map/all_to_all | solution.py:39
  23.8 107.2 %copy-start.8 = (s32[128]{0:T(128)}, s32[128]{0:T(128)S(1)}, u32[]{:S(2)}) copy-start(s32[128]{0:T(128)S(1)} %get-tuple-element.115) | copy-start | bytes 1540
  23.8 107.2 %copy-start.10 = (s32[128]{0:T(128)}, s32[128]{0:T(128)S(1)}, u32[]{:S(2)}) copy-start(s32[128]{0:T(128)S(1)} %get-tuple-element.116) | copy-start | bytes 1540
  24.1 64.4 %copy-start.15 = (s32[288]{0:T(512)}, s32[288]{0:T(512)S(1)}, u32[]{:S(2)}) copy-start(s32[288]{0:T(512)S(1)} %fusion.134) | copy-start | bytes 3460
  24.2 106.7 %copy-start.12 = (pred[128]{0:T(512)(128)(4,1)}, pred[128]{0:T(512)(128)(4,1)S(1)}, u32[]{:S(2)}) copy-start(pred[128]{0:T(512)(128)(4,1)S(1)} %compare_and_fusion.1) | copy-start | bytes 388
  44.7 20.9 %all-to-all-start.1 = ((f32[32,1,3968]{2,1,0:T(1,128)}), f32[32,1,3968]{2,1,0:T(1,128)S(1)}, u32[]{:S(2)}, u32[]{:S(2)}) async-start(f32[32,1,3968]{2,1,0:T(1,128)} %broadcast_in_dim.67), calls=%async_computation.1 | async-start | bytes 1015808 | tf_op jit(solution)/shard_map/all_to_all | solution.py:39
  49.2 6.7 %collective-permute-start.3 = (f32[64,256]{1,0:T(8,128)S(1)}, f32[64,256]{1,0:T(8,128)S(1)}, u32[]{:S(2)}, u32[]{:S(2)}) collective-permute-start(f32[64,256]{1,0:T(8,128)S(1)} %get-tuple-element.77), channel_id=1, source_target_pairs={{1,0},{2,1},{3,2},{4,3},{5,4},{6,5},{7,6},{8,7},{9,8},{10,9},{11,1... | collective-permute-start | bytes 196616 | tf_op jit(solution)/shard_map/ppermute | solution.py:47
  51.5 5.3 %collective-permute-start.2 = (f32[64,256]{1,0:T(8,128)S(1)}, f32[64,256]{1,0:T(8,128)S(1)}, u32[]{:S(2)}, u32[]{:S(2)}) collective-permute-start(f32[64,256]{1,0:T(8,128)S(1)} %get-tuple-element.76), channel_id=1, source_target_pairs={{0,1},{1,2},{2,3},{3,4},{4,5},{5,6},{6,7},{7,8},{8,9},{9,10},{10,1... | collective-permute-start | bytes 196616 | tf_op jit(solution)/shard_map/ppermute | solution.py:46
  66.4 20.9 %all-to-all-start.2 = ((f32[16,1,1920]{2,1,0:T(1,128)}), f32[16,1,1920]{2,1,0:T(1,128)S(1)}, u32[]{:S(2)}, u32[]{:S(2)}) async-start(f32[16,1,1920]{2,1,0:T(1,128)} %broadcast_in_dim.70), calls=%async_computation.2 | async-start | bytes 245760 | tf_op jit(solution)/shard_map/all_to_all | solution.py:35
  108.2 17.1 %all-to-all-start.3 = ((f32[32,1,2304]{2,1,0:T(1,128)}), f32[32,1,2304]{2,1,0:T(1,128)S(1)}, u32[]{:S(2)}, u32[]{:S(2)}) async-start(f32[32,1,2304]{2,1,0:T(1,128)} %copy.162), calls=%async_computation.3 | async-start | bytes 589824 | tf_op jit(solution)/shard_map/all_to_all | solution.py:39
  126.1 12.3 %all-to-all-start.4 = ((f32[16,1,256]{2,1,0:T(1,128)}), f32[16,1,256]{2,1,0:T(1,128)S(1)}, u32[]{:S(2)}, u32[]{:S(2)}) async-start(f32[16,1,256]{2,1,0:T(1,128)} %broadcast_in_dim.73), calls=%async_computation.4 | async-start | bytes 32768 | tf_op jit(solution)/shard_map/all_to_all | solution.py:35
  131.0 36.8 %copy-start = (f32[96,96]{1,0:T(8,128)S(1)}, f32[96,96]{1,0:T(8,128)}, u32[]{:S(2)}) copy-start(f32[96,96]{1,0:T(8,128)} %shard_map.86) | copy-start | bytes 110596
  139.8 17.8 %all-to-all-start.5 = ((f32[32,1,3072]{2,1,0:T(1,128)}), f32[32,1,3072]{2,1,0:T(1,128)S(1)}, u32[]{:S(2)}, u32[]{:S(2)}) async-start(f32[32,1,3072]{2,1,0:T(1,128)} %broadcast_in_dim.148), calls=%async_computation.5 | async-start | bytes 786432 | tf_op jit(solution)/shard_map/all_to_all | solution.py:39
  144.2 5.9 %collective-permute-start.5 = (f32[64,256]{1,0:T(8,128)S(1)}, f32[64,256]{1,0:T(8,128)S(1)}, u32[]{:S(2)}, u32[]{:S(2)}) collective-permute-start(f32[64,256]{1,0:T(8,128)S(1)} %bitcast.363), channel_id=1, source_target_pairs={{1,0},{2,1},{3,2},{4,3},{5,4},{6,5},{7,6},{8,7},{9,8},{10,9},{11,1... | collective-permute-start | bytes 196616 | tf_op jit(solution)/shard_map/ppermute | solution.py:47
  146.6 4.5 %collective-permute-start.4 = (f32[64,256]{1,0:T(8,128)S(1)}, f32[64,256]{1,0:T(8,128)S(1)}, u32[]{:S(2)}, u32[]{:S(2)}) collective-permute-start(f32[64,256]{1,0:T(8,128)S(1)} %bitcast.365), channel_id=1, source_target_pairs={{0,1},{1,2},{2,3},{3,4},{4,5},{5,6},{6,7},{7,8},{8,9},{9,10},{10,1... | collective-permute-start | bytes 196616 | tf_op jit(solution)/shard_map/ppermute | solution.py:46
  157.7 27.8 %copy-start.4 = (f32[96,96]{0,1:T(8,128)S(1)}, f32[96,96]{0,1:T(8,128)}, u32[]{:S(2)}) copy-start(f32[96,96]{0,1:T(8,128)} %get-tuple-element.38) | copy-start | bytes 110596
  157.9 35.8 %copy-start.18 = (s32[24]{0:T(128)S(1)}, s32[24]{0:T(128)}, u32[]{:S(2)}) copy-start(s32[24]{0:T(128)} %add_add_fusion) | copy-start | bytes 292
  166.5 26.5 %copy-start.2 = (f32[64,64]{1,0:T(8,128)S(1)}, f32[64,64]{1,0:T(8,128)}, u32[]{:S(2)}) copy-start(f32[64,64]{1,0:T(8,128)} %shard_map.87) | copy-start | bytes 49156
  170.3 39.6 %copy-start.6 = (f32[1536]{0:T(1024)S(1)}, f32[1536]{0:T(1024)}, u32[]{:S(2)}) copy-start(f32[1536]{0:T(1024)} %pad.106.clone) | copy-start | bytes 18436
  171.1 14.3 %all-to-all-start.6 = ((f32[32,1,1152]{2,1,0:T(1,128)}), f32[32,1,1152]{2,1,0:T(1,128)S(1)}, u32[]{:S(2)}, u32[]{:S(2)}) async-start(f32[32,1,1152]{2,1,0:T(1,128)} %broadcast_in_dim.151), calls=%async_computation.6 | async-start | bytes 294912 | tf_op jit(solution)/shard_map/all_to_all | solution.py:35
  176.2 38.5 %copy-start.3 = (f32[96,96]{1,0:T(8,128)S(1)}, f32[96,96]{1,0:T(8,128)}, u32[]{:S(2)}) copy-start(f32[96,96]{1,0:T(8,128)} %fusion.76) | copy-start | bytes 110596
  186.6 13.3 %all-to-all-start.7 = ((f32[16,1,128]{2,1,0:T(1,128)}), f32[16,1,128]{2,1,0:T(1,128)S(1)}, u32[]{:S(2)}, u32[]{:S(2)}) async-start(f32[16,1,128]{2,1,0:T(1,128)} %broadcast_in_dim.152), calls=%async_computation.7 | async-start | bytes 16384 | tf_op jit(solution)/shard_map/all_to_all | solution.py:35
  193.0 32.8 %copy-start.9 = (s32[128]{0:T(128)S(1)}, s32[128]{0:T(128)}, u32[]{:S(2)}) copy-start(s32[128]{0:T(128)} %copy-done.8) | copy-start | bytes 1540
  193.0 32.8 %copy-start.11 = (s32[128]{0:T(128)S(1)}, s32[128]{0:T(128)}, u32[]{:S(2)}) copy-start(s32[128]{0:T(128)} %copy-done.10) | copy-start | bytes 1540
  193.0 32.8 %copy-start.13 = (pred[128]{0:T(512)(128)(4,1)S(1)}, pred[128]{0:T(512)(128)(4,1)}, u32[]{:S(2)}) copy-start(pred[128]{0:T(512)(128)(4,1)} %copy-done.12) | copy-start | bytes 388
  203.6 5.9 %collective-permute-start.7 = (f32[1,256]{1,0:T(1,128)S(1)}, f32[1,256]{1,0:T(1,128)S(1)}, u32[]{:S(2)}, u32[]{:S(2)}) collective-permute-start(f32[1,256]{1,0:T(1,128)S(1)} %get-tuple-element.99), channel_id=1, source_target_pairs={{1,0},{2,1},{3,2},{4,3},{5,4},{6,5},{7,6},{8,7},{9,8},{10,9},{11,1... | collective-permute-start | bytes 3080 | tf_op jit(solution)/shard_map/ppermute | solution.py:47
  206.2 3.7 %collective-permute-start.6 = (f32[1,256]{1,0:T(1,128)S(1)}, f32[1,256]{1,0:T(1,128)S(1)}, u32[]{:S(2)}, u32[]{:S(2)}) collective-permute-start(f32[1,256]{1,0:T(1,128)S(1)} %get-tuple-element.98), channel_id=1, source_target_pairs={{0,1},{1,2},{2,3},{3,4},{4,5},{5,6},{6,7},{7,8},{8,9},{9,10},{10,1... | collective-permute-start | bytes 3080 | tf_op jit(solution)/shard_map/ppermute | solution.py:46
  210.7 15.0 %all-to-all-start.8 = ((f32[32,1,1280]{2,1,0:T(1,128)}), f32[32,1,1280]{2,1,0:T(1,128)S(1)}, u32[]{:S(2)}, u32[]{:S(2)}) async-start(f32[32,1,1280]{2,1,0:T(1,128)} %broadcast_in_dim.154), calls=%async_computation.8 | async-start | bytes 327680 | tf_op jit(solution)/shard_map/all_to_all | solution.py:35
  226.8 13.4 %all-to-all-start.9 = ((f32[16,1,256]{2,1,0:T(1,128)}), f32[16,1,256]{2,1,0:T(1,128)S(1)}, u32[]{:S(2)}, u32[]{:S(2)}) async-start(f32[16,1,256]{2,1,0:T(1,128)} %broadcast_in_dim.155), calls=%async_computation.9 | async-start | bytes 32768 | tf_op jit(solution)/shard_map/all_to_all | solution.py:35
  243.6 5.6 %collective-permute-start.9 = (f32[1,256]{1,0:T(1,128)S(1)}, f32[1,256]{1,0:T(1,128)S(1)}, u32[]{:S(2)}, u32[]{:S(2)}) collective-permute-start(f32[1,256]{1,0:T(1,128)S(1)} %get-tuple-element.97), channel_id=1, source_target_pairs={{1,0},{2,1},{3,2},{4,3},{5,4},{6,5},{7,6},{8,7},{9,8},{10,9},{11,1... | collective-permute-start | bytes 3080 | tf_op jit(solution)/shard_map/ppermute | solution.py:47
  246.0 4.0 %collective-permute-start.8 = (f32[1,256]{1,0:T(1,128)S(1)}, f32[1,256]{1,0:T(1,128)S(1)}, u32[]{:S(2)}, u32[]{:S(2)}) collective-permute-start(f32[1,256]{1,0:T(1,128)S(1)} %get-tuple-element.96), channel_id=1, source_target_pairs={{0,1},{1,2},{2,3},{3,4},{4,5},{5,6},{6,7},{7,8},{8,9},{9,10},{10,1... | collective-permute-start | bytes 3080 | tf_op jit(solution)/shard_map/ppermute | solution.py:46
  265.1 13.8 %all-to-all-start.11 = ((f32[16,1,256]{2,1,0:T(1,128)}), f32[16,1,256]{2,1,0:T(1,128)S(1)}, u32[]{:S(2)}, u32[]{:S(2)}) async-start(f32[16,1,256]{2,1,0:T(1,128)} %broadcast_in_dim.157), calls=%async_computation.11 | async-start | bytes 32768 | tf_op jit(solution)/shard_map/all_to_all | solution.py:35
  283.0 13.9 %all-to-all-start.12 = ((f32[32,1,1152]{2,1,0:T(1,128)}), f32[32,1,1152]{2,1,0:T(1,128)S(1)}, u32[]{:S(2)}, u32[]{:S(2)}) async-start(f32[32,1,1152]{2,1,0:T(1,128)} %broadcast_in_dim.158), calls=%async_computation.12 | async-start | bytes 294912 | tf_op jit(solution)/shard_map/all_to_all | solution.py:35
  286.9 16.1 %collective-permute-start.11 = (f32[1,256]{1,0:T(1,128)S(1)}, f32[1,256]{1,0:T(1,128)S(1)}, u32[]{:S(2)}, u32[]{:S(2)}) collective-permute-start(f32[1,256]{1,0:T(1,128)S(1)} %get-tuple-element.95), channel_id=1, source_target_pairs={{1,0},{2,1},{3,2},{4,3},{5,4},{6,5},{7,6},{8,7},{9,8},{10,9},{11,1... | collective-permute-start | bytes 3080 | tf_op jit(solution)/shard_map/ppermute | solution.py:47
  289.3 13.8 %collective-permute-start.10 = (f32[1,256]{1,0:T(1,128)S(1)}, f32[1,256]{1,0:T(1,128)S(1)}, u32[]{:S(2)}, u32[]{:S(2)}) collective-permute-start(f32[1,256]{1,0:T(1,128)S(1)} %get-tuple-element.94), channel_id=1, source_target_pairs={{0,1},{1,2},{2,3},{3,4},{4,5},{5,6},{6,7},{7,8},{8,9},{9,10},{10,1... | collective-permute-start | bytes 3080 | tf_op jit(solution)/shard_map/ppermute | solution.py:46
  297.6 12.1 %all-to-all-start.13 = ((f32[16,1,128]{2,1,0:T(1,128)}), f32[16,1,128]{2,1,0:T(1,128)S(1)}, u32[]{:S(2)}, u32[]{:S(2)}) async-start(f32[16,1,128]{2,1,0:T(1,128)} %broadcast_in_dim.159), calls=%async_computation.13 | async-start | bytes 16384 | tf_op jit(solution)/shard_map/all_to_all | solution.py:35
